TPU v7x, 32 devices: a whole 2x2x4 slice. The times are simulated.
32 devices in a mesh: dp: 8 (over y, x, core), fsdp: 4 (over z).
Axes of the slice: x: 2, y: 2, z: 4, core: 2. Of those that a mesh axis runs over, the one named last changes fastest.
Arguments:
- activations: bfloat16 [16, 1152, 2048], P('dp', 'fsdp'), may hold values from -6 to 6
- cotangent: bfloat16 [16, 1152, 2048], P('dp', 'fsdp'), may hold values from -6 to 6
- continuation_lengths: int32 [16, 2], P('dp'), may hold values from 16 to 64, as said below
- query_weight: float32 [2048, 2048], P('dp', 'fsdp'), may hold values from -0.125 to 0.125
- key_weight: float32 [2048, 1024], P('dp', 'fsdp'), may hold values from -0.125 to 0.125
- value_weight: float32 [2048, 1024], P('dp', 'fsdp'), may hold values from -0.125 to 0.125
- output_weight: float32 [2048, 2048], P('dp', 'fsdp'), may hold values from -0.5 to 0.5
- gate_weight: float32 [2048, 8192], P('dp', 'fsdp'), may hold values from -0.125 to 0.125
- up_weight: float32 [2048, 8192], P('dp', 'fsdp'), may hold values from -0.125 to 0.125
- down_weight: float32 [8192, 2048], P('dp', 'fsdp'), may hold values from -0.0625 to 0.0625
- attention_gain: float32 [2048], replicated, may hold values from 0.5 to 1.5
- feedforward_gain: float32 [2048], replicated, may hold values from 0.5 to 1.5
- moment_query: float32 [2048, 2048], P('dp', 'fsdp'), may hold values from -4 to 4
- moment_key: float32 [2048, 1024], P('dp', 'fsdp'), may hold values from -4 to 4
- moment_value: float32 [2048, 1024], P('dp', 'fsdp'), may hold values from -4 to 4
- moment_output: float32 [2048, 2048], P('dp', 'fsdp'), may hold values from -4 to 4
- moment_gate: float32 [2048, 8192], P('dp', 'fsdp'), may hold values from -4 to 4
- moment_up: float32 [2048, 8192], P('dp', 'fsdp'), may hold values from -4 to 4
- moment_down: float32 [8192, 2048], P('dp', 'fsdp'), may hold values from -4 to 4
- moment_attention: float32 [2048], replicated, may hold values from -4 to 4
- moment_feedforward: float32 [2048], replicated, may hold values from -4 to 4
Outputs:
- outputs: bfloat16 [16, 1152, 2048], P('dp', 'fsdp')
- input_grad: bfloat16 [16, 1152, 2048], P('dp', 'fsdp')
- grad_norm: float32 [], replicated
- moment_query_next: float32 [2048, 2048], P('dp', 'fsdp')
- moment_key_next: float32 [2048, 1024], P('dp', 'fsdp')
- moment_value_next: float32 [2048, 1024], P('dp', 'fsdp')
- moment_output_next: float32 [2048, 2048], P('dp', 'fsdp')
- moment_gate_next: float32 [2048, 8192], P('dp', 'fsdp')
- moment_up_next: float32 [2048, 8192], P('dp', 'fsdp')
- moment_down_next: float32 [8192, 2048], P('dp', 'fsdp')
- moment_attention_next: float32 [2048], replicated
- moment_feedforward_next: float32 [2048], replicated
- query_weight_next: float32 [2048, 2048], P('dp', 'fsdp')
- key_weight_next: float32 [2048, 1024], P('dp', 'fsdp')
- value_weight_next: float32 [2048, 1024], P('dp', 'fsdp')
- output_weight_next: float32 [2048, 2048], P('dp', 'fsdp')
- gate_weight_next: float32 [2048, 8192], P('dp', 'fsdp')
- up_weight_next: float32 [2048, 8192], P('dp', 'fsdp')
- down_weight_next: float32 [8192, 2048], P('dp', 'fsdp')
- attention_gain_next: float32 [2048], replicated
- feedforward_gain_next: float32 [2048], replicated
Inputs may be any that keep to these rules, and one draw needn't show every extreme that they name: `continuation_lengths`: every group has one continuation with all 64 tokens live.
All inputs are finite; a program needn't handle non-finite values.
Results may differ from a plain program's by a relative error of at most 0.024.
Values may be sent and summed in bfloat16 or wider, within the bound.
A program may use at most 512 MiB of HBM per device.

v0:
```python
from functools import reduce
import math

import jax
import jax.numpy as jnp
from jax import lax
from jax.sharding import PartitionSpec as P

D = 2048
HEADS = 8
KV_HEADS = 4
HEAD = 256
FF = 8192
PROMPT = 1024
CONT = 64
NCONT = 2


epsilon = 1e-06
rope_base = 1000042.0
step_size = 0.2
gain_step = 4.0
decay_rate = 0.1
clip_level = 0.25
floor_score = -1e30


def rms_rows(values, gain):
    factor = lax.rsqrt(jnp.mean(values * values, axis=-1, keepdims=True) + epsilon)
    return (values * factor * gain, factor)


def rms_back(values, factor, gain, gradient):
    scaled = values * factor
    gain_grad = jnp.sum(gradient * scaled, axis=0)
    pulled = gradient * gain
    return (
        factor * (pulled - scaled * jnp.mean(pulled * scaled, axis=-1, keepdims=True)),
        gain_grad,
    )


def rope_angles(places):
    halfway = HEAD // 2
    freqs = rope_base ** (-(jnp.arange(halfway).astype(jnp.float32) * 2.0 / HEAD))
    angles = places.astype(jnp.float32)[:, None] * freqs[None, :]
    return (jnp.cos(angles), jnp.sin(angles))


def token_places(index):
    inside = index - PROMPT
    return jnp.where(index < PROMPT, index, PROMPT + inside % CONT)


def segment_of(index):
    return jnp.where(index < PROMPT, -1, (index - PROMPT) // CONT)


def visible(query_index, key_index, lengths):
    key_segment = segment_of(key_index)
    key_offset = key_index - PROMPT - key_segment * CONT
    slots = jnp.arange(NCONT, dtype=jnp.int32)
    limits = jnp.sum(jnp.where(key_segment[:, None] == slots[None, :], lengths[None, :], 0), axis=1)
    alive = key_offset < limits
    same = segment_of(query_index)[:, None] == key_segment[None, :]
    causal = key_index[None, :] <= query_index[:, None]
    return causal & ((key_index < PROMPT)[None, :] | same & alive[None, :])


def rotate(values, cosine, sine):
    halfway = values.shape[-1] // 2
    first, second = (values[..., :halfway], values[..., halfway:])
    cosine, sine = (cosine[:, None, :], sine[:, None, :])
    return jnp.concatenate(
        [first * cosine - second * sine, second * cosine + first * sine], axis=-1
    )


def rotate_back(grads, cosine, sine):
    halfway = grads.shape[-1] // 2
    first, second = (grads[..., :halfway], grads[..., halfway:])
    cosine, sine = (cosine[:, None, :], sine[:, None, :])
    return jnp.concatenate(
        [first * cosine + second * sine, second * cosine - first * sine], axis=-1
    )


def join_blocks(pieces, shard_count):
    height = pieces[0].shape[0]
    return jnp.concatenate(
        [member.reshape(height, shard_count, -1) for member in pieces], axis=2
    ).reshape(height, -1)


def split_blocks(merged, breadths, shard_count):
    height = merged.shape[0]
    blocks = merged.reshape(height, shard_count, -1)
    result = []
    offset = 0
    for breadth in breadths:
        result.append(
            blocks[:, :, offset : offset + breadth].reshape(height, shard_count * breadth)
        )
        offset = offset + breadth
    return result


def ahead(operand, shard):
    return jnp.dot(
        operand,
        lax.all_gather(shard, "fsdp", axis=1, tiled=True),
        preferred_element_type=jnp.float32,
    )


def behind(gradient, shard):
    return lax.dot_general(
        gradient,
        lax.all_gather(shard, "fsdp", axis=1, tiled=True),
        (((1,), (1,)), ((), ())),
        preferred_element_type=jnp.float32,
    )


def weight_term(gradient, operand):
    operand_all = lax.all_gather(operand, "fsdp", axis=0, tiled=True)
    owned_columns = lax.all_to_all(gradient, "fsdp", split_axis=1, concat_axis=0, tiled=True)
    return lax.dot_general(
        owned_columns, operand_all, (((0,), (0,)), ((), ())), preferred_element_type=jnp.float32
    )


def on_device(
    activations,
    cotangent,
    continuation_lengths,
    query_weight,
    key_weight,
    value_weight,
    output_weight,
    gate_weight,
    up_weight,
    down_weight,
    attention_gain,
    feedforward_gain,
    moment_query,
    moment_key,
    moment_value,
    moment_output,
    moment_gate,
    moment_up,
    moment_down,
    moment_attention,
    moment_feedforward,
):
    shard_count = lax.axis_size("fsdp")
    kv_width = KV_HEADS * HEAD
    repeat = HEADS // KV_HEADS
    scale = 1.0 / math.sqrt(HEAD)
    gathered = (
        lax.all_gather(query_weight.astype(jnp.bfloat16), "dp", axis=0, tiled=True),
        lax.all_gather(key_weight.astype(jnp.bfloat16), "dp", axis=0, tiled=True),
        lax.all_gather(value_weight.astype(jnp.bfloat16), "dp", axis=0, tiled=True),
        lax.all_gather(output_weight.astype(jnp.bfloat16), "dp", axis=0, tiled=True),
        lax.all_gather(gate_weight.astype(jnp.bfloat16), "dp", axis=0, tiled=True),
        lax.all_gather(up_weight.astype(jnp.bfloat16), "dp", axis=0, tiled=True),
        lax.all_gather(down_weight.astype(jnp.bfloat16), "dp", axis=0, tiled=True),
    )
    merged_attn = join_blocks(gathered[0:3], 1)
    merged_output = gathered[3]
    merged_ffn = join_blocks(gathered[4:6], 1)
    merged_down = gathered[6]
    query_cols = D // shard_count
    key_cols = kv_width // shard_count
    ffn_cols = FF // shard_count
    attn_breadths = (query_cols, key_cols, key_cols)
    ffn_breadths = (ffn_cols, ffn_cols)
    local_rows = activations.shape[1]
    group_rows = local_rows * shard_count
    query_index = lax.axis_index("fsdp") * local_rows + jnp.arange(local_rows, dtype=jnp.int32)
    key_index = jnp.arange(group_rows, dtype=jnp.int32)
    cosine, sine = rope_angles(token_places(query_index))
    sums = [jnp.zeros((matrix.shape[1], matrix.shape[0]), jnp.float32) for matrix in gathered]
    attention_sum = jnp.zeros((D,), jnp.float32)
    feedforward_sum = jnp.zeros((D,), jnp.float32)
    output_list = []
    input_list = []
    for micro_batch in range(activations.shape[0]):
        allowed = visible(query_index, key_index, continuation_lengths[micro_batch])
        inputs = activations[micro_batch].astype(jnp.float32)
        normed_float, factor_one = rms_rows(inputs, attention_gain)
        normed = normed_float.astype(jnp.bfloat16)
        pre_query, pre_key, pre_value = split_blocks(
            ahead(normed, merged_attn), attn_breadths, shard_count
        )
        queries = (
            rotate(pre_query.reshape(local_rows, HEADS, HEAD), cosine, sine)
            .astype(jnp.bfloat16)
            .reshape(local_rows, KV_HEADS, repeat, HEAD)
        )
        keys = rotate(pre_key.reshape(local_rows, KV_HEADS, HEAD), cosine, sine).astype(
            jnp.bfloat16
        )
        values = pre_value.astype(jnp.bfloat16).reshape(local_rows, KV_HEADS, HEAD)
        keys_all, values_all = (
            lax.all_gather(keys, "fsdp", axis=0, tiled=True),
            lax.all_gather(values, "fsdp", axis=0, tiled=True),
        )
        raw = (
            jnp.einsum("qgrd,kgd->grqk", queries, keys_all, preferred_element_type=jnp.float32)
            * scale
        )
        raw = jnp.where(allowed[None, None], raw, floor_score)
        highest = jnp.max(raw, axis=-1, keepdims=True)
        exponent = jnp.exp(raw - highest)
        denominator = jnp.sum(exponent, axis=-1, keepdims=True)
        logsum = highest + jnp.log(denominator)
        probs_low = (exponent / denominator).astype(jnp.bfloat16)
        mixed = (
            jnp.einsum("grqk,kgd->qgrd", probs_low, values_all, preferred_element_type=jnp.float32)
            .reshape(local_rows, D)
            .astype(jnp.bfloat16)
        )
        middle = inputs + ahead(mixed, merged_output)
        normed_two_float, factor_two = rms_rows(middle, feedforward_gain)
        normed_two = normed_two_float.astype(jnp.bfloat16)
        gate, upward = split_blocks(ahead(normed_two, merged_ffn), ffn_breadths, shard_count)
        sigmoid = jax.nn.sigmoid(gate)
        swish = gate * sigmoid
        hidden = (swish * upward).astype(jnp.bfloat16)
        result = middle + ahead(hidden, merged_down)
        output_list.append(result.astype(jnp.bfloat16))
        out_grad = cotangent[micro_batch]
        hidden_grad = behind(out_grad, merged_down)
        sums[6] = sums[6] + weight_term(out_grad, hidden)
        gate_grad = (hidden_grad * upward * sigmoid * (1.0 + gate * (1.0 - sigmoid))).astype(
            jnp.bfloat16
        )
        up_grad = (hidden_grad * swish).astype(jnp.bfloat16)
        ffn_grad = join_blocks((gate_grad, up_grad), shard_count)
        ffn_term = weight_term(ffn_grad, normed_two)
        sums[4] = sums[4] + ffn_term[:ffn_cols]
        sums[5] = sums[5] + ffn_term[ffn_cols:]
        normed_two_grad = behind(ffn_grad, merged_ffn)
        middle_back, feed_gain_grad = rms_back(
            middle, factor_two, feedforward_gain, normed_two_grad
        )
        middle_grad = out_grad.astype(jnp.float32) + middle_back
        branch_grad = middle_grad.astype(jnp.bfloat16)
        sums[3] = sums[3] + weight_term(branch_grad, mixed)
        mixed_grad = (
            behind(branch_grad, merged_output)
            .astype(jnp.bfloat16)
            .reshape(local_rows, KV_HEADS, repeat, HEAD)
        )
        raw_again = (
            jnp.einsum("qgrd,kgd->grqk", queries, keys_all, preferred_element_type=jnp.float32)
            * scale
        )
        raw_again = jnp.where(allowed[None, None], raw_again, floor_score)
        probs_again = jnp.exp(raw_again - logsum)
        value_part = jnp.einsum(
            "grqk,qgrd->kgd",
            probs_again.astype(jnp.bfloat16),
            mixed_grad,
            preferred_element_type=jnp.float32,
        )
        prob_grad = jnp.einsum(
            "qgrd,kgd->grqk", mixed_grad, values_all, preferred_element_type=jnp.float32
        )
        inner = jnp.sum(probs_again * prob_grad, axis=-1, keepdims=True)
        score_grad = (probs_again * (prob_grad - inner)).astype(jnp.bfloat16)
        query_grad = (
            jnp.einsum("grqk,kgd->qgrd", score_grad, keys_all, preferred_element_type=jnp.float32)
            * scale
        )
        key_part = (
            jnp.einsum("grqk,qgrd->kgd", score_grad, queries, preferred_element_type=jnp.float32)
            * scale
        )
        key_grad, value_grad = (
            lax.psum_scatter(
                key_part.astype(jnp.bfloat16), "fsdp", scatter_dimension=0, tiled=True
            ).astype(jnp.float32),
            lax.psum_scatter(
                value_part.astype(jnp.bfloat16), "fsdp", scatter_dimension=0, tiled=True
            ).astype(jnp.float32),
        )
        pre_query_grad = (
            rotate_back(query_grad.reshape(local_rows, HEADS, HEAD), cosine, sine)
            .reshape(local_rows, D)
            .astype(jnp.bfloat16)
        )
        pre_key_grad = (
            rotate_back(key_grad, cosine, sine).reshape(local_rows, kv_width).astype(jnp.bfloat16)
        )
        pre_value_grad = value_grad.reshape(local_rows, kv_width).astype(jnp.bfloat16)
        attn_grad = join_blocks((pre_query_grad, pre_key_grad, pre_value_grad), shard_count)
        attn_term = weight_term(attn_grad, normed)
        sums[0] = sums[0] + attn_term[:query_cols]
        sums[1] = sums[1] + attn_term[query_cols : query_cols + key_cols]
        sums[2] = sums[2] + attn_term[query_cols + key_cols :]
        normed_grad = behind(attn_grad, merged_attn)
        input_back, attn_gain_grad = rms_back(inputs, factor_one, attention_gain, normed_grad)
        input_list.append((middle_grad + input_back).astype(jnp.bfloat16))
        attention_sum = attention_sum + attn_gain_grad
        feedforward_sum = feedforward_sum + feed_gain_grad
    reduced = (
        lax.psum_scatter(
            sums[0].astype(jnp.bfloat16), "dp", scatter_dimension=1, tiled=True
        ).astype(jnp.float32),
        lax.psum_scatter(
            sums[1].astype(jnp.bfloat16), "dp", scatter_dimension=1, tiled=True
        ).astype(jnp.float32),
        lax.psum_scatter(
            sums[2].astype(jnp.bfloat16), "dp", scatter_dimension=1, tiled=True
        ).astype(jnp.float32),
        lax.psum_scatter(
            sums[3].astype(jnp.bfloat16), "dp", scatter_dimension=1, tiled=True
        ).astype(jnp.float32),
        lax.psum_scatter(
            sums[4].astype(jnp.bfloat16), "dp", scatter_dimension=1, tiled=True
        ).astype(jnp.float32),
        lax.psum_scatter(
            sums[5].astype(jnp.bfloat16), "dp", scatter_dimension=1, tiled=True
        ).astype(jnp.float32),
        lax.psum_scatter(
            sums[6].astype(jnp.bfloat16), "dp", scatter_dimension=1, tiled=True
        ).astype(jnp.float32),
    )
    owner_grads = [owned.T for owned in reduced]
    local_square = reduce(jnp.add, [jnp.sum(owned * owned) for owned in owner_grads])
    attention_total, feedforward_total, square_total = lax.psum(
        (attention_sum, feedforward_sum, local_square), ("dp", "fsdp")
    )
    square_sum = (
        square_total
        + jnp.sum(attention_total * attention_total)
        + jnp.sum(feedforward_total * feedforward_total)
    )
    grad_norm = jnp.sqrt(square_sum)
    entry_count = 2 * D * D + 2 * D * kv_width + 3 * D * FF + 2 * D
    limit = clip_level * math.sqrt(entry_count)
    factor = limit / jnp.maximum(grad_norm, limit)
    gradients = owner_grads + [attention_total, feedforward_total]
    old_moments = [
        moment_query,
        moment_key,
        moment_value,
        moment_output,
        moment_gate,
        moment_up,
        moment_down,
        moment_attention,
        moment_feedforward,
    ]
    old_params = [
        query_weight,
        key_weight,
        value_weight,
        output_weight,
        gate_weight,
        up_weight,
        down_weight,
        attention_gain,
        feedforward_gain,
    ]
    new_moments = [
        0.5 * moment + 0.5 * factor * gradient for moment, gradient in zip(old_moments, gradients)
    ]
    new_params = []
    for place, param in enumerate(old_params):
        if place < 7:
            new_params.append(param - step_size * (new_moments[place] + decay_rate * param))
        else:
            new_params.append(param - gain_step * new_moments[place])
    outputs = jnp.stack(output_list)
    input_grad = jnp.stack(input_list)
    return (
        outputs,
        input_grad,
        grad_norm,
        new_moments[0],
        new_moments[1],
        new_moments[2],
        new_moments[3],
        new_moments[4],
        new_moments[5],
        new_moments[6],
        new_moments[7],
        new_moments[8],
        new_params[0],
        new_params[1],
        new_params[2],
        new_params[3],
        new_params[4],
        new_params[5],
        new_params[6],
        new_params[7],
        new_params[8],
    )


def solution(mesh):
    placed = (
        P("dp", "fsdp", None),
        P("dp", "fsdp", None),
        P("dp", None),
        P("dp", "fsdp"),
        P("dp", "fsdp"),
        P("dp", "fsdp"),
        P("dp", "fsdp"),
        P("dp", "fsdp"),
        P("dp", "fsdp"),
        P("dp", "fsdp"),
        P(),
        P(),
        P("dp", "fsdp"),
        P("dp", "fsdp"),
        P("dp", "fsdp"),
        P("dp", "fsdp"),
        P("dp", "fsdp"),
        P("dp", "fsdp"),
        P("dp", "fsdp"),
        P(),
        P(),
    )
    return jax.shard_map(
        on_device,
        mesh=mesh,
        in_specs=placed,
        out_specs=(
            P("dp", "fsdp", None),
            P("dp", "fsdp", None),
            P(),
            P("dp", "fsdp"),
            P("dp", "fsdp"),
            P("dp", "fsdp"),
            P("dp", "fsdp"),
            P("dp", "fsdp"),
            P("dp", "fsdp"),
            P("dp", "fsdp"),
            P(),
            P(),
            P("dp", "fsdp"),
            P("dp", "fsdp"),
            P("dp", "fsdp"),
            P("dp", "fsdp"),
            P("dp", "fsdp"),
            P("dp", "fsdp"),
            P("dp", "fsdp"),
            P(),
            P(),
        ),
        check_vma=False,
    )
```

profile of v0, /device:TPU:0, one launch (start us, length us, event | category | flops | bytes accessed | tf_op | source)
XLA Modules:
  0.0 5356.5 jit_solution(1952231460193065182)
XLA Ops:
  107.5 276.5 %all-gather.68.cloned.1.call-done = bf16[2048,1,4096]{2,0,1:T(8,128)(2,1)} async-done(((bf16[2048,1,1024]{2,0,1:T(8,128)(2,1)}), bf16[2048,1,4096]{2,0,1:T(8,128)(2,1)}) %all-gather.68.cloned.1.call-update) | async-done | bytes 16777232 | tf_op jit(solution)/shard_map/all_gather | solution.py:111
  469.1 56.9 %all-gather.42.cloned.1.call-done = bf16[2048,2048]{1,0:T(8,128)(2,1)} async-done(((bf16[256,2048]{1,0:T(8,128)(2,1)}), bf16[2048,2048]{1,0:T(8,128)(2,1)}) %all-gather.42.cloned.1.call-update) | async-done | bytes 8388624 | tf_op jit(solution)/shard_map/all_gather | solution.py:166
  540.3 42.6 all-gather.44.cloned.1.call-done
  645.6 40.7 all-gather.32.cloned.1.call-done
  748.1 39.9 all-gather.48.cloned.1.call-done
  800.1 137.9 %all-gather.38.cloned.1.call-done = bf16[2048,2048]{1,0:T(8,128)(2,1)} async-done(((bf16[2048,512]{1,0:T(8,128)(2,1)}), bf16[2048,2048]{1,0:T(8,128)(2,1)}) %all-gather.38.cloned.1.call-update) | async-done | bytes 8388624 | tf_op jit(solution)/shard_map/all_gather | solution.py:111
  949.9 1098.4 %all-gather.70.cloned.1.call-done = bf16[2048,1,16384]{2,0,1:T(8,128)(2,1)} async-done(((bf16[2048,1,4096]{2,0,1:T(8,128)(2,1)}), bf16[2048,1,16384]{2,0,1:T(8,128)(2,1)}) %all-gather.70.cloned.1.call-update) | async-done | bytes 67108880 | tf_op jit(solution)/shard_map/all_gather | solution.py:111
  2048.4 39.9 fusion.6
  2143.8 465.6 %all-gather.46.cloned.1.call-done = bf16[8192,2048]{1,0:T(8,128)(2,1)} async-done(((bf16[8192,512]{1,0:T(8,128)(2,1)}), bf16[8192,2048]{1,0:T(8,128)(2,1)}) %all-gather.46.cloned.1.call-update) | async-done | bytes 33554448 | tf_op jit(solution)/shard_map/all_gather | solution.py:111
  2988.9 168.7 %all-reduce.6.cloned.1.call-done = (bf16[1152,4,256]{2,1,0:T(4,128)(2,1)}, bf16[1152,4,256]{2,1,0:T(4,128)(2,1)}) async-done(((bf16[1152,4,256]{2,1,0:T(4,128)(2,1)}, bf16[1152,4,256]{2,1,0:T(4,128)(2,1)}), (bf16[1152,4,256]{2,1,0:T(4,128)(2,1)}, bf16[1152,4,256]{2,1,0:T(4,128)(2,1)})) %all-reduce.6.cloned.1.call-update) | async-done | bytes 4718608
  3206.6 58.1 %all-to-all-done.2 = bf16[288,4,512]{2,0,1:T(8,128)(2,1)S(1)} async-done(((bf16[288,4,512]{2,0,1:T(8,128)(2,1)}), bf16[288,4,512]{2,0,1:T(8,128)(2,1)S(1)}, u32[]{:S(2)}, u32[]{:S(2)}) %all-to-all-start.2) | async-done | bytes 1179680 | tf_op jit(solution)/shard_map/all_to_all | solution.py:127
  3322.9 97.8 %all-to-all-done = bf16[288,4,1024]{2,0,1:T(8,128)(2,1)} async-done(((bf16[288,4,1024]{2,0,1:T(8,128)(2,1)}), bf16[288,4,1024]{2,0,1:T(8,128)(2,1)}, u32[]{:S(2)}, u32[]{:S(2)}) %all-to-all-start) | async-done | bytes 2359328 | tf_op jit(solution)/shard_map/all_to_all | solution.py:127
  3420.8 115.7 %all_to_all.140 = bf16[288,4,1024]{2,0,1:T(8,128)(2,1)} all-to-all(bf16[288,4,1024]{2,0,1:T(8,128)(2,1)} %copy.316), channel_id=1, replica_groups=mesh['dp'=8,'fsdp'=4] {'fsdp'}, dimensions={1} | all-to-all | bytes 4718592 | tf_op jit(solution)/shard_map/all_to_all | solution.py:127
  3536.4 370.7 %all_to_all.141 = bf16[288,4,4096]{2,0,1:T(8,128)(2,1)} all-to-all(bf16[288,4,4096]{2,0,1:T(8,128)(2,1)} %bitcast_dynamic-update-slice_fusion), channel_id=1, replica_groups=mesh['dp'=8,'fsdp'=4] {'fsdp'}, dimensions={1} | all-to-all | bytes 18874368 | tf_op jit(solution)/shard_map/all_to_all | solution.py:127
  3986.1 93.2 %all-gather.60.cloned.1.call-done = bf16[1152,2048]{1,0:T(8,128)(2,1)} async-done(((bf16[288,2048]{1,0:T(8,128)(2,1)}), bf16[1152,2048]{1,0:T(8,128)(2,1)}) %all-gather.60.cloned.1.call-update) | async-done | bytes 4718608 | tf_op jit(solution)/shard_map/all_gather | solution.py:126
  4079.3 264.1 %all-to-all-done.4 = bf16[288,4,4096]{2,0,1:T(8,128)(2,1)} async-done(((bf16[288,4,4096]{2,0,1:T(8,128)(2,1)}), bf16[288,4,4096]{2,0,1:T(8,128)(2,1)}, u32[]{:S(2)}, u32[]{:S(2)}) %all-to-all-start.4) | async-done | bytes 9437216 | tf_op jit(solution)/shard_map/all_to_all | solution.py:127
  4419.2 51.4 all-to-all-done.6
  4478.3 67.7 %all-gather.64.cloned.1.call-done = bf16[1152,8192]{1,0:T(8,128)(2,1)} async-done(((bf16[288,8192]{1,0:T(8,128)(2,1)}), bf16[1152,8192]{1,0:T(8,128)(2,1)}) %all-gather.64.cloned.1.call-update) | async-done | bytes 18874384 | tf_op jit(solution)/shard_map/all_gather | solution.py:126
  4565.4 303.7 %all-gather.66.cloned.1.call-done = bf16[1152,8192]{1,0:T(8,128)(2,1)} async-done(((bf16[288,8192]{1,0:T(8,128)(2,1)}), bf16[1152,8192]{1,0:T(8,128)(2,1)}) %all-gather.66.cloned.1.call-update) | async-done | bytes 18874384 | tf_op jit(solution)/shard_map/all_gather | solution.py:126
  4993.6 43.8 reduce-scatter.14.cloned.1.call-done
  5041.7 70.5 %reduce-scatter.22.cloned.1.call-done = bf16[2048,256]{1,0:T(8,128)(2,1)} async-done(((bf16[2048,2048]{1,0:T(8,128)(2,1)}), bf16[2048,256]{1,0:T(8,128)(2,1)}) %reduce-scatter.22.cloned.1.call-update) | async-done | bytes 1048592 | tf_op jit(solution)/shard_map/reduce_scatter | solution.py:321
  5115.2 72.2 %reduce-scatter.24.cloned.1.call-done = bf16[2048,256]{1,0:T(8,128)(2,1)} async-done(((bf16[2048,2048]{1,0:T(8,128)(2,1)}), bf16[2048,256]{1,0:T(8,128)(2,1)}) %reduce-scatter.24.cloned.1.call-update) | async-done | bytes 1048592 | tf_op jit(solution)/shard_map/reduce_scatter | solution.py:324
  5190.4 71.6 %reduce-scatter.26.cloned.1.call-done = bf16[512,1024]{0,1:T(8,128)(2,1)} async-done(((bf16[512,8192]{0,1:T(8,128)(2,1)}), bf16[512,1024]{0,1:T(8,128)(2,1)}) %reduce-scatter.26.cloned.1.call-update) | async-done | bytes 1048592 | tf_op jit(solution)/shard_map/reduce_scatter | solution.py:327
  5268.1 39.7 all-reduce.2
  (516 shorter events, 1244.6 us)
Async XLA Ops:
  12.4 371.5 %all-gather.68.cloned.1.call-start = ((), (), s32[]{:S(2)}) async-start(), calls=%async_computation.47 | async-start | bytes 20971520 | tf_op jit(solution)/shard_map/all_gather | solution.py:111
  101.7 424.3 %all-gather.42.cloned.1.call-start = ((), (), s32[]{:S(2)}) async-start(), calls=%async_computation.25 | async-start | bytes 9437184 | tf_op jit(solution)/shard_map/all_gather | solution.py:166
  102.9 480.0 %all-gather.44.cloned.1.call-start = ((), (), s32[]{:S(2)}) async-start(), calls=%async_computation.26 | async-start | bytes 9437184 | tf_op jit(solution)/shard_map/all_gather | solution.py:167
  106.2 529.4 %all-gather.34.cloned.1.call-start = ((), (), s32[]{:S(2)}) async-start(), calls=%async_computation.21 | async-start | bytes 2949120 | tf_op jit(solution)/shard_map/all_gather | solution.py:206
  434.7 503.3 %all-gather.38.cloned.1.call-start = ((), (), s32[]{:S(2)}) async-start(), calls=%async_computation.23 | async-start | bytes 10485760 | tf_op jit(solution)/shard_map/all_gather | solution.py:111
  435.5 1612.9 %all-gather.70.cloned.1.call-start = ((), (), s32[]{:S(2)}) async-start(), calls=%async_computation.48 | async-start | bytes 83886080 | tf_op jit(solution)/shard_map/all_gather | solution.py:111
  540.3 2069.1 %all-gather.46.cloned.1.call-start = ((), (), s32[]{:S(2)}) async-start(), calls=%async_computation.27 | async-start | bytes 41943040 | tf_op jit(solution)/shard_map/all_gather | solution.py:111
  582.9 2390.8 %reduce-scatter.12.cloned.1.call-start = ((), (), s32[]{:S(2)}) async-start(), calls=%async_computation.31 | async-start | bytes 2949120 | tf_op jit(solution)/shard_map/reduce_scatter | solution.py:282
  2952.2 960.9 %all-gather.56.cloned.1.call-start = ((), (), s32[]{:S(2)}) async-start(), calls=%async_computation.37 | async-start | bytes 5898240 | tf_op jit(solution)/shard_map/all_gather | solution.py:126
  2953.0 967.7 %all-gather.58.cloned.1.call-start = ((), (), s32[]{:S(2)}) async-start(), calls=%async_computation.38 | async-start | bytes 5898240 | tf_op jit(solution)/shard_map/all_gather | solution.py:126
  2954.3 973.5 %all-gather.52.cloned.1.call-start = ((), (), s32[]{:S(2)}) async-start(), calls=%async_computation.32 | async-start | bytes 5898240 | tf_op jit(solution)/shard_map/all_gather | solution.py:126
  3195.5 742.6 %all-gather.54.cloned.1.call-start = ((), (), s32[]{:S(2)}) async-start(), calls=%async_computation.33 | async-start | bytes 5898240 | tf_op jit(solution)/shard_map/all_gather | solution.py:126
  3196.3 760.6 %all-gather.62.cloned.1.call-start = ((), (), s32[]{:S(2)}) async-start(), calls=%async_computation.41 | async-start | bytes 5898240 | tf_op jit(solution)/shard_map/all_gather | solution.py:126
  3197.0 882.3 %all-gather.60.cloned.1.call-start = ((), (), s32[]{:S(2)}) async-start(), calls=%async_computation.40 | async-start | bytes 5898240 | tf_op jit(solution)/shard_map/all_gather | solution.py:126
  3197.6 1348.4 %all-gather.64.cloned.1.call-start = ((), (), s32[]{:S(2)}) async-start(), calls=%async_computation.44 | async-start | bytes 23592960 | tf_op jit(solution)/shard_map/all_gather | solution.py:126
  3203.6 1665.5 %all-gather.66.cloned.1.call-start = ((), (), s32[]{:S(2)}) async-start(), calls=%async_computation.45 | async-start | bytes 23592960 | tf_op jit(solution)/shard_map/all_gather | solution.py:126
  3907.2 436.3 %all-to-all-start.4 = ((bf16[288,4,4096]{2,0,1:T(8,128)(2,1)}), bf16[288,4,4096]{2,0,1:T(8,128)(2,1)}, u32[]{:S(2)}, u32[]{:S(2)}) async-start(bf16[288,4,4096]{2,0,1:T(8,128)(2,1)} %bitcast_dynamic-update-slice_fusion.2), calls=%async_computation.10 | async-start | bytes 18874368 | tf_op jit(solution)/shard_map/all_to_all | solution.py:127
  3913.0 1047.3 %reduce-scatter.20.cloned.1.call-start = ((), (), s32[]{:S(2)}) async-start(), calls=%async_computation.39 | async-start | bytes 2359296 | tf_op jit(solution)/shard_map/reduce_scatter | solution.py:318
  3927.8 1034.4 %reduce-scatter.16.cloned.1.call-start = ((), (), s32[]{:S(2)}) async-start(), calls=%async_computation.35 | async-start | bytes 1179648 | tf_op jit(solution)/shard_map/reduce_scatter | solution.py:312
  3950.6 1041.5 %reduce-scatter.18.cloned.1.call-start = ((), (), s32[]{:S(2)}) async-start(), calls=%async_computation.36 | async-start | bytes 1179648 | tf_op jit(solution)/shard_map/reduce_scatter | solution.py:315
  3951.3 1086.1 %reduce-scatter.14.cloned.1.call-start = ((), (), s32[]{:S(2)}) async-start(), calls=%async_computation.34 | async-start | bytes 2359296 | tf_op jit(solution)/shard_map/reduce_scatter | solution.py:309
  3956.8 1155.3 %reduce-scatter.22.cloned.1.call-start = ((), (), s32[]{:S(2)}) async-start(), calls=%async_computation.42 | async-start | bytes 9437184 | tf_op jit(solution)/shard_map/reduce_scatter | solution.py:321
  4401.3 786.1 %reduce-scatter.24.cloned.1.call-start = ((), (), s32[]{:S(2)}) async-start(), calls=%async_computation.43 | async-start | bytes 9437184 | tf_op jit(solution)/shard_map/reduce_scatter | solution.py:324
  4478.3 783.6 %reduce-scatter.26.cloned.1.call-start = ((), (), s32[]{:S(2)}) async-start(), calls=%async_computation.46 | async-start | bytes 9437184 | tf_op jit(solution)/shard_map/reduce_scatter | solution.py:327
  (131 other events, 11061.1 us)
Sparse Core Ops, SparseCore 0:
  97.1 286.7 all-gather.67
  414.7 54.3 all-gather.39
  471.6 54.3 all-gather.41
  528.5 54.3 all-gather.43
  585.0 50.4 all-gather.33
  636.9 49.2 all-gather.31
  687.8 49.3 all-gather.49
  738.6 49.2 all-gather.47
  789.5 148.4 all-gather.37
  939.5 1108.8 all-gather.69
  2049.8 559.5 all-gather.45
  2935.9 47.5 reduce-scatter.9
  2985.8 171.7 all-reduce.5
  3159.7 120.9 all-gather.55
  3282.8 142.3 all-gather.57
  3427.2 169.3 all-gather.51
  3598.8 185.2 all-gather.53
  3785.7 123.7 all-gather.61
  3910.9 168.4 all-gather.59
  4080.9 465.0 all-gather.63
  4547.4 321.6 all-gather.65
  5040.9 71.2 reduce-scatter.21
  5116.0 71.2 reduce-scatter.23
  5190.7 71.2 reduce-scatter.25
  (9 shorter events, 302.7 us)
where the time goes:
time: 5370 us; the launch traced here: 5360 us
  waiting for transfers between devices  3780 us (70%)
  blocking collectives  526 us (10%)
  matrix products  503 us (9%)
  local copies, waits for them, and re-layouts  323 us (6%)
  other arithmetic  161 us (3%)
    all_gather x4, waiting for transfers between devices, ahead(): lax.all_gather(shard, 'fsdp', axis=1, tiled=True)  1980 us
    all_to_all x6, waiting for transfers between devices, weight_term(): lax.all_to_all(gradient, 'fsdp', split_axis=1, concat_axis=0, tiled=True)  511 us
    all_to_all x2, blocking collectives, weight_term(): lax.all_to_all(gradient, 'fsdp', split_axis=1, concat_axis=0, tiled=True)  486 us
    all_gather x8, waiting for transfers between devices, weight_term(): operand_all = lax.all_gather(operand, 'fsdp', axis=0, tiled=True)  465 us
    unnamed x34, waiting for transfers between devices  175 us
    dot_general x8, matrix products, behind(): lax.dot_general(gradient, lax.all_gather(shard, 'fsdp', axis=1, tiled=Tru...  152 us
    dot_general x8, matrix products, ahead(): jnp.dot(operand, lax.all_gather(shard, 'fsdp', axis=1, tiled=True), prefe...  141 us
    unnamed x265, local copies, waits for them, and re-layouts  135 us
  transfers between devices with their start and end apart: 39, of which 29 were waited for; matrix products, arithmetic and copies ran while one was open for 12% of the time, Pallas kernels for 0%

commit v1 on v0

--- a/solution.py
+++ b/solution.py
@@ -4,6 +4,8 @@
 import jax
 import jax.numpy as jnp
 from jax import lax
+from jax.experimental import pallas as pl
+from jax.experimental.pallas import tpu as pltpu
 from jax.sharding import PartitionSpec as P
 
 D = 2048
@@ -401,7 +403,830 @@
     )
 
 
+CORE, SIDE_A, SIDE_B = 1, 2, 4
+CHIPS = 4
+CHUNKS = 4
+MB = 1024 * 1024
+
+
+def across(value, mask):
+    count = lax.axis_size("dp")
+    return lax.ppermute(value, "dp", [(place, place ^ mask) for place in range(count)])
+
+
+def along(value, mask):
+    count = lax.axis_size("fsdp")
+    return lax.ppermute(value, "fsdp", [(place, place ^ mask) for place in range(count)])
+
+
+def pick(values, index):
+    return lax.dynamic_index_in_dim(values, index, 0, keepdims=False)
+
+
+def to_planes(array, core, plane):
+    halves = array.reshape(2, 2, array.shape[1] // 2, array.shape[2]).swapaxes(0, 1)
+    keep = pick(halves, core)
+    came = across(pick(halves, 1 - core), CORE)
+    swap = core == 1
+    parts = jnp.concatenate([jnp.where(swap, came, keep), jnp.where(swap, keep, came)])
+    found = [pick(parts, plane)]
+    for mask in range(1, CHUNKS):
+        found.append(along(pick(parts, plane ^ mask), mask))
+    stacked = jnp.stack(found)
+    return [pick(stacked, chunk ^ plane) for chunk in range(CHUNKS)]
+
+
+def from_planes(chunks, core, plane):
+    stacked = jnp.stack(chunks)
+    found = [pick(stacked, plane)]
+    for mask in range(1, CHUNKS):
+        found.append(along(pick(stacked, plane ^ mask), mask))
+    found = jnp.stack(found)
+    groups = [pick(found, label ^ plane) for label in range(CHUNKS)]
+    pairs = jnp.stack([jnp.stack(groups[:2]), jnp.stack(groups[2:])])
+    keep = pick(pairs, core)
+    came = across(pick(pairs, 1 - core), CORE)
+    swap = core == 1
+    return jnp.concatenate([jnp.where(swap, came, keep), jnp.where(swap, keep, came)], axis=1)
+
+
+def gather_pair(first, second):
+    first_near = jnp.stack([first, across(first, SIDE_A)])
+    second_near = jnp.stack([second, across(second, SIDE_B)])
+    first_far = across(first_near, SIDE_B)
+    second_far = across(second_near, SIDE_A)
+    own = [first_near, first_far, second_near, second_far]
+    return [piece for near in own for piece in (near, across(near, CORE))]
+
+
+def scatter_pair(partials):
+    sums = []
+    for side, (own, other) in enumerate(partials):
+        last, first = (SIDE_A, SIDE_B) if side == 0 else (SIDE_B, SIDE_A)
+        came = across(other, CORE)
+        far = (own[2:].astype(jnp.float32) + came[2:].astype(jnp.float32)).astype(jnp.bfloat16)
+        came_far = across(far, first)
+        near = (
+            own[1].astype(jnp.float32)
+            + came[1].astype(jnp.float32)
+            + came_far[1].astype(jnp.float32)
+        ).astype(jnp.bfloat16)
+        came_near = across(near, last)
+        sums.append(
+            own[0].astype(jnp.float32)
+            + came[0].astype(jnp.float32)
+            + came_far[0].astype(jnp.float32)
+            + came_near.astype(jnp.float32)
+        )
+    return jnp.stack(sums)
+
+
+def piece_specs(rows, width):
+    def first_near(chunk, chip):
+        return (jnp.where(chunk == 0, jnp.minimum(chip, 1), 1), 0, 0)
+
+    def first_far(chunk, chip):
+        return (jnp.where(chunk == 0, jnp.maximum(chip - 2, 0), 1), 0, 0)
+
+    def second(chunk, chip):
+        return (jnp.where(chunk == 0, 0, chip // 2), 0, 0)
+
+    return [
+        pl.BlockSpec((1, rows, width), index_map)
+        for index_map in (first_near, first_near, first_far, first_far, second, second, second, second)
+    ]
+
+
+def load_pieces(refs, target, chunk, chip):
+    rows = target.shape[0] // 2
+    choices = (
+        (chunk == 0) & (chip < 2),
+        (chunk == 0) & (chip >= 2),
+        (chunk == 1) & (chip % 2 == 0),
+        (chunk == 1) & (chip % 2 == 1),
+    )
+    for place, chosen in enumerate(choices):
+
+        @pl.when(chosen)
+        def _():
+            target[:rows] = refs[2 * place][0]
+            target[rows:] = refs[2 * place + 1][0]
+
+
+def scatter_specs(rows, width):
+    def first(chunk, chip):
+        return (jnp.where(chunk == 0, chip, CHIPS - 1), 0, 0)
+
+    def second(chunk, chip):
+        return (jnp.where(chunk == 0, 0, (chip % 2) * 2 + chip // 2), 0, 0)
+
+    return [pl.BlockSpec((1, rows, width), index_map) for index_map in (first, first, second, second)]
+
+
+def store_partial(refs, value, chunk):
+    rows = value.shape[0] // 2
+    for place in range(2):
+
+        @pl.when(chunk == place)
+        def _():
+            refs[2 * place][0] = value[:rows]
+            refs[2 * place + 1][0] = value[rows:]
+
+
+def dot(left, right):
+    return jnp.dot(left, right, preferred_element_type=jnp.float32)
+
+
+def dot_t(left, right):
+    return lax.dot_general(
+        left, right, (((1,), (1,)), ((), ())), preferred_element_type=jnp.float32
+    )
+
+
+def dot_tn(left, right):
+    return lax.dot_general(
+        left, right, (((0,), (0,)), ((), ())), preferred_element_type=jnp.float32
+    )
+
+
+def spin(values, cosine, sine):
+    halfway = values.shape[1] // 2
+    first, second = values[:, :halfway], values[:, halfway:]
+    return jnp.concatenate(
+        [first * cosine - second * sine, second * cosine + first * sine], axis=1
+    )
+
+
+def spin_back(values, cosine, sine):
+    return spin(values, cosine, -sine)
+
+
+def whole(shape):
+    return pl.BlockSpec(shape, lambda *_: (0,) * len(shape), pipeline_mode=pl.Buffered(1))
+
+
+def params(megabytes):
+    return pltpu.CompilerParams(vmem_limit_bytes=megabytes * MB)
+
+
+def project(pieces, weight, cosine, sine):
+    rows, width = pieces[0].shape[1:]
+    tokens = 2 * rows
+
+    def kernel(*refs):
+        pieces_in, (weight_ref, cosine_ref, sine_ref, out, joined, held) = refs[:8], refs[8:]
+        chunk, chip = pl.program_id(0), pl.program_id(1)
+        load_pieces(pieces_in, held, chunk, chip)
+        values = held[...]
+        joined[0, 0] = values
+        product = dot(values, weight_ref[...])
+        angles = (cosine_ref[0], sine_ref[0])
+        query = spin(product[:, :HEAD], *angles) * (1.0 / math.sqrt(HEAD))
+        key = spin(product[:, HEAD : 2 * HEAD], *angles)
+        out[0, 0] = jnp.concatenate([query, key, product[:, 2 * HEAD :]], axis=1).astype(jnp.bfloat16)
+
+    here = lambda chunk, chip: (chunk, chip, 0, 0)
+    table = pl.BlockSpec((1, tokens, HEAD // 2), lambda chunk, chip: (chunk, 0, 0))
+    return pl.pallas_call(
+        kernel,
+        grid=(2, CHIPS),
+        in_specs=piece_specs(rows, width) + [whole(weight.shape), table, table],
+        out_specs=[
+            pl.BlockSpec((1, 1, tokens, 3 * HEAD), here),
+            pl.BlockSpec((1, 1, tokens, width), here),
+        ],
+        out_shape=[
+            jax.ShapeDtypeStruct((2, CHIPS, tokens, 3 * HEAD), jnp.bfloat16),
+            jax.ShapeDtypeStruct((2, CHIPS, tokens, width), jnp.bfloat16),
+        ],
+        scratch_shapes=[pltpu.VMEM((tokens, width), jnp.bfloat16)],
+        compiler_params=params(40),
+        cost_estimate=pl.CostEstimate(
+            flops=2 * 2 * CHIPS * tokens * width * 3 * HEAD,
+            bytes_accessed=3 * 2 * CHIPS * tokens * width * 2,
+            transcendentals=0,
+        ),
+    )(*pieces, weight, cosine, sine)
+
+
+def seen(place_q, place_k, chunk, count, tokens, lengths_ref, chip):
+    query_index = tokens * chunk + place_q
+    key_index = place_k[:, :count]
+    ahead_or_here = key_index <= query_index
+    if tokens * (chunk + 1) <= PROMPT:
+        return ahead_or_here
+
+    def segment(index):
+        found = jnp.full(index.shape, -1, jnp.int32)
+        for slot in range(NCONT):
+            found = jnp.where(index >= PROMPT + slot * CONT, slot, found)
+        return found
+
+    key_segment, query_segment = segment(key_index), segment(query_index)
+    end = jnp.full(key_index.shape, PROMPT, jnp.int32)
+    for slot in range(NCONT):
+        end = jnp.where(
+            key_segment == slot, PROMPT + slot * CONT + lengths_ref[chip, slot], end
+        )
+    alive = key_index < end
+    return ahead_or_here & ((key_segment < 0) | ((key_segment == query_segment) & alive))
+
+
+def attend(pair, states, lengths, place_q, place_k, output_weight):
+    tokens = states[0].shape[2]
+    rows = tokens // 2
+    width = output_weight.shape[1]
+    blocks = 2 * (pair + 1)
+
+    def kernel(*refs):
+        state_refs = refs[: pair + 1]
+        lengths_ref, place_q_ref, place_k_ref, weight_ref = refs[pair + 1 : pair + 5]
+        mixed_ref, outs, (keys, values) = refs[pair + 5], refs[pair + 6 : pair + 10], refs[pair + 10 :]
+        chunk_at, chip = pl.program_id(1), pl.program_id(0)
+
+        @pl.when(chunk_at == 0)
+        def _():
+            for block in range(blocks):
+                ref = state_refs[block // 2]
+                span = pl.ds(block * tokens, tokens)
+                keys[span] = ref[block % 2, 0, :, HEAD : 2 * HEAD]
+                values[span] = ref[block % 2, 0, :, 2 * HEAD :]
+
+        for side in range(2):
+
+            @pl.when(chunk_at == side)
+            def _():
+                chunk = 2 * pair + side
+                count = tokens * (chunk + 1)
+                scores = dot_t(state_refs[pair][side, 0, :, :HEAD], keys[:count])
+                mask = seen(
+                    place_q_ref[...], place_k_ref[...], chunk, count, tokens, lengths_ref, chip
+                )
+                scores = jnp.where(mask, scores, floor_score)
+                highest = jnp.max(scores, axis=1, keepdims=True)
+                exponent = jnp.exp(scores - highest)
+                total = jnp.sum(exponent, axis=1, keepdims=True)
+                probs = (exponent * (1.0 / total)).astype(jnp.bfloat16)
+                mixed = dot(probs, values[:count]).astype(jnp.bfloat16)
+                mixed_ref[0, 0] = mixed
+                store_partial(outs, dot(mixed, weight_ref[...]).astype(jnp.bfloat16), chunk_at)
+
+    turned = [
+        pl.BlockSpec(spec.block_shape, (lambda index_map: lambda chip, chunk: index_map(chip, chunk))(index_map))
+        for spec, index_map in zip(scatter_specs(rows, width), pair_maps())
+    ]
+    return pl.pallas_call(
+        kernel,
+        grid=(CHIPS, 2),
+        in_specs=[
+            pl.BlockSpec((2, 1, tokens, 3 * HEAD), lambda chip, chunk: (0, chip, 0, 0))
+            for _ in range(pair + 1)
+        ]
+        + [
+            pl.BlockSpec(memory_space=pltpu.SMEM),
+            whole(place_q.shape),
+            whole(place_k.shape),
+            whole(output_weight.shape),
+        ],
+        out_specs=[pl.BlockSpec((1, 1, tokens, HEAD), lambda chip, chunk: (chunk, chip, 0, 0))] + turned,
+        out_shape=[jax.ShapeDtypeStruct((2, CHIPS, tokens, HEAD), jnp.bfloat16)]
+        + [jax.ShapeDtypeStruct((CHIPS, rows, width), jnp.bfloat16)] * 4,
+        scratch_shapes=[pltpu.VMEM((blocks * tokens, HEAD), jnp.bfloat16)] * 2,
+        compiler_params=params(40),
+        cost_estimate=pl.CostEstimate(
+            flops=2 * CHIPS * 2 * tokens * (2 * blocks * tokens * HEAD + HEAD * width),
+            bytes_accessed=CHIPS * tokens * (2 * width * 2 + blocks * 3 * HEAD * 2),
+            transcendentals=CHIPS * 2 * tokens * blocks * tokens,
+        ),
+    )(*states[: pair + 1], lengths, place_q, place_k, output_weight)
+
+
+def pair_maps():
+    def first(chip, chunk):
+        return (chip, 0, 0)
+
+    def second(chip, chunk):
+        return ((chip % 2) * 2 + chip // 2, 0, 0)
+
+    return (first, first, second, second)
+
+
+def attend_back(pair, pieces, states, lengths, place_q, place_k, output_weight, weight, cosine, sine, carry):
+    rows, width = pieces[0].shape[1:]
+    tokens = 2 * rows
+    blocks = 2 * (pair + 1)
+    count_in = 8 + (pair + 1) + 7 + (0 if carry is None else 2)
+    earlier = pair > 0
+
+    def kernel(*refs):
+        pieces_in, state_refs = refs[:8], refs[8 : 9 + pair]
+        lengths_ref, place_q_ref, place_k_ref, out_weight, weight_ref, cosine_ref, sine_ref = refs[
+            9 + pair : 16 + pair
+        ]
+        carried = refs[16 + pair : count_in]
+        grads_ref, joined, *outs = refs[count_in : count_in + 6]
+        handed = refs[count_in + 6 : count_in + 6 + (2 if earlier else 0)]
+        held, keys, values, key_grads, value_grads, query_grads = refs[-6:]
+        chip, step = pl.program_id(0), pl.program_id(1)
+
+        def gather(side):
+            near, far = (0, 2) if side == 0 else (4, 6)
+            chosen = chip < 2 if side == 0 else chip % 2 == 0
+            for base, when in ((near, chosen), (far, jnp.logical_not(chosen))):
+
+                @pl.when(when)
+                def _():
+                    held[side, :rows] = pieces_in[base][0]
+                    held[side, rows:] = pieces_in[base + 1][0]
+
+        @pl.when(step == 0)
+        def _():
+            for block in range(blocks):
+                ref = state_refs[block // 2]
+                span = pl.ds(block * tokens, tokens)
+                keys[span] = ref[block % 2, 0, :, HEAD : 2 * HEAD]
+                values[span] = ref[block % 2, 0, :, 2 * HEAD :]
+            if carried:
+                for block in range(2):
+                    span = pl.ds(block * tokens, tokens)
+                    key_grads[span] = carried[0][block, 0]
+                    value_grads[span] = carried[1][block, 0]
+            else:
+                key_grads[...] = jnp.zeros_like(key_grads)
+                value_grads[...] = jnp.zeros_like(value_grads)
+            for side in range(2):
+                gather(side)
+
+        for side in range(2):
+
+            @pl.when(step == side)
+            def _():
+                chunk = 2 * pair + side
+                count = tokens * (chunk + 1)
+                branch = held[side]
+                joined[0, 0] = branch
+                mixed_grad = dot_t(branch, out_weight[...]).astype(jnp.bfloat16)
+                query = state_refs[pair][side, 0, :, :HEAD]
+                scores = dot_t(query, keys[:count])
+                mask = seen(
+                    place_q_ref[...], place_k_ref[...], chunk, count, tokens, lengths_ref, chip
+                )
+                scores = jnp.where(mask, scores, floor_score)
+                highest = jnp.max(scores, axis=1, keepdims=True)
+                exponent = jnp.exp(scores - highest)
+                probs = exponent * (1.0 / jnp.sum(exponent, axis=1, keepdims=True))
+                value_grads[:count] += dot_tn(probs.astype(jnp.bfloat16), mixed_grad)
+                prob_grad = dot_t(mixed_grad, values[:count])
+                inner = jnp.sum(probs * prob_grad, axis=1, keepdims=True)
+                score_grad = (probs * (prob_grad - inner)).astype(jnp.bfloat16)
+                key_grads[:count] += dot_tn(score_grad, query)
+                query_grad = dot(score_grad, keys[:count]) * (1.0 / math.sqrt(HEAD))
+                query_grads[side] = spin_back(query_grad, cosine_ref[side], sine_ref[side]).astype(
+                    jnp.bfloat16
+                )
+
+        for side in range(2):
+
+            @pl.when(step == 2 + side)
+            def _():
+                span = pl.ds((2 * pair + side) * tokens, tokens)
+                key_grad = spin_back(key_grads[span], cosine_ref[side], sine_ref[side])
+                grads = jnp.concatenate(
+                    [
+                        query_grads[side],
+                        key_grad.astype(jnp.bfloat16),
+                        value_grads[span].astype(jnp.bfloat16),
+                    ],
+                    axis=1,
+                )
+                grads_ref[0, 0] = grads
+                partial = dot_t(grads, weight_ref[...]).astype(jnp.bfloat16)
+                outs[2 * side][0] = partial[:rows]
+                outs[2 * side + 1][0] = partial[rows:]
+                if earlier:
+                    span = pl.ds(side * tokens, tokens)
+                    handed[0][side, 0] = key_grads[span]
+                    handed[1][side, 0] = value_grads[span]
+
+    def piece(index_map):
+        return pl.BlockSpec((1, rows, width), index_map)
+
+    first_near = piece(lambda chip, step: (jnp.minimum(chip, 1), 0, 0))
+    first_far = piece(lambda chip, step: (jnp.maximum(chip - 2, 0), 0, 0))
+    second = piece(lambda chip, step: (chip // 2, 0, 0))
+    state = pl.BlockSpec((2, 1, tokens, 3 * HEAD), lambda chip, step: (0, chip, 0, 0))
+    carry_spec = pl.BlockSpec((2, 1, tokens, HEAD), lambda chip, step: (0, chip, 0, 0))
+    carry_shape = jax.ShapeDtypeStruct((2, CHIPS, tokens, HEAD), jnp.float32)
+    return pl.pallas_call(
+        kernel,
+        grid=(CHIPS, 4),
+        in_specs=[first_near, first_near, first_far, first_far, second, second, second, second]
+        + [state] * (pair + 1)
+        + [
+            pl.BlockSpec(memory_space=pltpu.SMEM),
+            whole(place_q.shape),
+            whole(place_k.shape),
+            whole(output_weight.shape),
+            whole(weight.shape),
+            whole(cosine.shape),
+            whole(sine.shape),
+        ]
+        + ([] if carry is None else [carry_spec] * 2),
+        out_specs=[
+            pl.BlockSpec((1, 1, tokens, 3 * HEAD), lambda chip, step: (jnp.maximum(step - 2, 0), chip, 0, 0)),
+            pl.BlockSpec((1, 1, tokens, width), lambda chip, step: (jnp.minimum(step, 1), chip, 0, 0)),
+        ]
+        + [pl.BlockSpec((1, rows, width), index_map) for index_map in pair_maps()]
+        + ([carry_spec] * 2 if earlier else []),
+        out_shape=[
+            jax.ShapeDtypeStruct((2, CHIPS, tokens, 3 * HEAD), jnp.bfloat16),
+            jax.ShapeDtypeStruct((2, CHIPS, tokens, width), jnp.bfloat16),
+        ]
+        + [jax.ShapeDtypeStruct((CHIPS, rows, width), jnp.bfloat16)] * 4
+        + ([carry_shape] * 2 if earlier else []),
+        scratch_shapes=[
+            pltpu.VMEM((2, tokens, width), jnp.bfloat16),
+            pltpu.VMEM((blocks * tokens, HEAD), jnp.bfloat16),
+            pltpu.VMEM((blocks * tokens, HEAD), jnp.bfloat16),
+            pltpu.VMEM((blocks * tokens, HEAD), jnp.float32),
+            pltpu.VMEM((blocks * tokens, HEAD), jnp.float32),
+            pltpu.VMEM((2, tokens, HEAD), jnp.bfloat16),
+        ],
+        compiler_params=params(56),
+        cost_estimate=pl.CostEstimate(
+            flops=2 * CHIPS * 2 * tokens * (5 * blocks * tokens * HEAD + 4 * HEAD * width),
+            bytes_accessed=CHIPS * tokens * (6 * width * 2 + blocks * 3 * HEAD * 2),
+            transcendentals=CHIPS * 2 * tokens * blocks * tokens,
+        ),
+    )(
+        *pieces,
+        *states[: pair + 1],
+        lengths,
+        place_q,
+        place_k,
+        output_weight,
+        weight,
+        cosine,
+        sine,
+        *(() if carry is None else carry),
+    )
+
+
+def feed_forward(pieces, out_grads, weights, units):
+    rows, width = pieces[0].shape[1:]
+    tokens = 2 * rows
+    shards, _, columns = weights.shape
+    share = columns // 2
+
+    def kernel(*refs):
+        pieces_in, grads_in, weight_ref = refs[:8], refs[8:16], refs[16]
+        joined, joined_grad, hidden_ref, unit_grads, *outs = refs[17:29]
+        held, held_grad = refs[29:]
+        chunk, chip = pl.program_id(0), pl.program_id(1)
+        load_pieces(pieces_in, held, chunk, chip)
+        load_pieces(grads_in, held_grad, chunk, chip)
+        joined[0, 0] = held[...]
+        joined_grad[0, 0] = held_grad[...]
+        hidden_grad = dot_t(held_grad[:, :columns], weight_ref[0, width:, :])
+        for shard in range(1, shards):
+            hidden_grad += dot_t(
+                held_grad[:, shard * columns : (shard + 1) * columns], weight_ref[shard, width:, :]
+            )
+        for shard in range(shards):
+            both = dot(held[...], weight_ref[shard, :width, :])
+            gate, upward = both[:, :share], both[:, share:]
+            grad = hidden_grad[:, shard * share : (shard + 1) * share]
+            sigmoid = jax.nn.sigmoid(gate)
+            swish = gate * sigmoid
+            hidden_ref[0, 0, :, shard * share : (shard + 1) * share] = (swish * upward).astype(jnp.bfloat16)
+            gate_grad = grad * upward * sigmoid * (1.0 + gate * (1.0 - sigmoid))
+            unit_grads[0, 0, :, shard * columns : shard * columns + share] = gate_grad.astype(jnp.bfloat16)
+            unit_grads[0, 0, :, shard * columns + share : (shard + 1) * columns] = (grad * swish).astype(
+                jnp.bfloat16
+            )
+        back = dot_t(unit_grads[0, 0, :, :columns], weight_ref[0, :width, :])
+        for shard in range(1, shards):
+            back += dot_t(
+                unit_grads[0, 0, :, shard * columns : (shard + 1) * columns], weight_ref[shard, :width, :]
+            )
+        store_partial(outs[:4], back.astype(jnp.bfloat16), chunk)
+        for shard in range(shards):
+            span = slice(shard * columns, (shard + 1) * columns)
+            value = dot(hidden_ref[0, 0], weight_ref[shard, width:, :]).astype(jnp.bfloat16)
+            for place in range(2):
+
+                @pl.when(chunk == place)
+                def _():
+                    outs[4 + 2 * place][0, :, span] = value[:rows]
+                    outs[5 + 2 * place][0, :, span] = value[rows:]
+
+    here = lambda chunk, chip: (chunk, chip, 0, 0)
+    return pl.pallas_call(
+        kernel,
+        grid=(2, CHIPS),
+        in_specs=piece_specs(rows, width) * 2 + [whole(weights.shape)],
+        out_specs=[
+            pl.BlockSpec((1, 1, tokens, width), here),
+            pl.BlockSpec((1, 1, tokens, width), here),
+            pl.BlockSpec((1, 1, tokens, units), here),
+            pl.BlockSpec((1, 1, tokens, 2 * units), here),
+        ]
+        + scatter_specs(rows, width) * 2,
+        out_shape=[
+            jax.ShapeDtypeStruct((2, CHIPS, tokens, width), jnp.bfloat16),
+            jax.ShapeDtypeStruct((2, CHIPS, tokens, width), jnp.bfloat16),
+            jax.ShapeDtypeStruct((2, CHIPS, tokens, units), jnp.bfloat16),
+            jax.ShapeDtypeStruct((2, CHIPS, tokens, 2 * units), jnp.bfloat16),
+        ]
+        + [jax.ShapeDtypeStruct((CHIPS, rows, width), jnp.bfloat16)] * 8,
+        scratch_shapes=[pltpu.VMEM((tokens, width), jnp.bfloat16)] * 2,
+        compiler_params=params(60),
+        cost_estimate=pl.CostEstimate(
+            flops=2 * CHIPS * tokens * width * units * 2 * 6,
+            bytes_accessed=2 * CHIPS * tokens * (6 * width + 3 * units) * 2 + weights.size * 2,
+            transcendentals=2 * CHIPS * tokens * units,
+        ),
+    )(*pieces, *out_grads, weights)
+
+
+def token_dot(left, right):
+    return lax.dot_general(
+        left.reshape(-1, left.shape[-1]),
+        right.reshape(-1, right.shape[-1]),
+        (((0,), (0,)), ((), ())),
+        preferred_element_type=jnp.float32,
+    )
+
+
+def exchange(value, axis):
+    return lax.all_to_all(value, axis, split_axis=0, concat_axis=0, tiled=True)
+
+
+def plane_device(
+    activations,
+    cotangent,
+    continuation_lengths,
+    query_weight,
+    key_weight,
+    value_weight,
+    output_weight,
+    gate_weight,
+    up_weight,
+    down_weight,
+    attention_gain,
+    feedforward_gain,
+    moment_query,
+    moment_key,
+    moment_value,
+    moment_output,
+    moment_gate,
+    moment_up,
+    moment_down,
+    moment_attention,
+    moment_feedforward,
+):
+    devices, planes = lax.axis_size("dp"), lax.axis_size("fsdp")
+    place, plane = lax.axis_index("dp"), lax.axis_index("fsdp")
+    core = place % 2
+    low = jnp.bfloat16
+    kv_width = KV_HEADS * HEAD
+    tokens = activations.shape[1]
+    half = tokens // 2
+
+    inputs = to_planes(activations, core, plane)
+
+    in_rows = query_weight.shape[0]
+    sub_rows = in_rows // planes
+    mixed_kv = jnp.stack([key_weight.astype(low), value_weight.astype(low)], axis=1)
+    block = jnp.concatenate([query_weight.astype(low).reshape(in_rows, 2, HEAD), mixed_kv], axis=2)
+    block = exchange(block.reshape(planes, sub_rows, 2, 2 * HEAD), "fsdp")
+    block = block.transpose(0, 2, 1, 3).reshape(devices, sub_rows, 2 * HEAD)
+    block = exchange(block, "dp")
+    attention_block = jnp.concatenate(
+        [block.reshape(devices * sub_rows, 2 * HEAD), output_weight.astype(low)], axis=0
+    )
+    attention_all = lax.all_gather(attention_block, "fsdp", axis=0, tiled=False)
+    spread = devices * sub_rows
+    packed = (
+        attention_all[:, :spread]
+        .reshape(planes, devices, sub_rows, 2 * HEAD)
+        .transpose(1, 0, 2, 3)
+        .reshape(D, 2 * HEAD)
+    )
+    other_half = across(packed[:, HEAD:], CORE)
+    key_part = jnp.where(core == 0, packed[:, HEAD:], other_half)
+    value_part = jnp.where(core == 0, other_half, packed[:, HEAD:])
+    head_weight = jnp.concatenate([packed[:, :HEAD], key_part, value_part], axis=1)
+    head_output = attention_all[:, spread:].transpose(1, 0, 2).reshape(HEAD, D)
+
+    strip = 128
+    runs = gate_weight.shape[1] // (devices * strip)
+    units = runs * strip * planes
+    gate_up = jnp.stack(
+        [
+            gate_weight.astype(low).reshape(in_rows, runs, devices, strip),
+            up_weight.astype(low).reshape(in_rows, runs, devices, strip),
+        ]
+    )
+    gate_up = gate_up.transpose(3, 1, 0, 2, 4).reshape(devices, in_rows, 2 * runs * strip)
+    gate_up = exchange(gate_up, "dp").reshape(devices * in_rows, 2 * runs * strip)
+    down_columns = down_weight.shape[1]
+    down = exchange(down_weight.astype(low).reshape(devices, strip, down_columns), "dp")
+    feed_block = jnp.concatenate([gate_up, down.reshape(devices * strip, down_columns)], axis=0)
+    feed_weights = lax.all_gather(feed_block, "fsdp", axis=0, tiled=False)
+
+    out_grads = to_planes(cotangent, core, plane)
+
+    all_lengths = lax.all_gather(continuation_lengths, "dp", axis=0, tiled=True)
+    first_core = place - core
+    lengths = jnp.stack(
+        [
+            pick(all_lengths, ((first_core ^ mask) + plane // 2) * 2 + plane % 2)
+            for mask in (0, SIDE_A, SIDE_B, SIDE_A + SIDE_B)
+        ]
+    )
+
+    inside = jnp.concatenate(
+        [core * half + jnp.arange(half), (1 - core) * half + jnp.arange(half)]
+    ).astype(jnp.int32)
+    order = (tokens * jnp.arange(CHUNKS, dtype=jnp.int32)[:, None] + inside[None, :]).reshape(-1)
+    cosine, sine = rope_angles(token_places(order))
+    cosine = cosine.reshape(2, 2, tokens, HEAD // 2)
+    sine = sine.reshape(2, 2, tokens, HEAD // 2)
+    place_q, place_k = inside[:, None], order[None, :]
+
+    xs, ones, states, joins, mixes, middles, twos = [], [], [], [], [], [], []
+    near_pieces, grad_pieces, grad_rows = [], [], []
+    for pair in range(2):
+        own = jnp.stack(inputs[2 * pair : 2 * pair + 2]).astype(jnp.float32)
+        normed, factor = rms_rows(own, attention_gain)
+        normed = normed.astype(low)
+        xs.append(own)
+        ones.append(factor)
+        state, joined = project(
+            gather_pair(normed[0], normed[1]), head_weight, cosine[pair], sine[pair]
+        )
+        states.append(state)
+        joins.append(joined)
+    for pair in range(2):
+        grad_rows.append(out_grads[2 * pair : 2 * pair + 2])
+        grad_pieces.append(gather_pair(*grad_rows[pair]))
+    for pair in range(2):
+        mixed, *partials = attend(pair, states, lengths, place_q, place_k, head_output)
+        mixes.append(mixed)
+        middle = xs[pair] + scatter_pair([partials[:2], partials[2:]])
+        middles.append(middle)
+        normed_two, factor_two = rms_rows(middle, feedforward_gain)
+        normed_two = normed_two.astype(low)
+        twos.append(factor_two)
+        near_pieces.append(gather_pair(normed_two[0], normed_two[1]))
+
+    feed_sums, out_chunks, branches = [], [], []
+    middle_grads, branch_pieces = [None, None], [None, None]
+    feedforward_sum = jnp.zeros((D,), jnp.float32)
+    late_outputs = [None, None]
+    for pair in (1, 0):
+        joined_two, joined_grad, hidden, unit_grads, *partials = feed_forward(
+            near_pieces[pair], grad_pieces[pair], feed_weights, units
+        )
+        feed_sums.append((joined_two, joined_grad, hidden, unit_grads))
+        normed_grad = scatter_pair([partials[0:2], partials[2:4]])
+        back, gain_grad = rms_back(
+            middles[pair].reshape(-1, D), twos[pair].reshape(-1, 1), feedforward_gain, normed_grad.reshape(-1, D)
+        )
+        feedforward_sum = feedforward_sum + gain_grad
+        middle_grads[pair] = jnp.stack(grad_rows[pair]).astype(jnp.float32) + back.reshape(2, half, D)
+        branch = middle_grads[pair].astype(low)
+        branch_pieces[pair] = gather_pair(branch[0], branch[1])
+        late_outputs[pair] = partials[4:]
+    gate_up_sum = reduce(jnp.add, [token_dot(two, grads) for two, _, _, grads in feed_sums])
+    down_sum = reduce(jnp.add, [token_dot(hidden, grads) for _, grads, hidden, _ in feed_sums])
+    feed_grad = jnp.concatenate([gate_up_sum.astype(low), down_sum.astype(low)], axis=0)
+    feed_grad = feed_grad.reshape(-1, planes, 2 * runs * strip).transpose(1, 0, 2)
+    feed_grad = lax.psum_scatter(feed_grad, "fsdp", scatter_dimension=0, tiled=False)
+    gate_up_owned = exchange(feed_grad[:D].reshape(devices, in_rows, 2 * runs * strip), "dp")
+    gate_up_owned = gate_up_owned.reshape(devices, in_rows, 2, runs, strip).transpose(2, 1, 3, 0, 4)
+    gate_up_owned = gate_up_owned.reshape(2, in_rows, runs * devices * strip)
+    down_owned = exchange(feed_grad[D:].reshape(devices, strip, down_columns), "dp")
+    down_owned = down_owned.reshape(devices * strip, down_columns)
+
+    out_chunks = [None] * CHUNKS
+    for pair in range(2):
+        result = middles[pair] + scatter_pair([late_outputs[pair][0:2], late_outputs[pair][2:4]])
+        out_chunks[2 * pair], out_chunks[2 * pair + 1] = result[0].astype(low), result[1].astype(low)
+    outputs = from_planes(out_chunks, core, plane)
+
+    carry = None
+    in_chunks = [None] * CHUNKS
+    head_terms, output_terms = [], []
+    attention_sum = jnp.zeros((D,), jnp.float32)
+    for pair in (1, 0):
+        head_grads, joined_branch, *rest = attend_back(
+            pair,
+            branch_pieces[pair],
+            states,
+            lengths,
+            place_q,
+            place_k,
+            head_output,
+            head_weight,
+            cosine[pair],
+            sine[pair],
+            carry,
+        )
+        partials, carry = rest[:4], rest[4:]
+        head_terms.append(token_dot(joins[pair], head_grads))
+        output_terms.append(token_dot(mixes[pair], joined_branch))
+        normed_grad = scatter_pair([partials[0:2], partials[2:4]])
+        back, gain_grad = rms_back(
+            xs[pair].reshape(-1, D), ones[pair].reshape(-1, 1), attention_gain, normed_grad.reshape(-1, D)
+        )
+        attention_sum = attention_sum + gain_grad
+        result = (middle_grads[pair] + back.reshape(2, half, D)).astype(low)
+        in_chunks[2 * pair], in_chunks[2 * pair + 1] = result[0], result[1]
+    head_sum = reduce(jnp.add, head_terms).astype(low)
+    output_sum = reduce(jnp.add, output_terms).astype(low)
+    given = jnp.where(core == 0, head_sum[:, 2 * HEAD :], head_sum[:, HEAD : 2 * HEAD])
+    kept = jnp.where(core == 0, head_sum[:, HEAD : 2 * HEAD], head_sum[:, 2 * HEAD :])
+    kv_sum = (kept.astype(jnp.float32) + across(given, CORE).astype(jnp.float32)).astype(low)
+    head_sum = jnp.concatenate([head_sum[:, :HEAD], kv_sum], axis=1)
+    head_sum = head_sum.reshape(devices, planes, sub_rows, 2 * HEAD).transpose(1, 0, 2, 3)
+    head_sum = head_sum.reshape(planes, spread, 2 * HEAD)
+    output_sum = output_sum.reshape(HEAD, planes, 2 * HEAD).transpose(1, 0, 2)
+    attention_grad = lax.psum_scatter(
+        jnp.concatenate([head_sum, output_sum], axis=1), "fsdp", scatter_dimension=0, tiled=False
+    )
+    output_owned = attention_grad[spread:]
+    block = exchange(attention_grad[:spread].reshape(devices, sub_rows, 2 * HEAD), "dp")
+    block = block.reshape(planes, 2, sub_rows, 2 * HEAD).transpose(0, 2, 1, 3)
+    block = exchange(block, "fsdp").reshape(in_rows, 2, 2 * HEAD)
+    query_owned = block[:, :, :HEAD].reshape(in_rows, 2 * HEAD)
+    key_owned, value_owned = block[:, 0, HEAD:], block[:, 1, HEAD:]
+    input_grad = from_planes(in_chunks, core, plane)
+
+    owner_grads = [
+        owned.astype(jnp.float32)
+        for owned in (
+            query_owned,
+            key_owned,
+            value_owned,
+            output_owned,
+            gate_up_owned[0],
+            gate_up_owned[1],
+            down_owned,
+        )
+    ]
+    local_square = reduce(jnp.add, [jnp.sum(owned * owned) for owned in owner_grads])
+    attention_total, feedforward_total, square_total = lax.psum(
+        (attention_sum, feedforward_sum, local_square), ("dp", "fsdp")
+    )
+    square_sum = (
+        square_total
+        + jnp.sum(attention_total * attention_total)
+        + jnp.sum(feedforward_total * feedforward_total)
+    )
+    grad_norm = jnp.sqrt(square_sum)
+    entry_count = 2 * D * D + 2 * D * kv_width + 3 * D * FF + 2 * D
+    limit = clip_level * math.sqrt(entry_count)
+    factor = limit / jnp.maximum(grad_norm, limit)
+    gradients = owner_grads + [attention_total, feedforward_total]
+    old_moments = [
+        moment_query,
+        moment_key,
+        moment_value,
+        moment_output,
+        moment_gate,
+        moment_up,
+        moment_down,
+        moment_attention,
+        moment_feedforward,
+    ]
+    old_params = [
+        query_weight,
+        key_weight,
+        value_weight,
+        output_weight,
+        gate_weight,
+        up_weight,
+        down_weight,
+        attention_gain,
+        feedforward_gain,
+    ]
+    new_moments = [
+        0.5 * moment + 0.5 * factor * gradient for moment, gradient in zip(old_moments, gradients)
+    ]
+    new_params = []
+    for at, param in enumerate(old_params):
+        if at < 7:
+            new_params.append(param - step_size * (new_moments[at] + decay_rate * param))
+        else:
+            new_params.append(param - gain_step * new_moments[at])
+    return (outputs, input_grad, grad_norm, *new_moments, *new_params)
+
+
 def solution(mesh):
+    whole_groups_on_planes = mesh.shape["dp"] == HEADS and mesh.shape["fsdp"] == KV_HEADS
+    body = plane_device if whole_groups_on_planes else on_device
     placed = (
         P("dp", "fsdp", None),
         P("dp", "fsdp", None),
@@ -426,7 +1251,7 @@
         P(),
     )
     return jax.shard_map(
-        on_device,
+        body,
         mesh=mesh,
         in_specs=placed,
         out_specs=(

time: 5370 us -> 1810 us (0.34)
  waiting for transfers between devices: 3780 us -> 855 us
  blocking collectives: 526 us -> 81.5 us
  matrix products: 503 us -> 116 us
  Pallas kernels: 0 us -> 309 us
  local copies, waits for them, and re-layouts: 323 us -> 90 us
  starting transfers between devices: 35.6 us -> 184 us
    all_gather x23 -> x2, waiting for transfers between devices: 2800 us -> 0.01 us  [the longest x1 0.01 us: plane_device(): attention_all = lax.all_gather(attention_block, 'fsdp', axis=0, tiled=False)]
    ppermute x0 -> x130, waiting for transfers between devices: none -> 771 us  [the longest x118 526 us: across(): lax.ppermute(value, 'dp', [(place, place ^ mask) for place in range(count)])]
    all_to_all x2 -> x1, blocking collectives: 486 us -> 20.6 us  [exchange(): return lax.all_to_all(value, axis, split_axis=0, concat_axis=0, tiled=True)]
    all_to_all x6 -> x7, waiting for transfers between devices: 511 us -> 70.4 us  [exchange(): return lax.all_to_all(value, axis, split_axis=0, concat_axis=0, tiled=True)]
    dot_general x36 -> x8, matrix products: 503 us -> 116 us  [token_dot(): lax.dot_general(left.reshape(-1, left.shape[-1]), right.reshape(-1, right...]
    pallas_call x0 -> x8, Pallas kernels: none -> 309 us  [the longest x2 175 us: feed_forward(): pl.pallas_call(kernel, grid=(2, CHIPS), in_specs=piece_specs(rows, width)...]
    reduce_scatter x9 -> x2, waiting for transfers between devices: 294 us -> 14.2 us  [the longest x1 14.2 us: plane_device(): lax.psum_scatter(feed_grad, 'fsdp', scatter_dimension=0, tiled=False)]
    unnamed x34 -> x4, waiting for transfers between devices: 175 us -> 0.07 us
  transfers between devices with their start and end apart: 39 -> 141, of which waited for: 29 -> 61; matrix products, arithmetic and copies ran while one was open for 12% -> 15% of each run, Pallas kernels for 0% -> 5%
where the time goes in v1:
time: 1810 us
  waiting for transfers between devices  855 us (47%)
  Pallas kernels  309 us (17%)
  starting transfers between devices  184 us (10%)
  other arithmetic  147 us (8%)
  matrix products  116 us (6%)
  local copies, waits for them, and re-layouts  90 us (5%)
  blocking collectives  81.5 us (5%)
  between operations  24.5 us (1%)
    ppermute x118, waiting for transfers between devices, across(): lax.ppermute(value, 'dp', [(place, place ^ mask) for place in range(count)])  526 us
    ppermute x12, waiting for transfers between devices, along(): lax.ppermute(value, 'fsdp', [(place, place ^ mask) for place in range(cou...  245 us
    pallas_call x2, Pallas kernels, feed_forward(): pl.pallas_call(kernel, grid=(2, CHIPS), in_specs=piece_specs(rows, width)...  175 us
    dot_general x8, matrix products, token_dot(): lax.dot_general(left.reshape(-1, left.shape[-1]), right.reshape(-1, right...  116 us
    ppermute x118, starting transfers between devices, across(): lax.ppermute(value, 'dp', [(place, place ^ mask) for place in range(count)])  81.9 us
    pallas_call x2, Pallas kernels, attend_back(): pl.pallas_call(kernel, grid=(CHIPS, 4), in_specs=[first_near, first_near,...  79.1 us
    all_to_all x7, waiting for transfers between devices, exchange(): return lax.all_to_all(value, axis, split_axis=0, concat_axis=0, tiled=True)  70.4 us
    all_to_all x7, starting transfers between devices, exchange(): return lax.all_to_all(value, axis, split_axis=0, concat_axis=0, tiled=True)  60.3 us
  transfers between devices with their start and end apart: 141, of which 61 were waited for; matrix products, arithmetic and copies ran while one was open for 15% of the time, Pallas kernels for 5%

profile of v1, /device:TPU:0, one launch (start us, length us, event | category | flops | bytes accessed | tf_op | source)
XLA Modules:
  0.0 1807.1 jit_solution(3453587194428605312)
XLA Ops:
  11.5 20.6 %all_to_all.40 = bf16[4,64,2,512]{3,2,1,0:T(2,128)(2,1)S(1)} all-to-all(bf16[4,64,2,512]{3,2,1,0:T(2,128)(2,1)S(1)} %maximum_maximum_fusion), channel_id=1, replica_groups=mesh['dp'=8,'fsdp'=4] {'fsdp'}, dimensions={0} | all-to-all | bytes 1048576 | tf_op jit(solution)/shard_map/all_to_all | solution.py:962
  92.5 28.0 %collective-permute-done.1 = bf16[144,2048]{1,0:T(8,128)(2,1)} collective-permute-done((bf16[144,2048]{1,0:T(8,128)(2,1)}, bf16[144,2048]{1,0:T(8,128)(2,1)}, u32[]{:S(2)}, u32[]{:S(2)}) %collective-permute-start.1) | collective-permute-done | bytes 589856 | tf_op jit(solution)/shard_map/ppermute | solution.py:419
  123.5 21.9 %collective-permute-done.3 = bf16[144,2048]{1,0:T(8,128)(2,1)} collective-permute-done((bf16[144,2048]{1,0:T(8,128)(2,1)}, bf16[144,2048]{1,0:T(8,128)(2,1)}, u32[]{:S(2)}, u32[]{:S(2)}) %collective-permute-start.3) | collective-permute-done | bytes 589856 | tf_op jit(solution)/shard_map/ppermute | solution.py:419
  192.1 46.1 %collective-permute-done.4 = bf16[144,2048]{1,0:T(8,128)(2,1)S(1)} collective-permute-done((bf16[144,2048]{1,0:T(8,128)(2,1)S(1)}, bf16[144,2048]{1,0:T(8,128)(2,1)S(1)}, u32[]{:S(2)}, u32[]{:S(2)}) %collective-permute-start.4) | collective-permute-done | bytes 589856 | tf_op jit(solution)/shard_map/ppermute | solution.py:414
  352.8 45.8 %collective-permute-done.28 = bf16[144,2048]{1,0:T(8,128)(2,1)S(1)} collective-permute-done((bf16[144,2048]{1,0:T(8,128)(2,1)S(1)}, bf16[144,2048]{1,0:T(8,128)(2,1)S(1)}, u32[]{:S(2)}, u32[]{:S(2)}) %collective-permute-start.28) | collective-permute-done | bytes 589856 | tf_op jit(solution)/shard_map/ppermute | solution.py:419
  523.3 91.5 %shard_map.369 = (bf16[2,4,288,2048]{3,2,1,0:T(8,128)(2,1)}, bf16[2,4,288,2048]{3,2,1,0:T(8,128)(2,1)}, bf16[2,4,288,1024]{3,2,1,0:T(8,128)(2,1)}, bf16[2,4,288,...) custom-call(bf16[2,144,2048]{2,1,0:T(8,128)(2,1)} %copy-done.104, ...), custom_call_target="tpu_custom_call" | custom-call | flops 57982058496 | bytes 83361792 | tf_op jit(solution)/shard_map/pallas_call | solution.py:924
  625.8 24.8 %collective-permute-done.100 = bf16[2,144,2048]{2,1,0:T(8,128)(2,1)S(1)} collective-permute-done((bf16[2,144,2048]{2,1,0:T(8,128)(2,1)S(1)}, bf16[2,144,2048]{2,1,0:T(8,128)(2,1)S(1)}, u32[]{:S(2)}, u32[]{:S(2)}) %collective-permute-start.100) | collective-permute-done | bytes 1179680 | tf_op jit(solution)/shard_map/ppermute | solution.py:414
  717.5 36.0 %collective-permute-done.35 = bf16[144,2048]{1,0:T(8,128)(2,1)S(1)} collective-permute-done((bf16[144,2048]{1,0:T(8,128)(2,1)S(1)}, bf16[144,2048]{1,0:T(8,128)(2,1)S(1)}, u32[]{:S(2)}, u32[]{:S(2)}) %collective-permute-start.35) | collective-permute-done | bytes 589856 | tf_op jit(solution)/shard_map/ppermute | solution.py:414
  764.2 42.3 %shard_map.370 = (bf16[2,4,288,768]{3,2,1,0:T(8,128)(2,1)}, bf16[2,4,288,2048]{3,2,1,0:T(8,128)(2,1)}, bf16[4,144,2048]{2,1,0:T(8,128)(2,1)}, bf16[4,144,2048]{2...) custom-call(bf16[2,144,2048]{2,1,0:T(8,128)(2,1)} %copy-done.101, ...), custom_call_target="tpu_custom_call" | custom-call | flops 16458448896 | bytes 35389440 | tf_op jit(solution)/shard_map/pallas_call | solution.py:820
  816.2 21.2 %collective-permute-done.76 = bf16[2,144,2048]{2,1,0:T(8,128)(2,1)S(1)} collective-permute-done((bf16[2,144,2048]{2,1,0:T(8,128)(2,1)S(1)}, bf16[2,144,2048]{2,1,0:T(8,128)(2,1)S(1)}, u32[]{:S(2)}, u32[]{:S(2)}) %collective-permute-start.76) | collective-permute-done | bytes 1179680 | tf_op jit(solution)/shard_map/ppermute | solution.py:414
  842.4 24.4 %collective-permute-done.79 = bf16[2,144,2048]{2,1,0:T(8,128)(2,1)S(1)} collective-permute-done((bf16[2,144,2048]{2,1,0:T(8,128)(2,1)S(1)}, bf16[2,144,2048]{2,1,0:T(8,128)(2,1)S(1)}, u32[]{:S(2)}, u32[]{:S(2)}) %collective-permute-start.79) | collective-permute-done | bytes 1179680 | tf_op jit(solution)/shard_map/ppermute | solution.py:414
  882.7 21.4 %collective-permute-done.123 = bf16[2,144,2048]{2,1,0:T(8,128)(2,1)S(1)} collective-permute-done((bf16[2,144,2048]{2,1,0:T(8,128)(2,1)S(1)}, bf16[2,144,2048]{2,1,0:T(8,128)(2,1)S(1)}, u32[]{:S(2)}, u32[]{:S(2)}) %collective-permute-start.123) | collective-permute-done | bytes 1179680 | tf_op jit(solution)/shard_map/ppermute | solution.py:414
  944.7 22.5 %collective-permute-done.33.refs_10_ = bf16[2,144,2048]{2,1,0:T(8,128)(2,1)S(1)} collective-permute-done((bf16[2,144,2048]{2,1,0:T(8,128)(2,1)S(1)}, bf16[2,144,2048]{2,1,0:T(8,128)(2,1)S(1)}, u32[]{:S(2)}, u32[]{:S(2)}) %collective-permute-start.33) | collective-permute-done | bytes 1179680 | tf_op jit(solution)/shard_map/ppermute | solution.py:414
  993.2 83.4 %shard_map.366 = (bf16[2,4,288,2048]{3,2,1,0:T(8,128)(2,1)}, bf16[2,4,288,2048]{3,2,1,0:T(8,128)(2,1)}, bf16[2,4,288,1024]{3,2,1,0:T(8,128)(2,1)}, bf16[2,4,288,...) custom-call(bf16[2,144,2048]{2,1,0:T(8,128)(2,1)} %copy-done.105, ...), custom_call_target="tpu_custom_call" | custom-call | flops 57982058496 | bytes 83361792 | tf_op jit(solution)/shard_map/pallas_call | solution.py:924
  1086.2 25.1 %collective-permute-done.86 = bf16[2,144,2048]{2,1,0:T(8,128)(2,1)S(1)} collective-permute-done((bf16[2,144,2048]{2,1,0:T(8,128)(2,1)S(1)}, bf16[2,144,2048]{2,1,0:T(8,128)(2,1)S(1)}, u32[]{:S(2)}, u32[]{:S(2)}) %collective-permute-start.86) | collective-permute-done | bytes 1179680 | tf_op jit(solution)/shard_map/ppermute | solution.py:414
  1133.1 27.2 %fusion.131 = f32[2048,2048,1,1]{1,0,3,2:T(8,128)} fusion(bf16[2,4,288,2048]{3,2,1,0:T(8,128)(2,1)} %get-tuple-element.117, bf16[2,4,288,2048]{3,2,1,0:T(8,128)(2,1)} %get-tuple-element.118), kind=kOutput, calls=%fused_computation.382 | convolution fusion | flops 19327352832 | bytes 35651584 | tf_op jit(solution)/shard_map/dot_general | solution.py:953
  1202.0 36.8 %shard_map.371 = (bf16[2,4,288,768]{3,2,1,0:T(8,128)(2,1)}, bf16[2,4,288,2048]{3,2,1,0:T(8,128)(2,1)}, bf16[4,144,2048]{2,1,0:T(8,128)(2,1)}, bf16[4,144,2048]{2...) custom-call(bf16[2,144,2048]{2,1,0:T(8,128)(2,1)} %copy-done.107, ...), custom_call_target="tpu_custom_call" | custom-call | flops 13061062656 | bytes 31850496 | tf_op jit(solution)/shard_map/pallas_call | solution.py:820
  1279.6 24.6 %fusion = bf16[2048,2048]{1,0:T(8,128)(2,1)S(1)} fusion(f32[2048,2048,1,1]{1,0,3,2:T(8,128)} %fusion.131, bf16[2,4,288,2048]{3,2,1,0:T(8,128)(2,1)S(1)} %bitcast.469, bf16[2,4,288,2048]{3,2,1,0:T(8,128)(2,1)} %get-tuple-element.120), kind=kOutput, calls=%fused_computation.1 | convolution fusion | flops 19335741440 | bytes 44040192 | tf_op jit(solution)/shard_map/dot_general | solution.py:953
  1333.3 23.7 %collective-permute-done.40 = bf16[2,144,2048]{2,1,0:T(8,128)(2,1)S(1)} collective-permute-done((bf16[2,144,2048]{2,1,0:T(8,128)(2,1)S(1)}, bf16[2,144,2048]{2,1,0:T(8,128)(2,1)S(1)}, u32[]{:S(2)}, u32[]{:S(2)}) %collective-permute-start.40) | collective-permute-done | bytes 1179680 | tf_op jit(solution)/shard_map/ppermute | solution.py:414
  1438.4 45.7 %collective-permute-done.81 = bf16[144,2048]{1,0:T(8,128)(2,1)S(1)} collective-permute-done((bf16[144,2048]{1,0:T(8,128)(2,1)S(1)}, bf16[144,2048]{1,0:T(8,128)(2,1)S(1)}, u32[]{:S(2)}, u32[]{:S(2)}) %collective-permute-start.81) | collective-permute-done | bytes 589856 | tf_op jit(solution)/shard_map/ppermute | solution.py:419
  1526.7 36.3 %all-to-all-start.5 = ((bf16[4,64,2,512]{3,1,2,0:T(8,128)(2,1)}), bf16[4,64,2,512]{3,1,2,0:T(8,128)(2,1)S(1)}, u32[]{:S(2)}, u32[]{:S(2)}) async-start(bf16[4,64,2,512]{3,1,2,0:T(8,128)(2,1)} %bitcast.154), calls=%async_computation.6 | async-start | bytes 1048576 | tf_op jit(solution)/shard_map/all_to_all | solution.py:962
  1564.5 50.7 %collective-permute-done.126 = bf16[144,2048]{1,0:T(8,128)(2,1)} collective-permute-done((bf16[144,2048]{1,0:T(8,128)(2,1)}, bf16[144,2048]{1,0:T(8,128)(2,1)}, u32[]{:S(2)}, u32[]{:S(2)}) %collective-permute-start.126) | collective-permute-done | bytes 589856 | tf_op jit(solution)/shard_map/ppermute | solution.py:419
  1634.8 24.0 %all-to-all-done.5 = bf16[4,64,2,512]{3,1,2,0:T(8,128)(2,1)S(1)} async-done(((bf16[4,64,2,512]{3,1,2,0:T(8,128)(2,1)}), bf16[4,64,2,512]{3,1,2,0:T(8,128)(2,1)S(1)}, u32[]{:S(2)}, u32[]{:S(2)}) %all-to-all-start.5) | async-done | bytes 524320 | tf_op jit(solution)/shard_map/all_to_all | solution.py:962
  1719.7 42.3 %all-reduce = (f32[]{:T(128)}, f32[2048]{0:T(1024)S(1)}, f32[2048]{0:T(1024)S(1)}) all-reduce(f32[]{:T(128)S(6)} %add.900, f32[2048]{0:T(1024)S(1)} %copy-done.127, f32[2048]{0:T(1024)S(1)} %copy-done.126), channel_id=1, replica_groups=mesh['dp'=8,'fsdp'=4] {'dp','fsdp'}, use_global_device_ids=true, to_apply=%region_17.18 | all-reduce | flops 4097 | bytes 32776 | tf_op jit(solution)/shard_map/psum | solution.py:1180
  (851 shorter events, 916.3 us)
Async XLA Ops:
  36.8 205.6 %all-gather.6.cloned.1.call-start = ((), (), s32[]{:S(2)}) async-start(), calls=%async_computation.12 | async-start | bytes 3932160 | tf_op jit(solution)/shard_map/all_gather | solution.py:1008
  68.3 77.1 %collective-permute-start.3 = (bf16[144,2048]{1,0:T(8,128)(2,1)}, bf16[144,2048]{1,0:T(8,128)(2,1)}, u32[]{:S(2)}, u32[]{:S(2)}) collective-permute-start(bf16[144,2048]{1,0:T(8,128)(2,1)} %get-tuple-element.335), channel_id=1, source_target_pairs={{0,3},{1,2},{2,1},{3,0},{4,7},{5,6},{6,5},{7,4},{8,11},{9,10},{10,... | collective-permute-start | bytes 1769480 | tf_op jit(solution)/shard_map/ppermute | solution.py:419
  88.9 63.5 %all-to-all-start.3 = ((bf16[8,128,512]{2,1,0:T(8,128)(2,1)}), bf16[8,128,512]{2,1,0:T(8,128)(2,1)S(1)}, u32[]{:S(2)}, u32[]{:S(2)}) async-start(bf16[8,128,512]{2,1,0:T(8,128)(2,1)} %bitcast.55), calls=%async_computation.3 | async-start | bytes 2097152 | tf_op jit(solution)/shard_map/all_to_all | solution.py:962
  92.4 430.9 %all-gather.8.cloned.1.call-start = ((), (), s32[]{:S(2)}) async-start(), calls=%async_computation.13 | async-start | bytes 15728640 | tf_op jit(solution)/shard_map/all_gather | solution.py:1036
  155.9 1355.1 %reduce-scatter.3.cloned.1.call-start = ((), (), s32[]{:S(2)}) async-start(), calls=%async_computation.10 | async-start | bytes 3932160 | tf_op jit(solution)/shard_map/reduce_scatter | solution.py:1156
  174.9 70.6 %collective-permute-start.51 = (bf16[2,144,2048]{2,1,0:T(8,128)(2,1)}, bf16[2,144,2048]{2,1,0:T(8,128)(2,1)S(1)}, u32[]{:S(2)}, u32[]{:S(2)}) collective-permute-start(bf16[2,144,2048]{2,1,0:T(8,128)(2,1)} %pad_maximum_fusion.27.refs_4_), channel_id=1, source_target_pairs={{0,8},{4,12},{8,0},{12,4},{16,24},{20,28},{24,16},{28,20},{1,9},{5... | collective-permute-start | bytes 3538952 | tf_op jit(solution)/shard_map/ppermute | solution.py:414
  331.4 67.1 %collective-permute-start.28 = (bf16[144,2048]{1,0:T(8,128)(2,1)S(1)}, bf16[144,2048]{1,0:T(8,128)(2,1)S(1)}, u32[]{:S(2)}, u32[]{:S(2)}) collective-permute-start(bf16[144,2048]{1,0:T(8,128)(2,1)S(1)} %get-tuple-element.329), channel_id=1, source_target_pairs={{0,1},{1,0},{2,3},{3,2},{4,5},{5,4},{6,7},{7,6},{8,9},{9,8},{10,11... | collective-permute-start | bytes 1769480 | tf_op jit(solution)/shard_map/ppermute | solution.py:419
  347.3 64.9 %collective-permute-start.29 = (bf16[144,2048]{1,0:T(8,128)(2,1)S(1)}, bf16[144,2048]{1,0:T(8,128)(2,1)S(1)}, u32[]{:S(2)}, u32[]{:S(2)}) collective-permute-start(bf16[144,2048]{1,0:T(8,128)(2,1)S(1)} %get-tuple-element.330), channel_id=1, source_target_pairs={{0,2},{1,3},{2,0},{3,1},{4,6},{5,7},{6,4},{7,5},{8,10},{9,11},{10,... | collective-permute-start | bytes 1769480 | tf_op jit(solution)/shard_map/ppermute | solution.py:419
  347.8 76.0 %collective-permute-start.30 = (bf16[144,2048]{1,0:T(8,128)(2,1)S(1)}, bf16[144,2048]{1,0:T(8,128)(2,1)S(1)}, u32[]{:S(2)}, u32[]{:S(2)}) collective-permute-start(bf16[144,2048]{1,0:T(8,128)(2,1)S(1)} %get-tuple-element.331), channel_id=1, source_target_pairs={{0,3},{1,2},{2,1},{3,0},{4,7},{5,6},{6,5},{7,4},{8,11},{9,10},{10,... | collective-permute-start | bytes 1769480 | tf_op jit(solution)/shard_map/ppermute | solution.py:419
  350.2 77.2 %collective-permute-start.54 = (bf16[2,144,2048]{2,1,0:T(8,128)(2,1)S(1)}, bf16[2,144,2048]{2,1,0:T(8,128)(2,1)S(1)}, u32[]{:S(2)}, u32[]{:S(2)}) collective-permute-start(bf16[2,144,2048]{2,1,0:T(8,128)(2,1)S(1)} %add_convert_fusion.11), channel_id=1, source_target_pairs={{0,16},{4,20},{8,24},{12,28},{16,0},{20,4},{24,8},{28,12},{1,17},{... | collective-permute-start | bytes 3538952 | tf_op jit(solution)/shard_map/ppermute | solution.py:414
  352.2 76.1 %collective-permute-start.57 = (bf16[2,144,2048]{2,1,0:T(8,128)(2,1)S(1)}, bf16[2,144,2048]{2,1,0:T(8,128)(2,1)S(1)}, u32[]{:S(2)}, u32[]{:S(2)}) collective-permute-start(bf16[2,144,2048]{2,1,0:T(8,128)(2,1)S(1)} %add_convert_fusion.10), channel_id=1, source_target_pairs={{0,8},{4,12},{8,0},{12,4},{16,24},{20,28},{24,16},{28,20},{1,9},{5... | collective-permute-start | bytes 3538952 | tf_op jit(solution)/shard_map/ppermute | solution.py:414
  678.7 74.8 %collective-permute-start.17 = (bf16[2,144,2048]{2,1,0:T(8,128)(2,1)S(1)}, bf16[2,144,2048]{2,1,0:T(8,128)(2,1)S(1)}, u32[]{:S(2)}, u32[]{:S(2)}) collective-permute-start(bf16[2,144,2048]{2,1,0:T(8,128)(2,1)S(1)} %add_convert_fusion.14), channel_id=1, source_target_pairs={{0,8},{4,12},{8,0},{12,4},{16,24},{20,28},{24,16},{28,20},{1,9},{5... | collective-permute-start | bytes 3538952 | tf_op jit(solution)/shard_map/ppermute | solution.py:414
  691.3 62.7 %collective-permute-start.111 = (bf16[2,144,2048]{2,1,0:T(8,128)(2,1)S(1)}, bf16[2,144,2048]{2,1,0:T(8,128)(2,1)S(1)}, u32[]{:S(2)}, u32[]{:S(2)}) collective-permute-start(bf16[2,144,2048]{2,1,0:T(8,128)(2,1)S(1)} %pad_maximum_fusion.34.refs_4_), channel_id=1, source_target_pairs={{0,8},{4,12},{8,0},{12,4},{16,24},{20,28},{24,16},{28,20},{1,9},{5... | collective-permute-start | bytes 3538952 | tf_op jit(solution)/shard_map/ppermute | solution.py:414
  758.8 169.2 %collective-permute-start.31 = (bf16[144,2048]{1,0:T(8,128)(2,1)S(1)}, bf16[144,2048]{1,0:T(8,128)(2,1)}, u32[]{:S(2)}, u32[]{:S(2)}) collective-permute-start(bf16[144,2048]{1,0:T(8,128)(2,1)S(1)} %bitcast.411), channel_id=1, source_target_pairs={{0,8},{4,12},{8,0},{12,4},{16,24},{20,28},{24,16},{28,20},{1,9},{5... | collective-permute-start | bytes 1769480 | tf_op jit(solution)/shard_map/ppermute | solution.py:414
  812.7 117.1 %collective-permute-start.37 = (bf16[2,144,2048]{2,1,0:T(8,128)(2,1)S(1)}, bf16[2,144,2048]{2,1,0:T(8,128)(2,1)S(1)}, u32[]{:S(2)}, u32[]{:S(2)}) collective-permute-start(bf16[2,144,2048]{2,1,0:T(8,128)(2,1)S(1)} %copy-done.94), channel_id=1, source_target_pairs={{0,8},{4,12},{8,0},{12,4},{16,24},{20,28},{24,16},{28,20},{1,9},{5... | collective-permute-start | bytes 3538952 | tf_op jit(solution)/shard_map/ppermute | solution.py:414
  879.5 63.7 %collective-permute-start.36 = (bf16[2,144,2048]{2,1,0:T(8,128)(2,1)S(1)}, bf16[2,144,2048]{2,1,0:T(8,128)(2,1)S(1)}, u32[]{:S(2)}, u32[]{:S(2)}) collective-permute-start(bf16[2,144,2048]{2,1,0:T(8,128)(2,1)S(1)} %copy-done.94), channel_id=1, source_target_pairs={{0,4},{4,0},{8,12},{12,8},{16,20},{20,16},{24,28},{28,24},{1,5},{5... | collective-permute-start | bytes 3538952 | tf_op jit(solution)/shard_map/ppermute | solution.py:414
  1263.8 368.7 %reduce-scatter.5.cloned.1.call-start = ((), (), s32[]{:S(2)}) async-start(), calls=%async_computation.11 | async-start | bytes 15728640 | tf_op jit(solution)/shard_map/reduce_scatter | solution.py:1106
  1418.4 65.6 %collective-permute-start.81 = (bf16[144,2048]{1,0:T(8,128)(2,1)S(1)}, bf16[144,2048]{1,0:T(8,128)(2,1)S(1)}, u32[]{:S(2)}, u32[]{:S(2)}) collective-permute-start(bf16[144,2048]{1,0:T(8,128)(2,1)S(1)} %get-tuple-element.317), channel_id=1, source_target_pairs={{0,1},{1,0},{2,3},{3,2},{4,5},{5,4},{6,7},{7,6},{8,9},{9,8},{10,11... | collective-permute-start | bytes 1769480 | tf_op jit(solution)/shard_map/ppermute | solution.py:419
  1432.1 77.5 %collective-permute-start.83 = (bf16[144,2048]{1,0:T(8,128)(2,1)S(1)}, bf16[144,2048]{1,0:T(8,128)(2,1)S(1)}, u32[]{:S(2)}, u32[]{:S(2)}) collective-permute-start(bf16[144,2048]{1,0:T(8,128)(2,1)S(1)} %get-tuple-element.319), channel_id=1, source_target_pairs={{0,3},{1,2},{2,1},{3,0},{4,7},{5,6},{6,5},{7,4},{8,11},{9,10},{10,... | collective-permute-start | bytes 1769480 | tf_op jit(solution)/shard_map/ppermute | solution.py:419
  1436.4 128.1 %collective-permute-start.125 = (bf16[144,2048]{1,0:T(8,128)(2,1)}, bf16[144,2048]{1,0:T(8,128)(2,1)}, u32[]{:S(2)}, u32[]{:S(2)}) collective-permute-start(bf16[144,2048]{1,0:T(8,128)(2,1)} %get-tuple-element.305), channel_id=1, source_target_pairs={{0,1},{1,0},{2,3},{3,2},{4,5},{5,4},{6,7},{7,6},{8,9},{9,8},{10,11... | collective-permute-start | bytes 1769480 | tf_op jit(solution)/shard_map/ppermute | solution.py:419
  1437.4 177.8 %collective-permute-start.126 = (bf16[144,2048]{1,0:T(8,128)(2,1)}, bf16[144,2048]{1,0:T(8,128)(2,1)}, u32[]{:S(2)}, u32[]{:S(2)}) collective-permute-start(bf16[144,2048]{1,0:T(8,128)(2,1)} %get-tuple-element.306), channel_id=1, source_target_pairs={{0,2},{1,3},{2,0},{3,1},{4,6},{5,7},{6,4},{7,5},{8,10},{9,11},{10,... | collective-permute-start | bytes 1769480 | tf_op jit(solution)/shard_map/ppermute | solution.py:419
  1484.0 131.2 %collective-permute-start.127 = (bf16[144,2048]{1,0:T(8,128)(2,1)}, bf16[144,2048]{1,0:T(8,128)(2,1)}, u32[]{:S(2)}, u32[]{:S(2)}) collective-permute-start(bf16[144,2048]{1,0:T(8,128)(2,1)} %get-tuple-element.307), channel_id=1, source_target_pairs={{0,3},{1,2},{2,1},{3,0},{4,7},{5,6},{6,5},{7,4},{8,11},{9,10},{10,... | collective-permute-start | bytes 1769480 | tf_op jit(solution)/shard_map/ppermute | solution.py:419
  1526.7 132.1 %all-to-all-start.5 = ((bf16[4,64,2,512]{3,1,2,0:T(8,128)(2,1)}), bf16[4,64,2,512]{3,1,2,0:T(8,128)(2,1)S(1)}, u32[]{:S(2)}, u32[]{:S(2)}) async-start(bf16[4,64,2,512]{3,1,2,0:T(8,128)(2,1)} %bitcast.154), calls=%async_computation.6 | async-start | bytes 1048576 | tf_op jit(solution)/shard_map/all_to_all | solution.py:962
  1564.5 119.2 %collective-permute-start.84 = (bf16[2,144,2048]{2,1,0:T(8,128)(2,1)}, bf16[2,144,2048]{2,1,0:T(8,128)(2,1)}, u32[]{:S(2)}, u32[]{:S(2)}) collective-permute-start(bf16[2,144,2048]{2,1,0:T(8,128)(2,1)} %fusion.41), channel_id=1, source_target_pairs={{0,4},{4,0},{8,12},{12,8},{16,20},{20,16},{24,28},{28,24},{1,5},{5... | collective-permute-start | bytes 3538952 | tf_op jit(solution)/shard_map/ppermute | solution.py:414
  (300 other events, 7631.8 us)
Sparse Core Ops, SparseCore 0:
  48.6 104.7 all-gather.5
  156.0 273.4 all-gather.7
  1264.0 69.1 reduce-scatter.2
  1335.3 297.2 reduce-scatter.4

commit v2 on v0

--- a/solution.py
+++ b/solution.py
@@ -4,6 +4,8 @@
 import jax
 import jax.numpy as jnp
 from jax import lax
+from jax.experimental import pallas as pl
+from jax.experimental.pallas import tpu as pltpu
 from jax.sharding import PartitionSpec as P
 
 D = 2048
@@ -401,7 +403,1185 @@
     )
 
 
+CORE, SIDE_A, SIDE_B = 1, 2, 4
+CHIPS = 4
+CHUNKS = 4
+MB = 1024 * 1024
+
+
+def across(value, mask):
+    count = lax.axis_size("dp")
+    return lax.ppermute(value, "dp", [(place, place ^ mask) for place in range(count)])
+
+
+def along(value, mask):
+    count = lax.axis_size("fsdp")
+    return lax.ppermute(value, "fsdp", [(place, place ^ mask) for place in range(count)])
+
+
+def pick(values, index):
+    return lax.dynamic_index_in_dim(values, index, 0, keepdims=False)
+
+
+def after(value, *earlier):
+    return lax.optimization_barrier((value, earlier))[0]
+
+
+def trade_planes(parts, plane):
+    found = [pick(parts, plane)]
+    for mask in range(1, CHUNKS):
+        found.append(along(pick(parts, plane ^ mask), mask))
+    found = jnp.stack(found)
+    return [pick(found, label ^ plane) for label in range(CHUNKS)]
+
+
+def gather_planes(block):
+    one, two = along(block, 1), along(block, 2)
+    return [block, one, two, along(two, 1)]
+
+
+def sum_planes(parts):
+    two = (parts[2].astype(jnp.float32) + along(parts[3], 1).astype(jnp.float32)).astype(jnp.bfloat16)
+    return (
+        parts[0].astype(jnp.float32)
+        + along(parts[1], 1).astype(jnp.float32)
+        + along(two, 2).astype(jnp.float32)
+    )
+
+
+def sum_all(value):
+    for mask in (CORE, SIDE_A, SIDE_B):
+        value = value + across(value, mask)
+    for mask in (1, 2):
+        value = value + along(value, mask)
+    return value
+
+
+def to_planes(array, core, plane):
+    halves = array.reshape(2, 2, array.shape[1] // 2, array.shape[2]).swapaxes(0, 1)
+    keep = pick(halves, core)
+    came = across(pick(halves, 1 - core), CORE)
+    swap = core == 1
+    parts = jnp.concatenate([jnp.where(swap, came, keep), jnp.where(swap, keep, came)])
+    return trade_planes(parts, plane)
+
+
+def from_planes(chunks, core, plane):
+    groups = trade_planes(jnp.stack(chunks), plane)
+    pairs = jnp.stack([jnp.stack(groups[:2]), jnp.stack(groups[2:])])
+    keep = pick(pairs, core)
+    came = across(pick(pairs, 1 - core), CORE)
+    swap = core == 1
+    return jnp.concatenate([jnp.where(swap, came, keep), jnp.where(swap, keep, came)], axis=1)
+
+
+MESH = pl.DeviceIdType.MESH
+SLOT = {0: 0, SIDE_A: 1, SIDE_B: 2}
+ROUTES = ((SIDE_A, SIDE_B), (SIDE_B, SIDE_A))
+STRIPE = 16
+
+
+def peer(mask):
+    place = lax.axis_index("dp")
+    other = place + mask - 2 * mask * lax.rem(lax.div(place, mask), 2)
+    return (other, lax.axis_index("fsdp"))
+
+
+def meet():
+    barrier = pltpu.get_barrier_semaphore()
+    for mask in (CORE, SIDE_A, SIDE_B):
+        pl.semaphore_signal(barrier, inc=1, device_id=peer(mask), device_id_type=MESH)
+    pl.semaphore_wait(barrier, 3)
+
+
+class Remote:
+    def __init__(self, wires, source, target, mask):
+        self.wires, self.source, self.target, self.mask = wires, source, target, mask
+        self.place = wires.count
+        wires.count += 1
+
+    def make(self):
+        return pltpu.make_async_remote_copy(
+            src_ref=self.source,
+            dst_ref=self.target,
+            send_sem=self.wires.send.at[self.place],
+            recv_sem=self.wires.recv.at[self.place],
+            device_id=peer(self.mask),
+            device_id_type=MESH,
+        )
+
+    def start(self):
+        self.make().start()
+
+    def arrived(self):
+        self.make().wait_recv()
+
+    def left(self):
+        self.make().wait_send()
+
+
+class Wires:
+    def __init__(self, send, recv, local):
+        self.send, self.recv, self.local = send, recv, local
+        self.count = 0
+        self.local_count = 0
+
+    def load(self, pairs):
+        copies = [
+            pltpu.make_async_copy(source, target, self.local.at[place])
+            for place, (source, target) in enumerate(pairs)
+        ]
+        for copy in copies:
+            copy.start()
+        for copy in copies:
+            copy.wait()
+
+
+class Gather:
+    def __init__(self, wires, own, target):
+        rows = target.shape[2] // 2
+        self.wires, self.own = wires, own
+        self.near, self.far, self.core_first, self.core_near, self.core_far = [], [], [], [], []
+        self.home = []
+
+        def place(chunk, slot, half):
+            return target.at[chunk, slot, pl.ds(half * rows, rows)]
+
+        for chunk, (first, second) in enumerate(ROUTES):
+            near, far = SLOT[first], SLOT[second]
+            self.home.append((own[chunk], place(chunk, 0, 0)))
+            self.near.append(Remote(wires, own[chunk], place(chunk, near, 0), first))
+            self.core_first.append(Remote(wires, own[chunk], place(chunk, 0, 1), CORE))
+            self.far.append(Remote(wires, own[chunk], place(chunk, far, 0), second))
+            self.far.append(Remote(wires, place(chunk, near, 0), place(chunk, 3, 0), second))
+            self.core_near.append(Remote(wires, place(chunk, near, 0), place(chunk, near, 1), CORE))
+            self.core_far.append(Remote(wires, place(chunk, far, 0), place(chunk, far, 1), CORE))
+            self.core_far.append(Remote(wires, place(chunk, 3, 0), place(chunk, 3, 1), CORE))
+
+    def first(self):
+        for copy in self.near + self.core_first:
+            copy.start()
+        self.wires.load(self.home)
+
+    def second(self):
+        for chunk, copy in enumerate(self.near):
+            copy.arrived()
+            self.far[2 * chunk].start()
+            self.far[2 * chunk + 1].start()
+            self.core_near[chunk].start()
+
+    def third(self):
+        for place, copy in enumerate(self.far):
+            copy.arrived()
+            self.core_far[place].start()
+
+    def last(self):
+        for copy in self.core_first + self.core_near + self.core_far:
+            copy.arrived()
+        for copy in self.near + self.far + self.core_first + self.core_near + self.core_far:
+            copy.left()
+
+    def steps(self):
+        return [self.first, self.second, self.third, self.last]
+
+
+class Scatter:
+    def __init__(self, wires, own, other, landing, stage, done):
+        from_core, from_far, from_near = landing
+        self.wires, self.own, self.landing, self.stage, self.done = wires, own, landing, stage, done
+        self.core = [Remote(wires, other.at[chunk], from_core.at[chunk], CORE) for chunk in range(2)]
+        self.far = [
+            Remote(wires, stage[0].at[chunk], from_far.at[chunk], first)
+            for chunk, (_, first) in enumerate(ROUTES)
+        ]
+        self.near = [
+            Remote(wires, stage[2].at[chunk, 0], from_near.at[chunk], last)
+            for chunk, (last, _) in enumerate(ROUTES)
+        ]
+
+    def first(self):
+        for copy in self.core:
+            copy.start()
+
+    def second(self):
+        left, right = self.stage[:2]
+        pairs = []
+        for chunk, (_, first) in enumerate(ROUTES):
+            self.core[chunk].arrived()
+            for place, slot in enumerate((SLOT[first], 3)):
+                pairs.append((self.own.at[chunk, slot], left.at[chunk, place]))
+                pairs.append((self.landing[0].at[chunk, slot], right.at[chunk, place]))
+        self.wires.load(pairs)
+        for chunk in range(2):
+
+            @pl.loop(0, left.shape[2] // STRIPE)
+            def _(step):
+                span = pl.ds(step * STRIPE, STRIPE)
+                total = left[chunk, :, span].astype(jnp.float32) + right[chunk, :, span].astype(jnp.float32)
+                left[chunk, :, span] = total.astype(jnp.bfloat16)
+
+            self.far[chunk].start()
+
+    def third(self):
+        stage = self.stage[2]
+        pairs = []
+        for chunk, (last, _) in enumerate(ROUTES):
+            self.far[chunk].arrived()
+            pairs.append((self.own.at[chunk, SLOT[last]], stage.at[chunk, 0]))
+            pairs.append((self.landing[0].at[chunk, SLOT[last]], stage.at[chunk, 1]))
+            pairs.append((self.landing[1].at[chunk, 1], stage.at[chunk, 2]))
+        self.wires.load(pairs)
+        for chunk in range(2):
+
+            @pl.loop(0, stage.shape[2] // STRIPE)
+            def _(step):
+                span = pl.ds(step * STRIPE, STRIPE)
+                total = stage[chunk, 0, span].astype(jnp.float32)
+                for place in range(1, 3):
+                    total += stage[chunk, place, span].astype(jnp.float32)
+                stage[chunk, 0, span] = total.astype(jnp.bfloat16)
+
+            self.near[chunk].start()
+        for copy in self.far:
+            copy.left()
+
+    def last(self):
+        stage = self.stage[3]
+        for chunk in range(2):
+            self.near[chunk].arrived()
+            self.wires.load(
+                [
+                    (self.own.at[chunk, 0], stage.at[0]),
+                    (self.landing[0].at[chunk, 0], stage.at[1]),
+                    (self.landing[1].at[chunk, 0], stage.at[2]),
+                    (self.landing[2].at[chunk], stage.at[3]),
+                ]
+            )
+
+            @pl.loop(0, stage.shape[1] // STRIPE)
+            def _(step):
+                span = pl.ds(step * STRIPE, STRIPE)
+                total = stage[0, span].astype(jnp.float32)
+                for place in range(1, 4):
+                    total += stage[place, span].astype(jnp.float32)
+                self.done(chunk, span, total)
+
+        for copy in self.near + self.core:
+            copy.left()
+
+    def steps(self):
+        return [self.first, self.second, self.third, self.last]
+
+
+def stage_shapes(rows, width):
+    return [
+        pltpu.VMEM((2, 2, rows, width), jnp.bfloat16),
+        pltpu.VMEM((2, 2, rows, width), jnp.bfloat16),
+        pltpu.VMEM((2, 3, rows, width), jnp.bfloat16),
+        pltpu.VMEM((4, rows, width), jnp.bfloat16),
+    ]
+
+
+def landing_shapes(rows, width):
+    return [
+        jax.ShapeDtypeStruct((2, CHIPS, rows, width), jnp.bfloat16),
+        jax.ShapeDtypeStruct((2, 2, rows, width), jnp.bfloat16),
+        jax.ShapeDtypeStruct((2, rows, width), jnp.bfloat16),
+    ]
+
+
+def partial_shapes(rows, width):
+    return [jax.ShapeDtypeStruct((2, CHIPS, rows, width), jnp.bfloat16)] * 2
+
+
+def wire_shapes(count):
+    return [
+        pltpu.SemaphoreType.DMA((count,)),
+        pltpu.SemaphoreType.DMA((count,)),
+        pltpu.SemaphoreType.DMA((8,)),
+    ]
+
+
+def call(kernel, identity, inputs, outputs, scratch, megabytes):
+    return pl.pallas_call(
+        kernel,
+        in_specs=[pl.BlockSpec(memory_space=place) for _, place in inputs],
+        out_specs=[pl.BlockSpec(memory_space=place) for _, place in outputs],
+        out_shape=[shape for shape, _ in outputs],
+        scratch_shapes=scratch,
+        compiler_params=pltpu.CompilerParams(
+            collective_id=identity, has_side_effects=True, vmem_limit_bytes=megabytes * MB
+        ),
+    )(*[array for array, _ in inputs])
+
+
+HBM, VMEM, SMEM = pl.ANY, pltpu.VMEM, pltpu.SMEM
+
+
+def at_step(step, actions):
+    for when, action in actions.items():
+        pl.when(step == when)(action)
+
+
+def project_phase(gathered, states, weight_ref, cosine, sine, actions):
+    tokens = gathered.shape[2]
+
+    def body(rows_ref, cosine_ref, sine_ref, out):
+        at_step(pl.program_id(0) * CHIPS + pl.program_id(1), actions)
+        product = dot(rows_ref[0, 0], weight_ref[...])
+        angles = (cosine_ref[0], sine_ref[0])
+        query = spin(product[:, :HEAD], *angles) * (1.0 / math.sqrt(HEAD))
+        key = spin(product[:, HEAD : 2 * HEAD], *angles)
+        out[0, 0] = jnp.concatenate([query, key, product[:, 2 * HEAD :]], axis=1).astype(jnp.bfloat16)
+
+    here = lambda chunk, chip: (chunk, chip, 0, 0)
+    table = pl.BlockSpec((1, tokens, HEAD // 2), lambda chunk, chip: (chunk, 0, 0))
+    pltpu.emit_pipeline(
+        body,
+        grid=(2, CHIPS),
+        in_specs=[pl.BlockSpec((1, 1, tokens, gathered.shape[3]), here), table, table],
+        out_specs=[pl.BlockSpec((1, 1, tokens, 3 * HEAD), here)],
+    )(gathered, cosine, sine, states)
+
+
+def attend_phase(pair, states, mixed, own, other, lengths_ref, places, weight_ref, keys, values, actions):
+    tokens, rows, width = mixed.shape[2], own.shape[2], own.shape[3]
+    blocks = 2 * (pair + 1)
+
+    def body(*refs):
+        state_refs, (mixed_ref, own_ref, other_ref) = refs[: pair + 1], refs[pair + 1 :]
+        chip, side_at = pl.program_id(0), pl.program_id(1)
+        at_step(2 * chip + side_at, actions)
+
+        @pl.when(side_at == 0)
+        def _():
+            for block in range(blocks):
+                ref = state_refs[block // 2]
+                keys[pl.ds(block * tokens, tokens)] = ref[block % 2, 0, :, HEAD : 2 * HEAD]
+                values[pl.ds(block * tokens, tokens)] = ref[block % 2, 0, :, 2 * HEAD :]
+
+        for side in range(2):
+
+            @pl.when(side_at == side)
+            def _():
+                chunk = 2 * pair + side
+                count = tokens * (chunk + 1)
+                scores = dot_t(state_refs[pair][side, 0, :, :HEAD], keys[:count])
+                mask = seen(places[0][...], places[1][...], chunk, count, tokens, lengths_ref, chip)
+                scores = jnp.where(mask, scores, floor_score)
+                highest = jnp.max(scores, axis=1, keepdims=True)
+                exponent = jnp.exp(scores - highest)
+                total = jnp.sum(exponent, axis=1, keepdims=True)
+                probs = (exponent * (1.0 / total)).astype(jnp.bfloat16)
+                mixed_ref[0, 0] = dot(probs, values[:count]).astype(jnp.bfloat16)
+
+        partial = dot(mixed_ref[0, 0], weight_ref[...]).astype(jnp.bfloat16)
+        own_ref[0, 0] = partial[:rows]
+        other_ref[0, 0] = partial[rows:]
+
+    here = lambda chip, side: (side, chip, 0, 0)
+    state = pl.BlockSpec((2, 1, tokens, 3 * HEAD), lambda chip, side: (0, chip, 0, 0))
+    pltpu.emit_pipeline(
+        body,
+        grid=(CHIPS, 2),
+        in_specs=[state] * (pair + 1),
+        out_specs=[pl.BlockSpec((1, 1, tokens, HEAD), here)] + [pl.BlockSpec((1, 1, rows, width), here)] * 2,
+    )(*states[: pair + 1], mixed, own, other)
+
+
+def attend_back_phase(
+    pair, branch, states, head_grads, own, other, lengths_ref, places, out_weight, weight_ref,
+    tables, keys, values, sums, late_sums, actions
+):
+    tokens, rows, width = branch.shape[2], own.shape[2], own.shape[3]
+    blocks = 2 * (pair + 1)
+    edge = 2 * tokens
+
+    def body(*refs):
+        branch_ref, state_refs = refs[0], refs[1 : pair + 2]
+        cosine_ref, sine_ref, grads_ref, own_ref, other_ref = refs[pair + 2 :]
+        chip, step = pl.program_id(0), pl.program_id(1)
+        at_step(2 * chip + step, actions)
+
+        @pl.when(step == 0)
+        def _():
+            for block in range(blocks):
+                ref = state_refs[block // 2]
+                keys[pl.ds(block * tokens, tokens)] = ref[block % 2, 0, :, HEAD : 2 * HEAD]
+                values[pl.ds(block * tokens, tokens)] = ref[block % 2, 0, :, 2 * HEAD :]
+            if pair == 1:
+                for place in range(2):
+                    sums[place][chip] = jnp.zeros(sums[place].shape[1:], jnp.float32)
+                    late_sums[place][...] = jnp.zeros(late_sums[place].shape, jnp.float32)
+
+        def add(place, term):
+            early = min(term.shape[0], edge)
+            sums[place][chip, :early] += term[:early]
+            if term.shape[0] > edge:
+                late_sums[place][: term.shape[0] - edge] += term[edge:]
+
+        for side in range(2):
+
+            @pl.when(step == 1 - side)
+            def _():
+                chunk = 2 * pair + side
+                count = tokens * (chunk + 1)
+                mixed_grad = dot_t(branch_ref[0, 0], out_weight[...]).astype(jnp.bfloat16)
+                query = state_refs[pair][side, 0, :, :HEAD]
+                scores = dot_t(query, keys[:count])
+                mask = seen(places[0][...], places[1][...], chunk, count, tokens, lengths_ref, chip)
+                scores = jnp.where(mask, scores, floor_score)
+                highest = jnp.max(scores, axis=1, keepdims=True)
+                exponent = jnp.exp(scores - highest)
+                probs = exponent * (1.0 / jnp.sum(exponent, axis=1, keepdims=True))
+                add(1, dot_tn(probs.astype(jnp.bfloat16), mixed_grad))
+                prob_grad = dot_t(mixed_grad, values[:count])
+                inner = jnp.sum(probs * prob_grad, axis=1, keepdims=True)
+                score_grad = (probs * (prob_grad - inner)).astype(jnp.bfloat16)
+                add(0, dot_tn(score_grad, query))
+                query_grad = dot(score_grad, keys[:count]) * (1.0 / math.sqrt(HEAD))
+                angles = (cosine_ref[0], sine_ref[0])
+                span = slice(side * tokens, (side + 1) * tokens)
+                if pair == 1:
+                    key_grad, value_grad = late_sums[0][span], late_sums[1][span]
+                else:
+                    key_grad, value_grad = sums[0][chip, span], sums[1][chip, span]
+                grads_ref[0, 0] = jnp.concatenate(
+                    [spin_back(query_grad, *angles), spin_back(key_grad, *angles), value_grad], axis=1
+                ).astype(jnp.bfloat16)
+
+        partial = dot_t(grads_ref[0, 0], weight_ref[...]).astype(jnp.bfloat16)
+        own_ref[0, 0] = partial[:rows]
+        other_ref[0, 0] = partial[rows:]
+
+    here = lambda chip, step: (1 - step, chip, 0, 0)
+    state = pl.BlockSpec((2, 1, tokens, 3 * HEAD), lambda chip, step: (0, chip, 0, 0))
+    table = pl.BlockSpec((1, tokens, HEAD // 2), lambda chip, step: (1 - step, 0, 0))
+    pltpu.emit_pipeline(
+        body,
+        grid=(CHIPS, 2),
+        in_specs=[pl.BlockSpec((1, 1, tokens, width), here)] + [state] * (pair + 1) + [table] * 2,
+        out_specs=[pl.BlockSpec((1, 1, tokens, 3 * HEAD), here)]
+        + [pl.BlockSpec((1, 1, rows, width), here)] * 2,
+    )(branch, *states[: pair + 1], *tables, head_grads, own, other)
+
+
+def feed_phase(rows_in, grads_in, hidden, unit_grads, back_parts, out_parts, weights, actions):
+    tokens, width = rows_in.shape[2:]
+    rows = tokens // 2
+    shards, columns = weights.shape[0], weights.shape[2]
+    share = columns // 2
+
+    def body(rows_ref, out_grad_ref, hidden_ref, units_ref, back_own, back_other, out_own, out_other):
+        at_step(pl.program_id(0) * CHIPS + pl.program_id(1), actions)
+        hidden_grad = None
+        for shard in range(shards):
+            grad = out_grad_ref[0, 0, :, shard * columns : (shard + 1) * columns]
+            term = dot_t(grad, weights[shard, width:, :])
+            hidden_grad = term if hidden_grad is None else hidden_grad + term
+        back = None
+        for shard in range(shards):
+            both = dot(rows_ref[0, 0], weights[shard, :width, :])
+            gate, upward = both[:, :share], both[:, share:]
+            grad = hidden_grad[:, shard * share : (shard + 1) * share]
+            sigmoid = jax.nn.sigmoid(gate)
+            swish = gate * sigmoid
+            hidden_ref[0, 0, :, shard * share : (shard + 1) * share] = (swish * upward).astype(jnp.bfloat16)
+            gate_grad = grad * upward * sigmoid * (1.0 + gate * (1.0 - sigmoid))
+            units_ref[shard, 0, 0] = jnp.concatenate([gate_grad, grad * swish], axis=1).astype(jnp.bfloat16)
+            term = dot_t(units_ref[shard, 0, 0], weights[shard, :width, :])
+            back = term if back is None else back + term
+        back = back.astype(jnp.bfloat16)
+        back_own[0, 0] = back[:rows]
+        back_other[0, 0] = back[rows:]
+        for shard in range(shards):
+            span = slice(shard * columns, (shard + 1) * columns)
+            value = dot(hidden_ref[0, 0], weights[shard, width:, :]).astype(jnp.bfloat16)
+            out_own[0, 0, :, span] = value[:rows]
+            out_other[0, 0, :, span] = value[rows:]
+
+    here = lambda chunk, chip: (chunk, chip, 0, 0)
+    wide = pl.BlockSpec((1, 1, tokens, width), here)
+    narrow = pl.BlockSpec((1, 1, rows, width), here)
+    pltpu.emit_pipeline(
+        body,
+        grid=(2, CHIPS),
+        in_specs=[wide, wide],
+        out_specs=[
+            pl.BlockSpec((1, 1, tokens, hidden.shape[3]), here),
+            pl.BlockSpec((shards, 1, 1, tokens, columns), lambda chunk, chip: (0, chunk, chip, 0, 0)),
+        ]
+        + [narrow] * 4,
+    )(rows_in, grads_in, hidden, unit_grads, *back_parts, *out_parts)
+
+
+def bf16(*shape):
+    return jax.ShapeDtypeStruct(shape, jnp.bfloat16)
+
+
+def f32(*shape):
+    return jax.ShapeDtypeStruct(shape, jnp.float32)
+
+
+def gather_and_project(normed, out_grads, weight, cosine, sine):
+    _, rows, width = normed.shape
+    tokens = 2 * rows
+    whole_pair = bf16(2, CHIPS, tokens, width)
+
+    def kernel(normed_ref, grads_ref, weight_ref, cosine_ref, sine_ref, *refs):
+        gathered, grads, states, wires = refs[:2], refs[2:4], refs[4:6], Wires(*refs[6:])
+        meet()
+        rows_moves = [
+            Gather(wires, [normed_ref.at[2 * pair], normed_ref.at[2 * pair + 1]], gathered[pair])
+            for pair in range(2)
+        ]
+        grad_moves = [
+            Gather(wires, [grads_ref.at[2 * pair], grads_ref.at[2 * pair + 1]], grads[pair])
+            for pair in range(2)
+        ]
+        rows_moves[0].first()
+        rows_moves[0].second()
+        rows_moves[1].first()
+        rows_moves[0].third()
+        rows_moves[1].second()
+        grad_moves[0].first()
+        rows_moves[0].last()
+        project_phase(
+            gathered[0], states[0], weight_ref, cosine_ref.at[0], sine_ref.at[0],
+            {4: rows_moves[1].third, 6: grad_moves[0].second},
+        )
+        grad_moves[1].first()
+        rows_moves[1].last()
+        project_phase(
+            gathered[1], states[1], weight_ref, cosine_ref.at[1], sine_ref.at[1],
+            {4: grad_moves[0].third, 6: grad_moves[1].second},
+        )
+        grad_moves[0].last()
+        grad_moves[1].third()
+        grad_moves[1].last()
+
+    outs = call(
+        kernel,
+        1,
+        [(normed, HBM), (out_grads, HBM), (weight, VMEM), (cosine, HBM), (sine, HBM)],
+        [(whole_pair, HBM)] * 4 + [(bf16(2, CHIPS, tokens, 3 * HEAD), HBM)] * 2,
+        wire_shapes(60),
+        40,
+    )
+    return outs[:2], outs[2:4], outs[4:6]
+
+
+def attend_and_norm(states, lengths, places, out_weight, inputs, gain):
+    _, rows, width = inputs.shape
+    tokens = 2 * rows
+
+    def kernel(*refs):
+        states_in, (lengths_ref, place_q, place_k, weight_ref, inputs_ref, gain_ref) = refs[:2], refs[2:8]
+        mixed, middle, normed, target = refs[8:10], refs[10], refs[11], refs[12]
+        parts, landings = (refs[13:15], refs[15:17]), (refs[17:20], refs[20:23])
+        stage, keys, values, wires = refs[23:27], refs[27], refs[28], Wires(*refs[29:])
+        meet()
+
+        def finish(pair):
+            def done(chunk, span, total):
+                at = 2 * pair + chunk
+                total = total + inputs_ref[at, span].astype(jnp.float32)
+                middle[at, span] = total
+                factor = lax.rsqrt(jnp.mean(total * total, axis=1, keepdims=True) + epsilon)
+                normed[at, span] = (total * factor * gain_ref[...]).astype(jnp.bfloat16)
+
+            return done
+
+        sums = [
+            Scatter(wires, *parts[pair], landings[pair], stage, finish(pair)) for pair in range(2)
+        ]
+        move = Gather(wires, [normed.at[2], normed.at[3]], target)
+        places_in = (place_q, place_k)
+        attend_phase(
+            1, states_in, mixed[1], *parts[1], lengths_ref, places_in, weight_ref, keys, values, {}
+        )
+        sums[1].first()
+        attend_phase(
+            0, states_in, mixed[0], *parts[0], lengths_ref, places_in, weight_ref, keys, values,
+            {5: sums[1].second},
+        )
+        sums[0].first()
+        sums[1].third()
+        sums[0].second()
+        sums[1].last()
+        move.first()
+        sums[0].third()
+        move.second()
+        sums[0].last()
+        move.third()
+        move.last()
+
+    pair_parts = [(shape, HBM) for shape in partial_shapes(rows, width)]
+    landing = [(shape, HBM) for shape in landing_shapes(rows, width)]
+    outs = call(
+        kernel,
+        2,
+        [(state, HBM) for state in states]
+        + [(lengths, SMEM), (places[0], VMEM), (places[1], VMEM), (out_weight, VMEM)]
+        + [(inputs, VMEM), (gain, VMEM)],
+        [(bf16(2, CHIPS, tokens, HEAD), HBM)] * 2
+        + [(f32(CHUNKS, rows, width), VMEM), (bf16(CHUNKS, rows, width), VMEM)]
+        + [(bf16(2, CHIPS, tokens, width), HBM)]
+        + pair_parts * 2
+        + landing * 2,
+        stage_shapes(rows, width)
+        + [pltpu.VMEM((CHUNKS * tokens, HEAD), jnp.bfloat16)] * 2
+        + wire_shapes(30),
+        56,
+    )
+    return outs[:2], outs[2], outs[3], outs[4]
+
+
+def norm_back(values, gain, gradient):
+    factor = lax.rsqrt(jnp.mean(values * values, axis=1, keepdims=True) + epsilon)
+    scaled = values * factor
+    pulled = gradient * gain
+    back = factor * (pulled - scaled * jnp.mean(pulled * scaled, axis=1, keepdims=True))
+    return back, gradient * scaled
+
+
+def feed_forward(normed_own, normed_late, out_grads, weights, middle, out_grad_own, gain, units):
+    _, rows, width = middle.shape
+    tokens = 2 * rows
+    shards, columns = weights.shape[0], weights.shape[2]
+    whole_pair = bf16(2, CHIPS, tokens, width)
+
+    def kernel(*refs):
+        normed_ref, normed_late_ref, *grads = refs[:4]
+        weight_ref, middle_ref, own_grad, gain_ref = refs[4:8]
+        normed_early, branch = refs[8:10]
+        hidden, unit_grads = refs[10:12], refs[12:14]
+        back_parts, out_parts = (refs[14:16], refs[16:18]), (refs[18:20], refs[20:22])
+        middle_grad, gain_sum, landing = refs[22], refs[23], refs[24:27]
+        stage, own_branch, wires = refs[27:31], refs[31], Wires(*refs[32:])
+        meet()
+        gain_sum[...] = jnp.zeros(gain_sum.shape, jnp.float32)
+
+        def done(chunk, span, total):
+            back, gain_terms = norm_back(middle_ref[2 + chunk, span], gain_ref[...], total)
+            gain_sum[...] += gain_terms
+            back = back + own_grad[2 + chunk, span].astype(jnp.float32)
+            middle_grad[chunk, span] = back
+            own_branch[chunk, span] = back.astype(jnp.bfloat16)
+
+        move = Gather(wires, [normed_ref.at[0], normed_ref.at[1]], normed_early)
+        sums = Scatter(wires, *back_parts[1], landing, stage, done)
+        late_move = Gather(wires, [own_branch.at[0], own_branch.at[1]], branch)
+        move.first()
+        feed_phase(
+            normed_late_ref, grads[1], hidden[1], unit_grads[1], back_parts[1], out_parts[1], weight_ref,
+            {2: move.second, 5: move.third},
+        )
+        sums.first()
+        move.last()
+        feed_phase(
+            normed_early, grads[0], hidden[0], unit_grads[0], back_parts[0], out_parts[0], weight_ref,
+            {1: sums.second, 4: sums.third, 6: lambda: (sums.last(), late_move.first()) and None},
+        )
+        late_move.second()
+        late_move.third()
+        late_move.last()
+
+    outs = call(
+        kernel,
+        3,
+        [(normed_own, HBM), (normed_late, HBM)]
+        + [(grads, HBM) for grads in out_grads]
+        + [(weights, VMEM), (middle, VMEM), (out_grad_own, VMEM), (gain, VMEM)],
+        [(whole_pair, HBM)] * 2
+        + [(bf16(2, CHIPS, tokens, units), HBM)] * 2
+        + [(bf16(shards, 2, CHIPS, tokens, columns), HBM)] * 2
+        + [(shape, HBM) for shape in partial_shapes(rows, width)] * 4
+        + [(f32(2, rows, width), VMEM), (f32(STRIPE, width), VMEM)]
+        + [(shape, HBM) for shape in landing_shapes(rows, width)],
+        stage_shapes(rows, width) + [pltpu.VMEM((2, rows, width), jnp.bfloat16)] + wire_shapes(40),
+        62,
+    )
+    return outs[0], outs[1], outs[2:4], outs[4:6], outs[6:8], (outs[10:12], outs[12:14]), outs[14], outs[15]
+
+
+def attend_back(
+    states, lengths, places, out_weight, weight, cosine, sine, branch_late, back_early, out_parts,
+    middle, out_grad_own, inputs, middle_grad_late, gains
+):
+    _, rows, width = middle.shape
+    tokens = 2 * rows
+
+    def kernel(*refs):
+        states_in, (lengths_ref, place_q, place_k, out_ref, weight_ref, cosine_ref, sine_ref) = (
+            refs[:2],
+            refs[2:9],
+        )
+        late_branch, back_parts, outs_in = refs[9], refs[10:12], (refs[12:14], refs[14:16])
+        middle_ref, own_grad, inputs_ref, late_grad, gain_one, gain_two = refs[16:22]
+        head_grads, early_branch, outputs, input_grad = refs[22:24], refs[24], refs[25], refs[26]
+        gain_sums = refs[27]
+        parts = (refs[28:30], refs[30:32])
+        landings = [refs[32 + 3 * place : 35 + 3 * place] for place in range(5)]
+        stage, early_grad, own_branch, keys, values = refs[47:51], refs[51], refs[52], refs[53], refs[54]
+        sums, late_sums, wires = refs[55:57], refs[57:59], Wires(*refs[59:])
+        meet()
+        gain_sums[...] = jnp.zeros(gain_sums.shape, jnp.float32)
+
+        def middle_done(chunk, span, total):
+            back, gain_terms = norm_back(
+                middle_ref[chunk, span].astype(jnp.float32), gain_two[...], total
+            )
+            gain_sums[1] += gain_terms
+            back = back + own_grad[chunk, span].astype(jnp.float32)
+            early_grad[chunk, span] = back
+            own_branch[chunk, span] = back.astype(jnp.bfloat16)
+
+        def output_done(pair):
+            def done(chunk, span, total):
+                at = 2 * pair + chunk
+                outputs[at, span] = (middle_ref[at, span] + total).astype(jnp.bfloat16)
+
+            return done
+
+        def input_done(pair):
+            def done(chunk, span, total):
+                at = 2 * pair + chunk
+                back, gain_terms = norm_back(
+                    inputs_ref[at, span].astype(jnp.float32), gain_one[...], total
+                )
+                gain_sums[0] += gain_terms
+                direct = late_grad if pair == 1 else early_grad
+                input_grad[at, span] = (direct[chunk, span] + back).astype(jnp.bfloat16)
+
+            return done
+
+        middle_sum = Scatter(wires, *back_parts, landings[0], stage, middle_done)
+        move = Gather(wires, [own_branch.at[0], own_branch.at[1]], early_branch)
+        output_sums = [
+            Scatter(wires, *outs_in[pair], landings[1 + pair], stage, output_done(pair))
+            for pair in range(2)
+        ]
+        input_sums = [
+            Scatter(wires, *parts[pair], landings[3 + pair], stage, input_done(pair)) for pair in range(2)
+        ]
+
+        def back_through(pair, branch, actions):
+            attend_back_phase(
+                pair, branch, states_in, head_grads[pair], *parts[pair], lengths_ref,
+                (place_q, place_k), out_ref, weight_ref, (cosine_ref.at[pair], sine_ref.at[pair]),
+                keys, values, sums, late_sums, actions,
+            )
+
+        def both(*steps):
+            def run():
+                for step in steps:
+                    step()
+
+            return run
+
+        middle_sum.first()
+        output_sums[1].first()
+        back_through(
+            1,
+            late_branch,
+            {1: middle_sum.second, 5: middle_sum.third, 7: both(middle_sum.last, move.first)},
+        )
+        move.second()
+        input_sums[1].first()
+        output_sums[1].second()
+        move.third()
+        move.last()
+        output_sums[0].first()
+        back_through(
+            0,
+            early_branch,
+            {
+                1: both(output_sums[1].third, input_sums[1].second),
+                4: both(output_sums[1].last, input_sums[1].third),
+                6: both(input_sums[1].last, output_sums[0].second),
+            },
+        )
+        input_sums[0].first()
+        output_sums[0].third()
+        input_sums[0].second()
+        output_sums[0].last()
+        input_sums[0].third()
+        input_sums[0].last()
+
+    outs = call(
+        kernel,
+        4,
+        [(state, HBM) for state in states]
+        + [(lengths, SMEM), (places[0], VMEM), (places[1], VMEM), (out_weight, VMEM), (weight, VMEM)]
+        + [(cosine, HBM), (sine, HBM), (branch_late, HBM)]
+        + [(part, HBM) for part in back_early]
+        + [(part, HBM) for parts in out_parts for part in parts]
+        + [(middle, VMEM), (out_grad_own, VMEM), (inputs, VMEM), (middle_grad_late, VMEM)]
+        + [(gains[0], VMEM), (gains[1], VMEM)],
+        [(bf16(2, CHIPS, tokens, 3 * HEAD), HBM)] * 2
+        + [(bf16(2, CHIPS, tokens, width), HBM)]
+        + [(bf16(CHUNKS, rows, width), VMEM)] * 2
+        + [(f32(2, STRIPE, width), VMEM)]
+        + [(shape, HBM) for shape in partial_shapes(rows, width)] * 2
+        + [(shape, HBM) for shape in landing_shapes(rows, width)] * 5,
+        stage_shapes(rows, width)
+        + [pltpu.VMEM((2, rows, width), jnp.float32), pltpu.VMEM((2, rows, width), jnp.bfloat16)]
+        + [pltpu.VMEM((CHUNKS * tokens, HEAD), jnp.bfloat16)] * 2
+        + [pltpu.VMEM((CHIPS, 2 * tokens, HEAD), jnp.float32)] * 2
+        + [pltpu.VMEM((2 * tokens, HEAD), jnp.float32)] * 2
+        + wire_shapes(50),
+        63,
+    )
+    return outs[:2], outs[2], outs[3], outs[4], outs[5]
+
+
+def unit_weight_grads(unit_grads, rows_in):
+    shards, _, _, tokens, columns = unit_grads[0].shape
+    width = rows_in[0].shape[3]
+
+    def kernel(late_units, late_rows, early_units, early_rows, out, total):
+        step = pl.program_id(1)
+
+        @pl.when(step == 0)
+        def _():
+            total[...] = jnp.zeros(total.shape, jnp.float32)
+
+        for place, (units, rows_ref) in enumerate(((late_units, late_rows), (early_units, early_rows))):
+
+            @pl.when(lax.div(step, 2) == place)
+            def _():
+                left = units[0, 0].reshape(CHIPS * tokens, columns)
+                right = rows_ref[0].reshape(CHIPS * tokens, width)
+                total[...] += dot_tn(left, right)
+
+        @pl.when(step == 3)
+        def _():
+            out[0] = total[...].astype(jnp.bfloat16)
+
+    late = lambda step: jnp.minimum(step, 1)
+    early = lambda step: jnp.maximum(step - 2, 0)
+    specs = []
+    for at in (late, early):
+        specs.append(
+            pl.BlockSpec(
+                (1, 1, CHIPS, tokens, columns),
+                (lambda at: lambda shard, step: (shard, at(step), 0, 0, 0))(at),
+            )
+        )
+        specs.append(
+            pl.BlockSpec(
+                (1, CHIPS, tokens, width), (lambda at: lambda shard, step: (at(step), 0, 0, 0))(at)
+            )
+        )
+    return pl.pallas_call(
+        kernel,
+        grid=(shards, 4),
+        in_specs=specs,
+        out_specs=pl.BlockSpec((1, columns, width), lambda shard, step: (shard, 0, 0)),
+        out_shape=bf16(shards, columns, width),
+        scratch_shapes=[pltpu.VMEM((columns, width), jnp.float32)],
+        compiler_params=params(60),
+    )(unit_grads[1], rows_in[1], unit_grads[0], rows_in[0])
+
+
+def dot(left, right):
+    return jnp.dot(left, right, preferred_element_type=jnp.float32)
+
+
+def dot_t(left, right):
+    return lax.dot_general(
+        left, right, (((1,), (1,)), ((), ())), preferred_element_type=jnp.float32
+    )
+
+
+def dot_tn(left, right):
+    return lax.dot_general(
+        left, right, (((0,), (0,)), ((), ())), preferred_element_type=jnp.float32
+    )
+
+
+def spin(values, cosine, sine):
+    halfway = values.shape[1] // 2
+    first, second = values[:, :halfway], values[:, halfway:]
+    return jnp.concatenate(
+        [first * cosine - second * sine, second * cosine + first * sine], axis=1
+    )
+
+
+def spin_back(values, cosine, sine):
+    return spin(values, cosine, -sine)
+
+
+def whole(shape):
+    return pl.BlockSpec(shape, lambda *_: (0,) * len(shape), pipeline_mode=pl.Buffered(1))
+
+
+def params(megabytes):
+    return pltpu.CompilerParams(vmem_limit_bytes=megabytes * MB)
+
+
+def seen(place_q, place_k, chunk, count, tokens, lengths_ref, chip):
+    query_index = tokens * chunk + place_q
+    key_index = place_k[:, :count]
+    ahead_or_here = key_index <= query_index
+    if tokens * (chunk + 1) <= PROMPT:
+        return ahead_or_here
+
+    def segment(index):
+        found = jnp.full(index.shape, -1, jnp.int32)
+        for slot in range(NCONT):
+            found = jnp.where(index >= PROMPT + slot * CONT, slot, found)
+        return found
+
+    key_segment, query_segment = segment(key_index), segment(query_index)
+    end = jnp.full(key_index.shape, PROMPT, jnp.int32)
+    for slot in range(NCONT):
+        end = jnp.where(
+            key_segment == slot, PROMPT + slot * CONT + lengths_ref[chip, slot], end
+        )
+    alive = key_index < end
+    return ahead_or_here & ((key_segment < 0) | ((key_segment == query_segment) & alive))
+
+
+def token_dot(left, right):
+    return lax.dot_general(
+        left.reshape(-1, left.shape[-1]),
+        right.reshape(-1, right.shape[-1]),
+        (((0,), (0,)), ((), ())),
+        preferred_element_type=jnp.float32,
+    )
+
+
+def exchange(value, axis):
+    return lax.all_to_all(value, axis, split_axis=0, concat_axis=0, tiled=True)
+
+
+def plane_device(
+    activations,
+    cotangent,
+    continuation_lengths,
+    query_weight,
+    key_weight,
+    value_weight,
+    output_weight,
+    gate_weight,
+    up_weight,
+    down_weight,
+    attention_gain,
+    feedforward_gain,
+    moment_query,
+    moment_key,
+    moment_value,
+    moment_output,
+    moment_gate,
+    moment_up,
+    moment_down,
+    moment_attention,
+    moment_feedforward,
+):
+    devices, planes = lax.axis_size("dp"), lax.axis_size("fsdp")
+    place, plane = lax.axis_index("dp"), lax.axis_index("fsdp")
+    core = place % 2
+    low = jnp.bfloat16
+    kv_width = KV_HEADS * HEAD
+    tokens = activations.shape[1]
+    half = tokens // 2
+
+    inputs = to_planes(activations, core, plane)
+
+    in_rows = query_weight.shape[0]
+    sub_rows = in_rows // planes
+    spread = devices * sub_rows
+    mixed_kv = jnp.stack([key_weight.astype(low), value_weight.astype(low)], axis=1)
+    block = jnp.concatenate([query_weight.astype(low).reshape(in_rows, 2, HEAD), mixed_kv], axis=2)
+    block = jnp.stack(trade_planes(block.reshape(planes, sub_rows, 2, 2 * HEAD), plane))
+    block = block.transpose(0, 2, 1, 3).reshape(devices, sub_rows, 2 * HEAD)
+    block = exchange(block, "dp")
+    attention_block = jnp.concatenate(
+        [block.reshape(spread, 2 * HEAD), output_weight.astype(low)], axis=0
+    )
+    found = jnp.stack(gather_planes(after(attention_block, inputs)))
+    attention_all = jnp.stack([pick(found, label ^ plane) for label in range(CHUNKS)])
+    packed = (
+        attention_all[:, :spread]
+        .reshape(planes, devices, sub_rows, 2 * HEAD)
+        .transpose(1, 0, 2, 3)
+        .reshape(D, 2 * HEAD)
+    )
+    other_half = across(packed[:, HEAD:], CORE)
+    key_part = jnp.where(core == 0, packed[:, HEAD:], other_half)
+    value_part = jnp.where(core == 0, other_half, packed[:, HEAD:])
+    head_weight = jnp.concatenate([packed[:, :HEAD], key_part, value_part], axis=1)
+    head_output = attention_all[:, spread:].transpose(1, 0, 2).reshape(HEAD, D)
+
+    strip = 128
+    runs = gate_weight.shape[1] // (devices * strip)
+    units = runs * strip * planes
+    gate_up = jnp.stack(
+        [
+            gate_weight.astype(low).reshape(in_rows, runs, devices, strip),
+            up_weight.astype(low).reshape(in_rows, runs, devices, strip),
+        ]
+    )
+    gate_up = gate_up.transpose(3, 1, 0, 2, 4).reshape(devices, in_rows, 2 * runs * strip)
+    gate_up = exchange(gate_up, "dp").reshape(devices * in_rows, 2 * runs * strip)
+    down_columns = down_weight.shape[1]
+    down = exchange(down_weight.astype(low).reshape(devices, strip, down_columns), "dp")
+    feed_block = jnp.concatenate([gate_up, down.reshape(devices * strip, down_columns)], axis=0)
+
+    out_grads = to_planes(after(cotangent, attention_all), core, plane)
+    feed_weights = lax.all_gather(after(feed_block, out_grads), "fsdp", axis=0, tiled=False)
+
+    others = across(continuation_lengths, CORE)
+    swap = core == 1
+    here = jnp.concatenate(
+        [
+            jnp.where(swap, others, continuation_lengths),
+            jnp.where(swap, continuation_lengths, others),
+        ]
+    )
+    here = pick(here, plane)
+    near = jnp.stack([here, across(here, SIDE_A)])
+    lengths = jnp.concatenate([near, across(near, SIDE_B)])
+
+    inside = jnp.concatenate(
+        [core * half + jnp.arange(half), (1 - core) * half + jnp.arange(half)]
+    ).astype(jnp.int32)
+    order = (tokens * jnp.arange(CHUNKS, dtype=jnp.int32)[:, None] + inside[None, :]).reshape(-1)
+    cosine, sine = rope_angles(token_places(order))
+    cosine = cosine.reshape(2, 2, tokens, HEAD // 2)
+    sine = sine.reshape(2, 2, tokens, HEAD // 2)
+    place_q, place_k = inside[:, None], order[None, :]
+    blocks = plane ^ jnp.arange(CHUNKS, dtype=jnp.int32)
+
+    own_inputs, own_grads = jnp.stack(inputs), jnp.stack(out_grads)
+    normed, _ = rms_rows(own_inputs.astype(jnp.float32), attention_gain)
+    gain_one, gain_two = attention_gain[None, :], feedforward_gain[None, :]
+    rows_all, grads_all, states = gather_and_project(
+        normed.astype(low), own_grads, head_weight, cosine, sine
+    )
+    mixed, middle, normed_two, normed_late = attend_and_norm(
+        states, lengths, (place_q, place_k), head_output, own_inputs, gain_two
+    )
+    normed_early, branch_late, hidden, unit_grads, back_early, out_parts, middle_grad, gain_sum = feed_forward(
+        normed_two, normed_late, grads_all, feed_weights, middle, own_grads, gain_two, units
+    )
+    unit_sum = unit_weight_grads(unit_grads, (normed_early, normed_late))
+    unit_sum = lax.psum_scatter(unit_sum, "fsdp", scatter_dimension=0, tiled=False)
+    down_sum = reduce(jnp.add, [token_dot(hidden[pair], grads_all[pair]) for pair in (1, 0)]).astype(low)
+    down_sum = down_sum.reshape(-1, planes, down_columns).transpose(1, 0, 2)
+    down_sum = lax.psum_scatter(down_sum, "fsdp", scatter_dimension=0, tiled=False)
+    head_grads, branch_early, own_outputs, own_input_grad, gain_sums = attend_back(
+        states,
+        lengths,
+        (place_q, place_k),
+        head_output,
+        head_weight,
+        cosine,
+        sine,
+        branch_late,
+        back_early,
+        out_parts,
+        middle,
+        own_grads,
+        own_inputs,
+        middle_grad,
+        (gain_one, gain_two),
+    )
+    outputs = from_planes([own_outputs[chunk] for chunk in range(CHUNKS)], core, plane)
+    input_grad = from_planes([own_input_grad[chunk] for chunk in range(CHUNKS)], core, plane)
+    attention_sum = jnp.sum(gain_sums[0], axis=0)
+    feedforward_sum = jnp.sum(gain_sums[1] + gain_sum, axis=0)
+
+    strips = runs * strip
+    unit_sum = unit_sum.reshape(2 * strips, devices, in_rows).swapaxes(0, 1)
+    unit_sum = exchange(unit_sum, "dp").reshape(devices, 2, runs, strip, in_rows)
+    gate_up_owned = unit_sum.transpose(1, 4, 2, 0, 3).reshape(2, in_rows, runs * devices * strip)
+    down_owned = exchange(down_sum.reshape(devices, strip, down_columns), "dp")
+    down_owned = down_owned.reshape(devices * strip, down_columns)
+    head_sum = reduce(
+        jnp.add, [token_dot(rows_all[pair], head_grads[pair]) for pair in (1, 0)]
+    ).astype(low)
+    branches = (branch_early, branch_late)
+    output_sum = reduce(jnp.add, [token_dot(mixed[pair], branches[pair]) for pair in (1, 0)]).astype(low)
+    given = jnp.where(core == 0, head_sum[:, 2 * HEAD :], head_sum[:, HEAD : 2 * HEAD])
+    kept = jnp.where(core == 0, head_sum[:, HEAD : 2 * HEAD], head_sum[:, 2 * HEAD :])
+    kv_sum = (kept.astype(jnp.float32) + across(given, CORE).astype(jnp.float32)).astype(low)
+    head_sum = jnp.concatenate([head_sum[:, :HEAD], kv_sum], axis=1)
+    head_sum = head_sum.reshape(devices, planes, sub_rows, 2 * HEAD).transpose(1, 0, 2, 3)
+    head_sum = head_sum.reshape(planes, spread, 2 * HEAD)
+    output_sum = output_sum.reshape(HEAD, planes, 2 * HEAD).transpose(1, 0, 2)
+    attention_parts = jnp.concatenate([head_sum, output_sum], axis=1)
+    attention_grad = sum_planes([pick(attention_parts, blocks[shard]) for shard in range(CHUNKS)])
+    output_owned = attention_grad[spread:]
+    block = exchange(attention_grad[:spread].astype(low).reshape(devices, sub_rows, 2 * HEAD), "dp")
+    block = block.reshape(planes, 2, sub_rows, 2 * HEAD).transpose(0, 2, 1, 3)
+    block = jnp.stack(trade_planes(block, plane)).reshape(in_rows, 2, 2 * HEAD)
+    query_owned = block[:, :, :HEAD].reshape(in_rows, 2 * HEAD)
+    key_owned, value_owned = block[:, 0, HEAD:], block[:, 1, HEAD:]
+    owner_grads = [
+        owned.astype(jnp.float32)
+        for owned in (
+            query_owned,
+            key_owned,
+            value_owned,
+            output_owned,
+            gate_up_owned[0],
+            gate_up_owned[1],
+            down_owned,
+        )
+    ]
+    local_square = reduce(jnp.add, [jnp.sum(owned * owned) for owned in owner_grads])
+    attention_total, feedforward_total = sum_all(jnp.stack([attention_sum, feedforward_sum]))
+    square_total = sum_all(jnp.full((8, 128), local_square))[0, 0]
+    square_sum = (
+        square_total
+        + jnp.sum(attention_total * attention_total)
+        + jnp.sum(feedforward_total * feedforward_total)
+    )
+    grad_norm = jnp.sqrt(square_sum)
+    entry_count = 2 * D * D + 2 * D * kv_width + 3 * D * FF + 2 * D
+    limit = clip_level * math.sqrt(entry_count)
+    factor = limit / jnp.maximum(grad_norm, limit)
+    gradients = owner_grads + [attention_total, feedforward_total]
+    old_moments = [
+        moment_query,
+        moment_key,
+        moment_value,
+        moment_output,
+        moment_gate,
+        moment_up,
+        moment_down,
+        moment_attention,
+        moment_feedforward,
+    ]
+    old_params = [
+        query_weight,
+        key_weight,
+        value_weight,
+        output_weight,
+        gate_weight,
+        up_weight,
+        down_weight,
+        attention_gain,
+        feedforward_gain,
+    ]
+    new_moments = [
+        0.5 * moment + 0.5 * factor * gradient for moment, gradient in zip(old_moments, gradients)
+    ]
+    new_params = []
+    for at, param in enumerate(old_params):
+        if at < 7:
+            new_params.append(param - step_size * (new_moments[at] + decay_rate * param))
+        else:
+            new_params.append(param - gain_step * new_moments[at])
+    return (outputs, input_grad, grad_norm, *new_moments, *new_params)
+
+
 def solution(mesh):
+    whole_groups_on_planes = mesh.shape["dp"] == HEADS and mesh.shape["fsdp"] == KV_HEADS
+    body = plane_device if whole_groups_on_planes else on_device
     placed = (
         P("dp", "fsdp", None),
         P("dp", "fsdp", None),
@@ -426,7 +1606,7 @@
         P(),
     )
     return jax.shard_map(
-        on_device,
+        body,
         mesh=mesh,
         in_specs=placed,
         out_specs=(

time: 5370 us -> 1670 us (0.31)
  waiting for transfers between devices: 3780 us -> 429 us
  Pallas kernels: 0 us -> 904 us
  blocking collectives: 526 us -> 0 us
  matrix products: 503 us -> 58.3 us
  local copies, waits for them, and re-layouts: 323 us -> 52.6 us
  other arithmetic: 161 us -> 74.1 us
  starting transfers between devices: 35.6 us -> 111 us
    all_gather x23 -> x1, waiting for transfers between devices: 2800 us -> 0.02 us  [plane_device(): lax.all_gather(after(feed_block, out_grads), 'fsdp', axis=0, tiled=False)]
    pallas_call x0 -> x5, Pallas kernels: none -> 904 us  [the longest x4 843 us: call(): pl.pallas_call(kernel, in_specs=[pl.BlockSpec(memory_space=place) for _,...]
    all_to_all x2 -> x0, blocking collectives: 486 us -> none  [weight_term(): lax.all_to_all(gradient, 'fsdp', split_axis=1, concat_axis=0, tiled=True)]
    all_to_all x6, waiting for transfers between devices: 511 us -> 48.1 us  [exchange(): return lax.all_to_all(value, axis, split_axis=0, concat_axis=0, tiled=True)]
    dot_general x36 -> x6, matrix products: 503 us -> 58.3 us  [token_dot(): lax.dot_general(left.reshape(-1, left.shape[-1]), right.reshape(-1, right...]
    ppermute x0 -> x43, waiting for transfers between devices: none -> 381 us  [the longest x28 371 us: along(): lax.ppermute(value, 'fsdp', [(place, place ^ mask) for place in range(cou...]
    reduce_scatter x9 -> x2, waiting for transfers between devices: 294 us -> 0.01 us  [the longest x1 0.01 us: plane_device(): lax.psum_scatter(down_sum, 'fsdp', scatter_dimension=0, tiled=False)]
    unnamed x34 -> x3, waiting for transfers between devices: 175 us -> 0.05 us
  transfers between devices with their start and end apart: 39 -> 52, of which waited for: 29 -> 29; matrix products, arithmetic and copies ran while one was open for 12% -> 6% of each run, Pallas kernels for 0% -> 40%
where the time goes in v2:
time: 1670 us; the launch traced here: 1660 us
  Pallas kernels  904 us (54%)
  waiting for transfers between devices  429 us (26%)
  starting transfers between devices  111 us (7%)
  other arithmetic  74.1 us (4%)
  matrix products  58.3 us (3%)
  local copies, waits for them, and re-layouts  52.6 us (3%)
  between operations  31 us (2%)
    pallas_call x4, Pallas kernels, call(): pl.pallas_call(kernel, in_specs=[pl.BlockSpec(memory_space=place) for _,...  843 us
    ppermute x28, waiting for transfers between devices, along(): lax.ppermute(value, 'fsdp', [(place, place ^ mask) for place in range(cou...  371 us
    ppermute x28, starting transfers between devices, along(): lax.ppermute(value, 'fsdp', [(place, place ^ mask) for place in range(cou...  81 us
    pallas_call x1, Pallas kernels, unit_weight_grads(): pl.pallas_call(kernel, grid=(shards, 4), in_specs=specs, out_specs=pl.Blo...  60.7 us
    dot_general x6, matrix products, token_dot(): lax.dot_general(left.reshape(-1, left.shape[-1]), right.reshape(-1, right...  58.3 us
    all_to_all x6, waiting for transfers between devices, exchange(): return lax.all_to_all(value, axis, split_axis=0, concat_axis=0, tiled=True)  48.1 us
  transfers between devices with their start and end apart: 52, of which 29 were waited for; matrix products, arithmetic and copies ran while one was open for 6% of the time, Pallas kernels for 40%

profile of v2, /device:TPU:0, one launch (start us, length us, event | category | flops | bytes accessed | tf_op | source)
XLA Modules:
  0.0 1659.8 jit_solution(9814891493496698293)
XLA Ops:
  20.1 25.6 %all-to-all-done.1 = bf16[8,256,512]{1,2,0:T(8,128)(2,1)} async-done(((bf16[8,256,512]{1,2,0:T(8,128)(2,1)}), bf16[8,256,512]{1,2,0:T(8,128)(2,1)}, u32[]{:S(2)}, u32[]{:S(2)}) %all-to-all-start.1) | async-done | bytes 2097184 | tf_op jit(solution)/shard_map/all_to_all | solution.py:1357
  52.2 12.4 all-to-all-done.2
  80.2 19.9 %collective-permute-done.5 = bf16[64,2,512]{2,1,0:T(2,128)(2,1)S(1)} collective-permute-done((bf16[64,2,512]{2,1,0:T(2,128)(2,1)S(1)}, bf16[64,2,512]{2,1,0:T(2,128)(2,1)S(1)}, u32[]{:S(2)}, u32[]{:S(2)}) %collective-permute-start.5) | collective-permute-done | bytes 131104 | tf_op jit(solution)/shard_map/ppermute | solution.py:419
  133.1 78.6 %collective-permute-done.8 = bf16[768,512]{1,0:T(8,128)(2,1)S(1)} collective-permute-done((bf16[768,512]{1,0:T(8,128)(2,1)S(1)}, bf16[768,512]{1,0:T(8,128)(2,1)S(1)}, u32[]{:S(2)}, u32[]{:S(2)}) %collective-permute-start.8) | collective-permute-done | bytes 786464 | tf_op jit(solution)/shard_map/ppermute | solution.py:419
  213.8 39.5 %collective-permute-done.2 = bf16[144,2048]{1,0:T(8,128)(2,1)} collective-permute-done((bf16[144,2048]{1,0:T(8,128)(2,1)}, bf16[144,2048]{1,0:T(8,128)(2,1)}, u32[]{:S(2)}, u32[]{:S(2)}) %collective-permute-start.2) | collective-permute-done | bytes 589856 | tf_op jit(solution)/shard_map/ppermute | solution.py:419
  260.8 52.0 %collective-permute-done.9 = bf16[768,512]{1,0:T(8,128)(2,1)} collective-permute-done((bf16[768,512]{1,0:T(8,128)(2,1)S(1)}, bf16[768,512]{1,0:T(8,128)(2,1)}, u32[]{:S(2)}, u32[]{:S(2)}) %collective-permute-start.9) | collective-permute-done | bytes 786464 | tf_op jit(solution)/shard_map/ppermute | solution.py:419
  327.0 44.7 %collective-permute-done.11 = bf16[144,2048]{1,0:T(8,128)(2,1)S(1)} collective-permute-done((bf16[144,2048]{1,0:T(8,128)(2,1)S(1)}, bf16[144,2048]{1,0:T(8,128)(2,1)S(1)}, u32[]{:S(2)}, u32[]{:S(2)}) %collective-permute-start.11) | collective-permute-done | bytes 589856 | tf_op jit(solution)/shard_map/ppermute | solution.py:419
  371.7 12.7 collective-permute-done.12
  384.4 17.2 %collective-permute-done.13 = bf16[144,2048]{1,0:T(8,128)(2,1)S(1)} collective-permute-done((bf16[144,2048]{1,0:T(8,128)(2,1)S(1)}, bf16[144,2048]{1,0:T(8,128)(2,1)S(1)}, u32[]{:S(2)}, u32[]{:S(2)}) %collective-permute-start.13) | collective-permute-done | bytes 589856 | tf_op jit(solution)/shard_map/ppermute | solution.py:419
  402.5 160.7 %shard_map.364 = (bf16[2,4,288,2048]{3,2,1,0:T(8,128)(2,1)}, bf16[2,4,288,2048]{3,2,1,0:T(8,128)(2,1)}, bf16[2,4,288,2048]{3,2,1,0:T(8,128)(2,1)}, bf16[2,4,288,...) custom-call(bf16[4,144,2048]{2,1,0:T(8,128)(2,1)S(1)} %fusion.4.normed_ref, ...), custom_call_target="tpu_custom_call" | custom-call | tf_op jit(solution)/shard_map/pallas_call | solution.py:706
  564.9 158.6 %shard_map.365 = (bf16[2,4,288,256]{3,2,1,0:T(8,128)(2,1)}, bf16[2,4,288,256]{3,2,1,0:T(8,128)(2,1)}, f32[4,144,2048]{2,1,0:T(8,128)}, bf16[4,144,2048]{2,1,0:T(...) custom-call(bf16[2,4,288,768]{3,2,1,0:T(8,128)(2,1)} %copy-done.2, ...), custom_call_target="tpu_custom_call" | custom-call | tf_op jit(solution)/shard_map/pallas_call | solution.py:706
  723.5 238.2 %shard_map.366 = (bf16[2,4,288,2048]{3,2,1,0:T(8,128)(2,1)}, bf16[2,4,288,2048]{3,2,1,0:T(8,128)(2,1)}, bf16[2,4,288,1024]{3,2,1,0:T(8,128)(2,1)}, bf16[2,4,288,...) custom-call(bf16[4,144,2048]{2,1,0:T(8,128)(2,1)} %get-tuple-element, ...), custom_call_target="tpu_custom_call" | custom-call | tf_op jit(solution)/shard_map/pallas_call | solution.py:706
  961.7 14.6 fusion.60
  976.4 13.6 fusion
  992.4 60.7 %shard_map.368 = bf16[4,512,2048]{2,1,0:T(8,128)(2,1)} custom-call(bf16[4,2,4,288,512]{4,3,2,1,0:T(8,128)(2,1)} %get-tuple-element.78.late_units, bf16[2,4,288,2048]{3,2,1,0:T(8,128)(2,1)} %get-tuple-element.57.refs_1_.late_rows, bf16[4,2,4,288,512]{4,3,2,1,0:T(8,128)(2,1)} %get-tuple-element.79.early_units, ...), custom_call_target="tpu_custom_call" | custom-call | tf_op jit(solution)/shard_map/pallas_call | solution.py:1277
  1057.6 285.6 %shard_map.367 = (bf16[2,4,288,768]{3,2,1,0:T(8,128)(2,1)}, bf16[2,4,288,768]{3,2,1,0:T(8,128)(2,1)}, bf16[2,4,288,2048]{3,2,1,0:T(8,128)(2,1)}, bf16[4,144,2048...) custom-call(bf16[2,4,288,768]{3,2,1,0:T(8,128)(2,1)} %copy-done.2, ...), custom_call_target="tpu_custom_call" | custom-call | tf_op jit(solution)/shard_map/pallas_call | solution.py:706
  1343.2 13.1 fusion.59
  1356.4 11.7 fusion.1
  1376.9 23.4 %collective-permute-start.28 = (bf16[768,512]{1,0:T(8,128)(2,1)}, bf16[768,512]{1,0:T(8,128)(2,1)}, u32[]{:S(2)}, u32[]{:S(2)}) collective-permute-start(bf16[768,512]{1,0:T(8,128)(2,1)} %get-tuple-element.120), channel_id=1, source_target_pairs={{0,1},{1,0},{2,3},{3,2},{4,5},{5,4},{6,7},{7,6},{8,9},{9,8},{10,11... | collective-permute-start | bytes 2359304 | tf_op jit(solution)/shard_map/ppermute | solution.py:419
  1403.6 15.4 collective-permute-done.28
  1428.1 23.0 %collective-permute-done.41 = f32[2,2048]{1,0:T(2,128)S(1)} collective-permute-done((f32[2,2048]{1,0:T(2,128)S(1)}, f32[2,2048]{1,0:T(2,128)S(1)}, u32[]{:S(2)}, u32[]{:S(2)}) %collective-permute-start.41) | collective-permute-done | bytes 16416 | tf_op jit(solution)/shard_map/ppermute | solution.py:419
  1474.4 25.2 %collective-permute-start.22 = (bf16[144,2048]{1,0:T(8,128)(2,1)}, bf16[144,2048]{1,0:T(8,128)(2,1)}, u32[]{:S(2)}, u32[]{:S(2)}) collective-permute-start(bf16[144,2048]{1,0:T(8,128)(2,1)} %get-tuple-element.136), channel_id=1, source_target_pairs={{0,1},{1,0},{2,3},{3,2},{4,5},{5,4},{6,7},{7,6},{8,9},{9,8},{10,11... | collective-permute-start | bytes 1769480 | tf_op jit(solution)/shard_map/ppermute | solution.py:419
  1499.6 35.1 %collective-permute-done.19 = bf16[144,2048]{1,0:T(8,128)(2,1)} collective-permute-done((bf16[144,2048]{1,0:T(8,128)(2,1)}, bf16[144,2048]{1,0:T(8,128)(2,1)}, u32[]{:S(2)}, u32[]{:S(2)}) %collective-permute-start.19) | collective-permute-done | bytes 589856 | tf_op jit(solution)/shard_map/ppermute | solution.py:419
  1545.9 12.4 collective-permute-done.23
  (349 shorter events, 234.9 us)
Async XLA Ops:
  49.3 674.2 %all-gather.3.cloned.1.call-start = ((), (), s32[]{:S(2)}) async-start(), calls=%async_computation.10 | async-start | bytes 15728640 | tf_op jit(solution)/shard_map/all_gather | solution.py:1434
  67.2 42.0 %collective-permute-start.15 = (s32[2,2]{1,0:T(2,128)S(1)}, s32[2,2]{1,0:T(2,128)S(1)}, u32[]{:S(2)}, u32[]{:S(2)}) collective-permute-start(s32[2,2]{1,0:T(2,128)S(1)} %copy-done.51), channel_id=1, source_target_pairs={{0,4},{4,0},{8,12},{12,8},{16,20},{20,16},{24,28},{28,24},{1,5},{5... | collective-permute-start | bytes 56 | tf_op jit(solution)/shard_map/ppermute | solution.py:414
  76.9 39.7 %collective-permute-start = (bf16[2,144,2048]{2,1,0:T(8,128)(2,1)}, bf16[2,144,2048]{2,1,0:T(8,128)(2,1)}, u32[]{:S(2)}, u32[]{:S(2)}) collective-permute-start(bf16[2,144,2048]{2,1,0:T(8,128)(2,1)} %dynamic-slice_bitcast_fusion.1), channel_id=1, source_target_pairs={{0,4},{4,0},{8,12},{12,8},{16,20},{20,16},{24,28},{28,24},{1,5},{5... | collective-permute-start | bytes 3538952 | tf_op jit(solution)/shard_map/ppermute | solution.py:414
  106.7 1431.0 %reduce-scatter.5.cloned.1.call-start = ((), (), s32[]{:S(2)}) async-start(), calls=%async_computation.9 | async-start | bytes 5242880 | tf_op jit(solution)/shard_map/reduce_scatter | solution.py:1474
  116.5 95.2 %collective-permute-start.8 = (bf16[768,512]{1,0:T(8,128)(2,1)S(1)}, bf16[768,512]{1,0:T(8,128)(2,1)S(1)}, u32[]{:S(2)}, u32[]{:S(2)}) collective-permute-start(bf16[768,512]{1,0:T(8,128)(2,1)S(1)} %pad_maximum_fusion.13), channel_id=1, source_target_pairs={{0,2},{1,3},{2,0},{3,1},{4,6},{5,7},{6,4},{7,5},{8,10},{9,11},{10,... | collective-permute-start | bytes 2359304 | tf_op jit(solution)/shard_map/ppermute | solution.py:419
  120.2 93.6 %collective-permute-start.1 = (bf16[144,2048]{1,0:T(8,128)(2,1)}, bf16[144,2048]{1,0:T(8,128)(2,1)}, u32[]{:S(2)}, u32[]{:S(2)}) collective-permute-start(bf16[144,2048]{1,0:T(8,128)(2,1)} %get-tuple-element.158), channel_id=1, source_target_pairs={{0,1},{1,0},{2,3},{3,2},{4,5},{5,4},{6,7},{7,6},{8,9},{9,8},{10,11... | collective-permute-start | bytes 1769480 | tf_op jit(solution)/shard_map/ppermute | solution.py:419
  122.4 130.9 %collective-permute-start.2 = (bf16[144,2048]{1,0:T(8,128)(2,1)}, bf16[144,2048]{1,0:T(8,128)(2,1)}, u32[]{:S(2)}, u32[]{:S(2)}) collective-permute-start(bf16[144,2048]{1,0:T(8,128)(2,1)} %get-tuple-element.159), channel_id=1, source_target_pairs={{0,2},{1,3},{2,0},{3,1},{4,6},{5,7},{6,4},{7,5},{8,10},{9,11},{10,... | collective-permute-start | bytes 1769480 | tf_op jit(solution)/shard_map/ppermute | solution.py:419
  123.1 130.2 %collective-permute-start.3 = (bf16[144,2048]{1,0:T(8,128)(2,1)}, bf16[144,2048]{1,0:T(8,128)(2,1)}, u32[]{:S(2)}, u32[]{:S(2)}) collective-permute-start(bf16[144,2048]{1,0:T(8,128)(2,1)} %get-tuple-element.160), channel_id=1, source_target_pairs={{0,3},{1,2},{2,1},{3,0},{4,7},{5,6},{6,5},{7,4},{8,11},{9,10},{10,... | collective-permute-start | bytes 1769480 | tf_op jit(solution)/shard_map/ppermute | solution.py:419
  132.0 128.8 %collective-permute-start.7 = (bf16[768,512]{1,0:T(8,128)(2,1)S(1)}, bf16[768,512]{1,0:T(8,128)(2,1)}, u32[]{:S(2)}, u32[]{:S(2)}) collective-permute-start(bf16[768,512]{1,0:T(8,128)(2,1)S(1)} %pad_maximum_fusion.13), channel_id=1, source_target_pairs={{0,1},{1,0},{2,3},{3,2},{4,5},{5,4},{6,7},{7,6},{8,9},{9,8},{10,11... | collective-permute-start | bytes 2359304 | tf_op jit(solution)/shard_map/ppermute | solution.py:419
  211.7 101.2 %collective-permute-start.9 = (bf16[768,512]{1,0:T(8,128)(2,1)S(1)}, bf16[768,512]{1,0:T(8,128)(2,1)}, u32[]{:S(2)}, u32[]{:S(2)}) collective-permute-start(bf16[768,512]{1,0:T(8,128)(2,1)S(1)} %collective-permute-done.8), channel_id=1, source_target_pairs={{0,1},{1,0},{2,3},{3,2},{4,5},{5,4},{6,7},{7,6},{8,9},{9,8},{10,11... | collective-permute-start | bytes 2359304 | tf_op jit(solution)/shard_map/ppermute | solution.py:419
  322.1 49.6 %collective-permute-start.11 = (bf16[144,2048]{1,0:T(8,128)(2,1)S(1)}, bf16[144,2048]{1,0:T(8,128)(2,1)S(1)}, u32[]{:S(2)}, u32[]{:S(2)}) collective-permute-start(bf16[144,2048]{1,0:T(8,128)(2,1)S(1)} %get-tuple-element.150), channel_id=1, source_target_pairs={{0,1},{1,0},{2,3},{3,2},{4,5},{5,4},{6,7},{7,6},{8,9},{9,8},{10,11... | collective-permute-start | bytes 1769480 | tf_op jit(solution)/shard_map/ppermute | solution.py:419
  322.1 62.2 %collective-permute-start.12 = (bf16[144,2048]{1,0:T(8,128)(2,1)S(1)}, bf16[144,2048]{1,0:T(8,128)(2,1)S(1)}, u32[]{:S(2)}, u32[]{:S(2)}) collective-permute-start(bf16[144,2048]{1,0:T(8,128)(2,1)S(1)} %get-tuple-element.151), channel_id=1, source_target_pairs={{0,2},{1,3},{2,0},{3,1},{4,6},{5,7},{6,4},{7,5},{8,10},{9,11},{10,... | collective-permute-start | bytes 1769480 | tf_op jit(solution)/shard_map/ppermute | solution.py:419
  325.0 76.6 %collective-permute-start.13 = (bf16[144,2048]{1,0:T(8,128)(2,1)S(1)}, bf16[144,2048]{1,0:T(8,128)(2,1)S(1)}, u32[]{:S(2)}, u32[]{:S(2)}) collective-permute-start(bf16[144,2048]{1,0:T(8,128)(2,1)S(1)} %get-tuple-element.152), channel_id=1, source_target_pairs={{0,3},{1,2},{2,1},{3,0},{4,7},{5,6},{6,5},{7,4},{8,11},{9,10},{10,... | collective-permute-start | bytes 1769480 | tf_op jit(solution)/shard_map/ppermute | solution.py:419
  992.4 569.1 %reduce-scatter.3.cloned.1.call-start = ((), (), s32[]{:S(2)}) async-start(), calls=%async_computation.8 | async-start | bytes 10485760 | tf_op jit(solution)/shard_map/reduce_scatter | solution.py:1471
  1376.9 42.1 %collective-permute-start.28 = (bf16[768,512]{1,0:T(8,128)(2,1)}, bf16[768,512]{1,0:T(8,128)(2,1)}, u32[]{:S(2)}, u32[]{:S(2)}) collective-permute-start(bf16[768,512]{1,0:T(8,128)(2,1)} %get-tuple-element.120), channel_id=1, source_target_pairs={{0,1},{1,0},{2,3},{3,2},{4,5},{5,4},{6,7},{7,6},{8,9},{9,8},{10,11... | collective-permute-start | bytes 2359304 | tf_op jit(solution)/shard_map/ppermute | solution.py:419
  1403.6 61.8 %collective-permute-start.27 = (bf16[768,512]{1,0:T(8,128)(2,1)}, bf16[768,512]{1,0:T(8,128)(2,1)}, u32[]{:S(2)}, u32[]{:S(2)}) collective-permute-start(bf16[768,512]{1,0:T(8,128)(2,1)} %get-tuple-element.119), channel_id=1, source_target_pairs={{0,1},{1,0},{2,3},{3,2},{4,5},{5,4},{6,7},{7,6},{8,9},{9,8},{10,11... | collective-permute-start | bytes 2359304 | tf_op jit(solution)/shard_map/ppermute | solution.py:419
  1421.2 45.7 %collective-permute-start.29 = (bf16[768,512]{1,0:T(8,128)(2,1)}, bf16[768,512]{1,0:T(8,128)(2,1)}, u32[]{:S(2)}, u32[]{:S(2)}) collective-permute-start(bf16[768,512]{1,0:T(8,128)(2,1)} %fusion.10), channel_id=1, source_target_pairs={{0,2},{1,3},{2,0},{3,1},{4,6},{5,7},{6,4},{7,5},{8,10},{9,11},{10,... | collective-permute-start | bytes 2359304 | tf_op jit(solution)/shard_map/ppermute | solution.py:419
  1457.4 77.3 %collective-permute-start.19 = (bf16[144,2048]{1,0:T(8,128)(2,1)}, bf16[144,2048]{1,0:T(8,128)(2,1)}, u32[]{:S(2)}, u32[]{:S(2)}) collective-permute-start(bf16[144,2048]{1,0:T(8,128)(2,1)} %get-tuple-element.143), channel_id=1, source_target_pairs={{0,2},{1,3},{2,0},{3,1},{4,6},{5,7},{6,4},{7,5},{8,10},{9,11},{10,... | collective-permute-start | bytes 1769480 | tf_op jit(solution)/shard_map/ppermute | solution.py:419
  1457.9 76.8 %collective-permute-start.18 = (bf16[144,2048]{1,0:T(8,128)(2,1)}, bf16[144,2048]{1,0:T(8,128)(2,1)}, u32[]{:S(2)}, u32[]{:S(2)}) collective-permute-start(bf16[144,2048]{1,0:T(8,128)(2,1)} %get-tuple-element.144), channel_id=1, source_target_pairs={{0,1},{1,0},{2,3},{3,2},{4,5},{5,4},{6,7},{7,6},{8,9},{9,8},{10,11... | collective-permute-start | bytes 1769480 | tf_op jit(solution)/shard_map/ppermute | solution.py:419
  1465.4 80.5 %collective-permute-start.24 = (bf16[144,2048]{1,0:T(8,128)(2,1)}, bf16[144,2048]{1,0:T(8,128)(2,1)}, u32[]{:S(2)}, u32[]{:S(2)}) collective-permute-start(bf16[144,2048]{1,0:T(8,128)(2,1)} %get-tuple-element.134), channel_id=1, source_target_pairs={{0,3},{1,2},{2,1},{3,0},{4,7},{5,6},{6,5},{7,4},{8,11},{9,10},{10,... | collective-permute-start | bytes 1769480 | tf_op jit(solution)/shard_map/ppermute | solution.py:419
  1466.9 91.4 %collective-permute-start.23 = (bf16[144,2048]{1,0:T(8,128)(2,1)}, bf16[144,2048]{1,0:T(8,128)(2,1)}, u32[]{:S(2)}, u32[]{:S(2)}) collective-permute-start(bf16[144,2048]{1,0:T(8,128)(2,1)} %get-tuple-element.135), channel_id=1, source_target_pairs={{0,2},{1,3},{2,0},{3,1},{4,6},{5,7},{6,4},{7,5},{8,10},{9,11},{10,... | collective-permute-start | bytes 1769480 | tf_op jit(solution)/shard_map/ppermute | solution.py:419
  1470.6 67.0 %all-to-all-start.3 = ((bf16[8,64,512]{2,1,0:T(8,128)(2,1)}), bf16[8,64,512]{2,1,0:T(8,128)(2,1)S(1)}, u32[]{:S(2)}, u32[]{:S(2)}) async-start(bf16[8,64,512]{2,1,0:T(8,128)(2,1)} %bitcast.87), calls=%async_computation.3 | async-start | bytes 1048576 | tf_op jit(solution)/shard_map/all_to_all | solution.py:1357
  1474.4 83.9 %collective-permute-start.22 = (bf16[144,2048]{1,0:T(8,128)(2,1)}, bf16[144,2048]{1,0:T(8,128)(2,1)}, u32[]{:S(2)}, u32[]{:S(2)}) collective-permute-start(bf16[144,2048]{1,0:T(8,128)(2,1)} %get-tuple-element.136), channel_id=1, source_target_pairs={{0,1},{1,0},{2,3},{3,2},{4,5},{5,4},{6,7},{7,6},{8,9},{9,8},{10,11... | collective-permute-start | bytes 1769480 | tf_op jit(solution)/shard_map/ppermute | solution.py:419
  1545.5 56.0 %collective-permute-start.21 = (bf16[2,144,2048]{2,1,0:T(8,128)(2,1)}, bf16[2,144,2048]{2,1,0:T(8,128)(2,1)}, u32[]{:S(2)}, u32[]{:S(2)}) collective-permute-start(bf16[2,144,2048]{2,1,0:T(8,128)(2,1)} %fusion.19), channel_id=1, source_target_pairs={{0,4},{4,0},{8,12},{12,8},{16,20},{20,16},{24,28},{28,24},{1,5},{5... | collective-permute-start | bytes 3538952 | tf_op jit(solution)/shard_map/ppermute | solution.py:414
  (88 other events, 1588.4 us)
Sparse Core Ops, SparseCore 0:
  66.7 354.9 all-gather.2
  992.5 97.9 reduce-scatter.4
  1092.9 144.9 reduce-scatter.2

commit v3 on v2

--- a/solution.py
+++ b/solution.py
@@ -481,22 +481,32 @@
 STRIPE = 16
 
 
-def peer(mask):
-    place = lax.axis_index("dp")
-    other = place + mask - 2 * mask * lax.rem(lax.div(place, mask), 2)
-    return (other, lax.axis_index("fsdp"))
-
-
-def meet():
+def flip(place, mask):
+    for bit in (1, 2, 4):
+        if mask & bit:
+            place = place + bit - 2 * bit * lax.rem(lax.div(place, bit), 2)
+    return place
+
+
+def peer(mask, planes=0):
+    return (flip(lax.axis_index("dp"), mask), flip(lax.axis_index("fsdp"), planes))
+
+
+SIDES = ((CORE, 0), (SIDE_A, 0), (SIDE_B, 0))
+PLANE = tuple((mask, 0) for mask in range(1, 8))
+PLANES = tuple((0, mask) for mask in range(1, CHUNKS))
+
+
+def meet(others):
     barrier = pltpu.get_barrier_semaphore()
-    for mask in (CORE, SIDE_A, SIDE_B):
-        pl.semaphore_signal(barrier, inc=1, device_id=peer(mask), device_id_type=MESH)
-    pl.semaphore_wait(barrier, 3)
+    for mask, planes in others:
+        pl.semaphore_signal(barrier, inc=1, device_id=peer(mask, planes), device_id_type=MESH)
+    pl.semaphore_wait(barrier, len(others))
 
 
 class Remote:
-    def __init__(self, wires, source, target, mask):
-        self.wires, self.source, self.target, self.mask = wires, source, target, mask
+    def __init__(self, wires, source, target, mask, planes=0):
+        self.wires, self.source, self.target, self.mask = wires, source, target, (mask, planes)
         self.place = wires.count
         wires.count += 1
 
@@ -506,7 +516,7 @@
             dst_ref=self.target,
             send_sem=self.wires.send.at[self.place],
             recv_sem=self.wires.recv.at[self.place],
-            device_id=peer(self.mask),
+            device_id=peer(*self.mask),
             device_id_type=MESH,
         )
 
@@ -728,7 +738,7 @@
 
     def body(rows_ref, cosine_ref, sine_ref, out):
         at_step(pl.program_id(0) * CHIPS + pl.program_id(1), actions)
-        product = dot(rows_ref[0, 0], weight_ref[...])
+        product = dot(rows_ref[0, 0], weight_ref[...].reshape(D, 3 * HEAD))
         angles = (cosine_ref[0], sine_ref[0])
         query = spin(product[:, :HEAD], *angles) * (1.0 / math.sqrt(HEAD))
         key = spin(product[:, HEAD : 2 * HEAD], *angles)
@@ -850,7 +860,7 @@
                     [spin_back(query_grad, *angles), spin_back(key_grad, *angles), value_grad], axis=1
                 ).astype(jnp.bfloat16)
 
-        partial = dot_t(grads_ref[0, 0], weight_ref[...]).astype(jnp.bfloat16)
+        partial = dot_t(grads_ref[0, 0], weight_ref[...].reshape(D, 3 * HEAD)).astype(jnp.bfloat16)
         own_ref[0, 0] = partial[:rows]
         other_ref[0, 0] = partial[rows:]
 
@@ -923,64 +933,218 @@
     return jax.ShapeDtypeStruct(shape, jnp.float32)
 
 
-def gather_and_project(normed, out_grads, weight, cosine, sine):
-    _, rows, width = normed.shape
-    tokens = 2 * rows
-    whole_pair = bf16(2, CHIPS, tokens, width)
-
-    def kernel(normed_ref, grads_ref, weight_ref, cosine_ref, sine_ref, *refs):
-        gathered, grads, states, wires = refs[:2], refs[2:4], refs[4:6], Wires(*refs[6:])
-        meet()
-        rows_moves = [
-            Gather(wires, [normed_ref.at[2 * pair], normed_ref.at[2 * pair + 1]], gathered[pair])
+def start_up(
+    activations, cotangent, head_block, out_block, unit_block, down_block, lengths_block, gain
+):
+    _, tokens, width = activations.shape
+    rows = tokens // 2
+    devices, unit_rows, columns = unit_block.shape
+    down_rows = down_block.shape[1]
+    planes, _, sub_rows, _ = head_block.shape
+    edge = devices * unit_rows
+
+    def kernel(*refs):
+        act, cot, head_in, out_in, unit_in, down_in, length_in, gain_ref = refs[:8]
+        own_rows, own_grads, gathered = refs[8], refs[9], refs[10:12]
+        head_weight, head_output, feed_own, lengths_all = refs[12:16]
+        act_groups, cot_groups, traded, spread, other_half, normed = refs[16:22]
+        wires = Wires(*refs[22:])
+        place, plane = lax.axis_index("dp"), lax.axis_index("fsdp")
+        core = lax.rem(place, 2)
+
+        def half(index):
+            return pl.ds(pl.multiple_of(index * rows, STRIPE), rows)
+
+        def move(source, target):
+            @pl.loop(0, rows // STRIPE)
+            def _(step):
+                span = pl.ds(step * STRIPE, STRIPE)
+                target[span] = source[span]
+
+        def trade(array, groups, own):
+            label = [2 * core + group for group in range(2)]
+            inside = [
+                Remote(wires, array.at[group, half(1 - core)], groups.at[label[group]], CORE)
+                for group in range(2)
+            ]
+            outside = [
+                Remote(wires, groups.at[flip(plane, mask)], own.at[plane], 0, mask)
+                for mask in range(1, CHUNKS)
+            ]
+
+            def keep():
+                for group in range(2):
+                    move(array.at[group, half(core)], groups.at[label[group]])
+
+            return inside, keep, outside, lambda: move(groups.at[plane], own.at[plane])
+
+        act_inside, act_keep, act_outside, act_own = trade(act, act_groups, own_rows)
+        cot_inside, cot_keep, cot_outside, cot_own = trade(cot, cot_groups, own_grads)
+        head_trade = [
+            Remote(wires, head_in.at[flip(plane, mask)], traded.at[plane], 0, mask)
+            for mask in range(1, CHUNKS)
+        ]
+        head_spread, feed_spread = [], []
+        for mask in range(1, devices):
+            other = flip(place, mask)
+            head_spread.append(
+                Remote(
+                    wires,
+                    traded.at[lax.div(other, 2), lax.rem(other, 2)],
+                    spread.at[place, plane],
+                    mask,
+                )
+            )
+            feed_spread.append(
+                Remote(
+                    wires,
+                    unit_in.at[other],
+                    feed_own.at[pl.ds(pl.multiple_of(place * unit_rows, unit_rows), unit_rows)],
+                    mask,
+                )
+            )
+            feed_spread.append(
+                Remote(
+                    wires,
+                    down_in.at[other],
+                    feed_own.at[pl.ds(pl.multiple_of(edge + place * down_rows, down_rows), down_rows)],
+                    mask,
+                )
+            )
+            feed_spread.append(Remote(wires, length_in, lengths_all.at[place], mask))
+
+        def over_planes(block):
+            mine, theirs = block(plane), block(flip(plane, 2))
+            return (
+                [Remote(wires, mine, mine, 0, 1), Remote(wires, mine, mine, 0, 2)],
+                Remote(wires, theirs, theirs, 0, 1),
+            )
+
+        head_near, head_relay = over_planes(lambda index: spread.at[:, index])
+        out_near, out_relay = over_planes(
+            lambda index: head_output.at[:, pl.ds(pl.multiple_of(index * columns, columns), columns)]
+        )
+        core_half = Remote(wires, spread.at[:, :, :, pl.ds(HEAD, HEAD)], other_half, CORE)
+        moves = [
+            Gather(wires, [normed.at[2 * pair], normed.at[2 * pair + 1]], gathered[pair])
             for pair in range(2)
         ]
-        grad_moves = [
-            Gather(wires, [grads_ref.at[2 * pair], grads_ref.at[2 * pair + 1]], grads[pair])
-            for pair in range(2)
-        ]
-        rows_moves[0].first()
-        rows_moves[0].second()
-        rows_moves[1].first()
-        rows_moves[0].third()
-        rows_moves[1].second()
-        grad_moves[0].first()
-        rows_moves[0].last()
-        project_phase(
-            gathered[0], states[0], weight_ref, cosine_ref.at[0], sine_ref.at[0],
-            {4: rows_moves[1].third, 6: grad_moves[0].second},
-        )
-        grad_moves[1].first()
-        rows_moves[1].last()
-        project_phase(
-            gathered[1], states[1], weight_ref, cosine_ref.at[1], sine_ref.at[1],
-            {4: grad_moves[0].third, 6: grad_moves[1].second},
-        )
-        grad_moves[0].last()
-        grad_moves[1].third()
-        grad_moves[1].last()
-
+
+        meet(PLANE + PLANES)
+        for copy in act_inside + cot_inside + head_trade + feed_spread:
+            copy.start()
+        act_keep()
+        for copy in act_inside:
+            copy.arrived()
+        for copy in act_outside:
+            copy.start()
+        cot_keep()
+        act_own()
+        traded[plane] = head_in[plane]
+        columns_at = pl.ds(pl.multiple_of(plane * columns, columns), columns)
+        head_output[:, columns_at] = out_in[...]
+        feed_own[pl.ds(pl.multiple_of(place * unit_rows, unit_rows), unit_rows)] = unit_in[place]
+        feed_own[pl.ds(pl.multiple_of(edge + place * down_rows, down_rows), down_rows)] = down_in[place]
+        lengths_all[place] = length_in[...]
+        for copy in head_trade:
+            copy.arrived()
+        for copy in head_spread:
+            copy.start()
+        spread[place, plane] = traded[lax.div(place, 2), core]
+        for copy in head_spread + cot_inside:
+            copy.arrived()
+        cot_own()
+        for copy in act_outside:
+            copy.arrived()
+        for copy in head_near + out_near:
+            copy.start()
+
+        for chunk in range(CHUNKS):
+
+            @pl.loop(0, rows // STRIPE)
+            def _(step):
+                span = pl.ds(step * STRIPE, STRIPE)
+                values = own_rows[chunk, span].astype(jnp.float32)
+                factor = lax.rsqrt(jnp.mean(values * values, axis=1, keepdims=True) + epsilon)
+                normed[chunk, span] = (values * factor * gain_ref[...]).astype(jnp.bfloat16)
+
+        moves[0].first()
+        moves[0].second()
+        moves[1].first()
+        moves[0].third()
+        moves[1].second()
+        for copy in head_near + out_near:
+            copy.arrived()
+        head_relay.start()
+        out_relay.start()
+        for copy in cot_outside:
+            copy.start()
+        moves[0].last()
+        moves[1].third()
+        head_relay.arrived()
+        core_half.start()
+        moves[1].last()
+        out_relay.arrived()
+        core_half.arrived()
+        head_weight[:, :, :, :HEAD] = spread[:, :, :, :HEAD]
+        for index in range(2):
+
+            @pl.when(core == index)
+            def _():
+                mine, theirs = (1 + index) * HEAD, (2 - index) * HEAD
+                head_weight[:, :, :, mine : mine + HEAD] = spread[:, :, :, HEAD:]
+                head_weight[:, :, :, theirs : theirs + HEAD] = other_half[...]
+
+        for copy in feed_spread + cot_outside:
+            copy.arrived()
+        for copy in (
+            act_inside + cot_inside + head_trade + feed_spread + act_outside + head_spread
+            + head_near + out_near + [head_relay, out_relay, core_half] + cot_outside
+        ):
+            copy.left()
+
+    own = bf16(CHUNKS, rows, width)
     outs = call(
         kernel,
         1,
-        [(normed, HBM), (out_grads, HBM), (weight, VMEM), (cosine, HBM), (sine, HBM)],
-        [(whole_pair, HBM)] * 4 + [(bf16(2, CHIPS, tokens, 3 * HEAD), HBM)] * 2,
-        wire_shapes(60),
-        40,
-    )
-    return outs[:2], outs[2:4], outs[4:6]
-
-
-def attend_and_norm(states, lengths, places, out_weight, inputs, gain):
+        [(activations, VMEM), (cotangent, VMEM), (head_block, VMEM), (out_block, VMEM)]
+        + [(unit_block, VMEM), (down_block, VMEM), (lengths_block, VMEM), (gain, VMEM)],
+        [(own, VMEM), (own, VMEM)]
+        + [(bf16(2, CHIPS, tokens, width), HBM)] * 2
+        + [(bf16(devices, planes, sub_rows, 3 * HEAD), VMEM), (bf16(HEAD, width), VMEM)]
+        + [(bf16(devices * (unit_rows + down_rows), columns), VMEM)]
+        + [(jax.ShapeDtypeStruct((devices,) + lengths_block.shape, jnp.int32), VMEM)],
+        [
+            pltpu.VMEM((CHUNKS, rows, width), jnp.bfloat16),
+            pltpu.VMEM((CHUNKS, rows, width), jnp.bfloat16),
+            pltpu.VMEM((planes, 2, sub_rows, columns), jnp.bfloat16),
+            pltpu.VMEM((devices, planes, sub_rows, columns), jnp.bfloat16),
+            pltpu.VMEM((devices, planes, sub_rows, HEAD), jnp.bfloat16),
+            pltpu.VMEM((CHUNKS, rows, width), jnp.bfloat16),
+        ]
+        + wire_shapes(90),
+        56,
+    )
+    return outs[0], outs[1], outs[2:4], outs[4], outs[5], outs[6], outs[7]
+
+
+def attend_and_norm(
+    rows_all, out_grads, feed_own, weight, cosine, sine, lengths, places, out_weight, inputs, gain
+):
     _, rows, width = inputs.shape
     tokens = 2 * rows
+    planes = CHUNKS
+    whole_pair = bf16(2, CHIPS, tokens, width)
 
     def kernel(*refs):
-        states_in, (lengths_ref, place_q, place_k, weight_ref, inputs_ref, gain_ref) = refs[:2], refs[2:8]
-        mixed, middle, normed, target = refs[8:10], refs[10], refs[11], refs[12]
-        parts, landings = (refs[13:15], refs[15:17]), (refs[17:20], refs[20:23])
-        stage, keys, values, wires = refs[23:27], refs[27], refs[28], Wires(*refs[29:])
-        meet()
+        gathered, grads_ref, feed_ref, head_ref, cosine_ref, sine_ref = refs[:2], *refs[2:7]
+        lengths_ref, place_q, place_k, weight_ref, inputs_ref, gain_ref = refs[7:13]
+        refs = refs[13:]
+        states, mixed, middle, normed, target, grads_all, feed_all = refs[:2], refs[2:4], *refs[4:9]
+        parts, landings = (refs[9:11], refs[11:13]), (refs[13:16], refs[16:19])
+        stage, keys, values, normed_late = refs[19:23], refs[23], refs[24], refs[25]
+        wires = Wires(*refs[26:])
+        plane = lax.axis_index("fsdp")
 
         def finish(pair):
             def done(chunk, span, total):
@@ -988,53 +1152,82 @@
                 total = total + inputs_ref[at, span].astype(jnp.float32)
                 middle[at, span] = total
                 factor = lax.rsqrt(jnp.mean(total * total, axis=1, keepdims=True) + epsilon)
-                normed[at, span] = (total * factor * gain_ref[...]).astype(jnp.bfloat16)
+                kept = normed if pair == 0 else normed_late
+                kept[chunk, span] = (total * factor * gain_ref[...]).astype(jnp.bfloat16)
 
             return done
 
         sums = [
             Scatter(wires, *parts[pair], landings[pair], stage, finish(pair)) for pair in range(2)
         ]
-        move = Gather(wires, [normed.at[2], normed.at[3]], target)
+        move = Gather(wires, [normed_late.at[0], normed_late.at[1]], target)
+        grad_move = Gather(wires, [grads_ref.at[2], grads_ref.at[3]], grads_all)
+        near = Remote(wires, feed_ref, feed_all.at[plane], 0, 1)
+        across_middle = Remote(wires, feed_ref, feed_all.at[plane], 0, 2)
+        relay = Remote(
+            wires, feed_all.at[flip(plane, 2)], feed_all.at[flip(plane, 2)], 0, 1
+        )
         places_in = (place_q, place_k)
+
+        meet(SIDES + PLANES[:2])
+        near.start()
+        across_middle.start()
+        grad_move.first()
+        wires.load([(feed_ref, feed_all.at[plane])])
+        project_phase(
+            gathered[0], states[0], head_ref, cosine_ref.at[0], sine_ref.at[0], {7: grad_move.second}
+        )
+        project_phase(gathered[1], states[1], head_ref, cosine_ref.at[1], sine_ref.at[1], {})
         attend_phase(
-            1, states_in, mixed[1], *parts[1], lengths_ref, places_in, weight_ref, keys, values, {}
+            1, states, mixed[1], *parts[1], lengths_ref, places_in, weight_ref, keys, values,
+            {3: grad_move.third},
         )
         sums[1].first()
         attend_phase(
-            0, states_in, mixed[0], *parts[0], lengths_ref, places_in, weight_ref, keys, values,
+            0, states, mixed[0], *parts[0], lengths_ref, places_in, weight_ref, keys, values,
             {5: sums[1].second},
         )
         sums[0].first()
+        grad_move.last()
         sums[1].third()
         sums[0].second()
         sums[1].last()
         move.first()
         sums[0].third()
+        across_middle.arrived()
+        relay.start()
         move.second()
         sums[0].last()
         move.third()
         move.last()
+        near.arrived()
+        relay.arrived()
+        for copy in (near, across_middle, relay):
+            copy.left()
 
     pair_parts = [(shape, HBM) for shape in partial_shapes(rows, width)]
     landing = [(shape, HBM) for shape in landing_shapes(rows, width)]
     outs = call(
         kernel,
         2,
-        [(state, HBM) for state in states]
+        [(rows_all[0], HBM), (rows_all[1], HBM), (out_grads, VMEM), (feed_own, VMEM)]
+        + [(weight, VMEM), (cosine, HBM), (sine, HBM)]
         + [(lengths, SMEM), (places[0], VMEM), (places[1], VMEM), (out_weight, VMEM)]
         + [(inputs, VMEM), (gain, VMEM)],
-        [(bf16(2, CHIPS, tokens, HEAD), HBM)] * 2
-        + [(f32(CHUNKS, rows, width), VMEM), (bf16(CHUNKS, rows, width), VMEM)]
-        + [(bf16(2, CHIPS, tokens, width), HBM)]
+        [(bf16(2, CHIPS, tokens, 3 * HEAD), HBM)] * 2
+        + [(bf16(2, CHIPS, tokens, HEAD), HBM)] * 2
+        + [(f32(CHUNKS, rows, width), VMEM), (bf16(2, rows, width), VMEM)]
+        + [(whole_pair, HBM)] * 2
+        + [(bf16(planes, *feed_own.shape), HBM)]
         + pair_parts * 2
         + landing * 2,
         stage_shapes(rows, width)
         + [pltpu.VMEM((CHUNKS * tokens, HEAD), jnp.bfloat16)] * 2
-        + wire_shapes(30),
-        56,
-    )
-    return outs[:2], outs[2], outs[3], outs[4]
+        + [pltpu.VMEM((2, rows, width), jnp.bfloat16)]
+        + wire_shapes(50),
+        60,
+    )
+    return outs[:2], outs[2:4], outs[4], outs[5], outs[6], outs[7], outs[8]
 
 
 def norm_back(values, gain, gradient):
@@ -1045,21 +1238,22 @@
     return back, gradient * scaled
 
 
-def feed_forward(normed_own, normed_late, out_grads, weights, middle, out_grad_own, gain, units):
+def feed_forward(normed_own, normed_late, grads_late, weights, middle, out_grad_own, gain, units):
     _, rows, width = middle.shape
     tokens = 2 * rows
     shards, columns = weights.shape[0], weights.shape[2]
     whole_pair = bf16(2, CHIPS, tokens, width)
 
     def kernel(*refs):
-        normed_ref, normed_late_ref, *grads = refs[:4]
-        weight_ref, middle_ref, own_grad, gain_ref = refs[4:8]
-        normed_early, branch = refs[8:10]
+        normed_ref, normed_late_ref, grads_late_ref = refs[:3]
+        weight_ref, middle_ref, own_grad, gain_ref = refs[3:7]
+        refs = (None, *refs)
+        normed_early, branch, grads_early = refs[8], refs[9], refs[27]
         hidden, unit_grads = refs[10:12], refs[12:14]
         back_parts, out_parts = (refs[14:16], refs[16:18]), (refs[18:20], refs[20:22])
         middle_grad, gain_sum, landing = refs[22], refs[23], refs[24:27]
-        stage, own_branch, wires = refs[27:31], refs[31], Wires(*refs[32:])
-        meet()
+        stage, own_branch, wires = refs[28:32], refs[32], Wires(*refs[33:])
+        meet(SIDES)
         gain_sum[...] = jnp.zeros(gain_sum.shape, jnp.float32)
 
         def done(chunk, span, total):
@@ -1072,15 +1266,19 @@
         move = Gather(wires, [normed_ref.at[0], normed_ref.at[1]], normed_early)
         sums = Scatter(wires, *back_parts[1], landing, stage, done)
         late_move = Gather(wires, [own_branch.at[0], own_branch.at[1]], branch)
+        grad_move = Gather(wires, [own_grad.at[0], own_grad.at[1]], grads_early)
         move.first()
+        grad_move.first()
         feed_phase(
-            normed_late_ref, grads[1], hidden[1], unit_grads[1], back_parts[1], out_parts[1], weight_ref,
-            {2: move.second, 5: move.third},
+            normed_late_ref, grads_late_ref, hidden[1], unit_grads[1], back_parts[1], out_parts[1],
+            weight_ref,
+            {2: move.second, 3: grad_move.second, 5: move.third, 7: grad_move.third},
         )
         sums.first()
         move.last()
+        grad_move.last()
         feed_phase(
-            normed_early, grads[0], hidden[0], unit_grads[0], back_parts[0], out_parts[0], weight_ref,
+            normed_early, grads_early, hidden[0], unit_grads[0], back_parts[0], out_parts[0], weight_ref,
             {1: sums.second, 4: sums.third, 6: lambda: (sums.last(), late_move.first()) and None},
         )
         late_move.second()
@@ -1090,19 +1288,19 @@
     outs = call(
         kernel,
         3,
-        [(normed_own, HBM), (normed_late, HBM)]
-        + [(grads, HBM) for grads in out_grads]
+        [(normed_own, VMEM), (normed_late, HBM), (grads_late, HBM)]
         + [(weights, VMEM), (middle, VMEM), (out_grad_own, VMEM), (gain, VMEM)],
         [(whole_pair, HBM)] * 2
         + [(bf16(2, CHIPS, tokens, units), HBM)] * 2
         + [(bf16(shards, 2, CHIPS, tokens, columns), HBM)] * 2
         + [(shape, HBM) for shape in partial_shapes(rows, width)] * 4
         + [(f32(2, rows, width), VMEM), (f32(STRIPE, width), VMEM)]
-        + [(shape, HBM) for shape in landing_shapes(rows, width)],
-        stage_shapes(rows, width) + [pltpu.VMEM((2, rows, width), jnp.bfloat16)] + wire_shapes(40),
+        + [(shape, HBM) for shape in landing_shapes(rows, width)]
+        + [(whole_pair, HBM)],
+        stage_shapes(rows, width) + [pltpu.VMEM((2, rows, width), jnp.bfloat16)] + wire_shapes(50),
         62,
     )
-    return outs[0], outs[1], outs[2:4], outs[4:6], outs[6:8], (outs[10:12], outs[12:14]), outs[14], outs[15]
+    return outs[19], outs[0], outs[1], outs[2:4], outs[4:6], outs[6:8], (outs[10:12], outs[12:14]), outs[14], outs[15]
 
 
 def attend_back(
@@ -1125,7 +1323,7 @@
         landings = [refs[32 + 3 * place : 35 + 3 * place] for place in range(5)]
         stage, early_grad, own_branch, keys, values = refs[47:51], refs[51], refs[52], refs[53], refs[54]
         sums, late_sums, wires = refs[55:57], refs[57:59], Wires(*refs[59:])
-        meet()
+        meet(SIDES)
         gain_sums[...] = jnp.zeros(gain_sums.shape, jnp.float32)
 
         def middle_done(chunk, span, total):
@@ -1388,32 +1586,13 @@
     tokens = activations.shape[1]
     half = tokens // 2
 
-    inputs = to_planes(activations, core, plane)
-
     in_rows = query_weight.shape[0]
     sub_rows = in_rows // planes
     spread = devices * sub_rows
+
     mixed_kv = jnp.stack([key_weight.astype(low), value_weight.astype(low)], axis=1)
     block = jnp.concatenate([query_weight.astype(low).reshape(in_rows, 2, HEAD), mixed_kv], axis=2)
-    block = jnp.stack(trade_planes(block.reshape(planes, sub_rows, 2, 2 * HEAD), plane))
-    block = block.transpose(0, 2, 1, 3).reshape(devices, sub_rows, 2 * HEAD)
-    block = exchange(block, "dp")
-    attention_block = jnp.concatenate(
-        [block.reshape(spread, 2 * HEAD), output_weight.astype(low)], axis=0
-    )
-    found = jnp.stack(gather_planes(after(attention_block, inputs)))
-    attention_all = jnp.stack([pick(found, label ^ plane) for label in range(CHUNKS)])
-    packed = (
-        attention_all[:, :spread]
-        .reshape(planes, devices, sub_rows, 2 * HEAD)
-        .transpose(1, 0, 2, 3)
-        .reshape(D, 2 * HEAD)
-    )
-    other_half = across(packed[:, HEAD:], CORE)
-    key_part = jnp.where(core == 0, packed[:, HEAD:], other_half)
-    value_part = jnp.where(core == 0, other_half, packed[:, HEAD:])
-    head_weight = jnp.concatenate([packed[:, :HEAD], key_part, value_part], axis=1)
-    head_output = attention_all[:, spread:].transpose(1, 0, 2).reshape(HEAD, D)
+    head_block = block.reshape(planes, sub_rows, 2, 2 * HEAD).swapaxes(1, 2)
 
     strip = 128
     runs = gate_weight.shape[1] // (devices * strip)
@@ -1425,25 +1604,29 @@
         ]
     )
     gate_up = gate_up.transpose(3, 1, 0, 2, 4).reshape(devices, in_rows, 2 * runs * strip)
-    gate_up = exchange(gate_up, "dp").reshape(devices * in_rows, 2 * runs * strip)
     down_columns = down_weight.shape[1]
-    down = exchange(down_weight.astype(low).reshape(devices, strip, down_columns), "dp")
-    feed_block = jnp.concatenate([gate_up, down.reshape(devices * strip, down_columns)], axis=0)
-
-    out_grads = to_planes(after(cotangent, attention_all), core, plane)
-    feed_weights = lax.all_gather(after(feed_block, out_grads), "fsdp", axis=0, tiled=False)
-
-    others = across(continuation_lengths, CORE)
-    swap = core == 1
-    here = jnp.concatenate(
+    down = down_weight.astype(low).reshape(devices, strip, down_columns)
+
+    gain_one, gain_two = attention_gain[None, :], feedforward_gain[None, :]
+    length_block = jnp.zeros((8, 128), jnp.int32).at[:2, :NCONT].set(continuation_lengths)
+    own_inputs, own_grads, rows_all, head_weight, head_output, feed_own, all_lengths = start_up(
+        activations,
+        cotangent,
+        head_block,
+        output_weight.astype(low),
+        gate_up,
+        down,
+        length_block,
+        gain_one,
+    )
+
+    first_core = place - core
+    lengths = jnp.stack(
         [
-            jnp.where(swap, others, continuation_lengths),
-            jnp.where(swap, continuation_lengths, others),
+            pick(pick(all_lengths, (first_core ^ mask) + plane // 2), plane % 2)[:NCONT]
+            for mask in (0, SIDE_A, SIDE_B, SIDE_A + SIDE_B)
         ]
     )
-    here = pick(here, plane)
-    near = jnp.stack([here, across(here, SIDE_A)])
-    lengths = jnp.concatenate([near, across(near, SIDE_B)])
 
     inside = jnp.concatenate(
         [core * half + jnp.arange(half), (1 - core) * half + jnp.arange(half)]
@@ -1455,18 +1638,31 @@
     place_q, place_k = inside[:, None], order[None, :]
     blocks = plane ^ jnp.arange(CHUNKS, dtype=jnp.int32)
 
-    own_inputs, own_grads = jnp.stack(inputs), jnp.stack(out_grads)
-    normed, _ = rms_rows(own_inputs.astype(jnp.float32), attention_gain)
-    gain_one, gain_two = attention_gain[None, :], feedforward_gain[None, :]
-    rows_all, grads_all, states = gather_and_project(
-        normed.astype(low), own_grads, head_weight, cosine, sine
-    )
-    mixed, middle, normed_two, normed_late = attend_and_norm(
-        states, lengths, (place_q, place_k), head_output, own_inputs, gain_two
-    )
-    normed_early, branch_late, hidden, unit_grads, back_early, out_parts, middle_grad, gain_sum = feed_forward(
-        normed_two, normed_late, grads_all, feed_weights, middle, own_grads, gain_two, units
-    )
+    states, mixed, middle, normed_two, normed_late, grads_late, feed_weights = attend_and_norm(
+        rows_all,
+        own_grads,
+        feed_own,
+        head_weight,
+        cosine,
+        sine,
+        lengths,
+        (place_q, place_k),
+        head_output,
+        own_inputs,
+        gain_two,
+    )
+    (
+        grads_early,
+        normed_early,
+        branch_late,
+        hidden,
+        unit_grads,
+        back_early,
+        out_parts,
+        middle_grad,
+        gain_sum,
+    ) = feed_forward(normed_two, normed_late, grads_late, feed_weights, middle, own_grads, gain_two, units)
+    grads_all = (grads_early, grads_late)
     unit_sum = unit_weight_grads(unit_grads, (normed_early, normed_late))
     unit_sum = lax.psum_scatter(unit_sum, "fsdp", scatter_dimension=0, tiled=False)
     down_sum = reduce(jnp.add, [token_dot(hidden[pair], grads_all[pair]) for pair in (1, 0)]).astype(low)

time: 1670 us -> 1350 us (0.81)
  waiting for transfers between devices: 429 us -> 109 us
  Pallas kernels: 904 us -> 967 us
  starting transfers between devices: 111 us -> 55.3 us
    ppermute x28 -> x16, waiting for transfers between devices: 371 us -> 102 us  [along(): lax.ppermute(value, 'fsdp', [(place, place ^ mask) for place in range(cou...]
    pallas_call x4, Pallas kernels: 843 us -> 905 us  [call(): pl.pallas_call(kernel, in_specs=[pl.BlockSpec(memory_space=place) for _,...]
    all_to_all x6 -> x3, waiting for transfers between devices: 48.1 us -> 2.87 us  [exchange(): return lax.all_to_all(value, axis, split_axis=0, concat_axis=0, tiled=True)]
    ppermute x28 -> x16, starting transfers between devices: 81 us -> 39.9 us  [along(): lax.ppermute(value, 'fsdp', [(place, place ^ mask) for place in range(cou...]
  transfers between devices with their start and end apart: 52 -> 30, of which waited for: 29 -> 14; matrix products, arithmetic and copies ran while one was open for 6% -> 6% of each run, Pallas kernels for 40% -> 26%
where the time goes in v3:
time: 1350 us; the launch traced here: 1340 us
  Pallas kernels  967 us (72%)
  waiting for transfers between devices  109 us (8%)
  other arithmetic  69.1 us (5%)
  matrix products  62.5 us (5%)
  starting transfers between devices  55.3 us (4%)
  local copies, waits for them, and re-layouts  47.6 us (4%)
  between operations  30.7 us (2%)
    pallas_call x4, Pallas kernels, call(): pl.pallas_call(kernel, in_specs=[pl.BlockSpec(memory_space=place) for _,...  905 us
    ppermute x16, waiting for transfers between devices, along(): lax.ppermute(value, 'fsdp', [(place, place ^ mask) for place in range(cou...  102 us
    dot_general x6, matrix products, token_dot(): lax.dot_general(left.reshape(-1, left.shape[-1]), right.reshape(-1, right...  62.5 us
    pallas_call x1, Pallas kernels, unit_weight_grads(): pl.pallas_call(kernel, grid=(shards, 4), in_specs=specs, out_specs=pl.Blo...  62.2 us
    ppermute x16, starting transfers between devices, along(): lax.ppermute(value, 'fsdp', [(place, place ^ mask) for place in range(cou...  39.9 us
  transfers between devices with their start and end apart: 30, of which 14 were waited for; matrix products, arithmetic and copies ran while one was open for 6% of the time, Pallas kernels for 26%

profile of v3, /device:TPU:0, one launch (start us, length us, event | category | flops | bytes accessed | tf_op | source)
XLA Modules:
  0.0 1341.5 jit_solution(10670845287428421055)
XLA Ops:
  17.4 4.3 maximum_bitcast_fusion
  21.7 4.2 reshape.269.refs_4_
  27.0 3.2 multiply_sine_fusion
  31.1 184.3 %shard_map.364 = (bf16[4,144,2048]{2,1,0:T(8,128)(2,1)}, bf16[4,144,2048]{2,1,0:T(8,128)(2,1)}, bf16[2,4,288,2048]{3,2,1,0:T(8,128)(2,1)}, bf16[2,4,288,2048]{3,...) custom-call(bf16[2,288,2048]{2,1,0:T(8,128)(2,1)} %refs_0_.1, ...), custom_call_target="tpu_custom_call" | custom-call | tf_op jit(solution)/shard_map/pallas_call | solution.py:716
  216.6 215.1 %shard_map.365 = (bf16[2,4,288,768]{3,2,1,0:T(8,128)(2,1)}, bf16[2,4,288,768]{3,2,1,0:T(8,128)(2,1)}, bf16[2,4,288,256]{3,2,1,0:T(8,128)(2,1)}, bf16[2,4,288,256...) custom-call(bf16[2,4,288,2048]{3,2,1,0:T(8,128)(2,1)} %get-tuple-ele, ...), custom_call_target="tpu_custom_call" | custom-call | tf_op jit(solution)/shard_map/pallas_call | solution.py:716
  431.8 221.6 %shard_map.366 = (bf16[2,4,288,2048]{3,2,1,0:T(8,128)(2,1)}, bf16[2,4,288,2048]{3,2,1,0:T(8,128)(2,1)}, bf16[2,4,288,1024]{3,2,1,0:T(8,128)(2,1)}, bf16[2,4,288,...) custom-call(bf16[2,144,2048]{2,1,0:T(8,128)(2,1)} %get-tuple-element, ...), custom_call_target="tpu_custom_call" | custom-call | tf_op jit(solution)/shard_map/pallas_call | solution.py:716
  653.4 16.7 %fusion.43 = f32[1024,2048,1,1]{1,0,3,2:T(8,128)} fusion(bf16[2,4,288,1024]{3,2,1,0:T(8,128)(2,1)} %get-tuple-element.104, bf16[2,4,288,2048]{3,2,1,0:T(8,128)(2,1)} %get-tuple-element.83.refs_2_), kind=kOutput, calls=%fused_computation.173 | convolution fusion | flops 9663676416 | bytes 22544384 | tf_op jit(solution)/shard_map/dot_general | solution.py:1546
  670.2 12.3 fusion
  684.9 62.2 %shard_map.368 = bf16[4,512,2048]{2,1,0:T(8,128)(2,1)} custom-call(bf16[4,2,4,288,512]{4,3,2,1,0:T(8,128)(2,1)} %get-tuple-element.101.late_units, bf16[2,4,288,2048]{3,2,1,0:T(8,128)(2,1)} %get-tuple-element.82.refs_1_.late_rows, bf16[4,2,4,288,512]{4,3,2,1,0:T(8,128)(2,1)} %get-tuple-element.102.early_units, ...), custom_call_target="tpu_custom_call" | custom-call | tf_op jit(solution)/shard_map/pallas_call | solution.py:1475
  747.1 283.9 %shard_map.367 = (bf16[2,4,288,768]{3,2,1,0:T(8,128)(2,1)}, bf16[2,4,288,768]{3,2,1,0:T(8,128)(2,1)}, bf16[2,4,288,2048]{3,2,1,0:T(8,128)(2,1)}, bf16[4,144,2048...) custom-call(bf16[2,4,288,768]{3,2,1,0:T(8,128)(2,1)} %get-tuple-elem, ...), custom_call_target="tpu_custom_call" | custom-call | tf_op jit(solution)/shard_map/pallas_call | solution.py:716
  1031.0 11.4 fusion.42
  1042.4 10.5 fusion.1
  1058.1 5.3 convolution_bitcast_fusion
  1063.4 6.3 fusion.3
  1084.3 15.4 %collective-permute-done.10 = bf16[768,512]{1,0:T(8,128)(2,1)} collective-permute-done((bf16[768,512]{1,0:T(8,128)(2,1)}, bf16[768,512]{1,0:T(8,128)(2,1)}, u32[]{:S(2)}, u32[]{:S(2)}) %collective-permute-start.10) | collective-permute-done | bytes 786464 | tf_op jit(solution)/shard_map/ppermute | solution.py:419
  1108.0 23.2 %collective-permute-done.23 = f32[2,2048]{1,0:T(2,128)S(1)} collective-permute-done((f32[2,2048]{1,0:T(2,128)S(1)}, f32[2,2048]{1,0:T(2,128)S(1)}, u32[]{:S(2)}, u32[]{:S(2)}) %collective-permute-start.23) | collective-permute-done | bytes 16416 | tf_op jit(solution)/shard_map/ppermute | solution.py:419
  1152.4 3.5 all-to-all-start
  1155.9 22.7 %collective-permute-start.4 = (bf16[144,2048]{1,0:T(8,128)(2,1)}, bf16[144,2048]{1,0:T(8,128)(2,1)}, u32[]{:S(2)}, u32[]{:S(2)}) collective-permute-start(bf16[144,2048]{1,0:T(8,128)(2,1)} %get-tuple-element.148), channel_id=1, source_target_pairs={{0,1},{1,0},{2,3},{3,2},{4,5},{5,4},{6,7},{7,6},{8,9},{9,8},{10,11... | collective-permute-start | bytes 1769480 | tf_op jit(solution)/shard_map/ppermute | solution.py:419
  1178.6 37.4 %collective-permute-done.1 = bf16[144,2048]{1,0:T(8,128)(2,1)} collective-permute-done((bf16[144,2048]{1,0:T(8,128)(2,1)}, bf16[144,2048]{1,0:T(8,128)(2,1)}, u32[]{:S(2)}, u32[]{:S(2)}) %collective-permute-start.1) | collective-permute-done | bytes 589856 | tf_op jit(solution)/shard_map/ppermute | solution.py:419
  1219.0 3.7 all-to-all-start.2
  1227.2 13.6 %collective-permute-done.5 = bf16[144,2048]{1,0:T(8,128)(2,1)} collective-permute-done((bf16[144,2048]{1,0:T(8,128)(2,1)}, bf16[144,2048]{1,0:T(8,128)(2,1)}, u32[]{:S(2)}, u32[]{:S(2)}) %collective-permute-start.5) | collective-permute-done | bytes 589856 | tf_op jit(solution)/shard_map/ppermute | solution.py:419
  1248.9 3.6 all-to-all-start.1
  1264.9 4.7 collective-permute-done.13
  1321.7 4.5 multiply_subtract_fusion.2
  (239 shorter events, 137.1 us)
Async XLA Ops:
  7.2 1211.8 %reduce-scatter.5.cloned.1.call-start = ((), (), s32[]{:S(2)}) async-start(), calls=%async_computation.6 | async-start | bytes 5242880 | tf_op jit(solution)/shard_map/reduce_scatter | solution.py:1670
  684.8 559.1 %reduce-scatter.3.cloned.1.call-start = ((), (), s32[]{:S(2)}) async-start(), calls=%async_computation.5 | async-start | bytes 10485760 | tf_op jit(solution)/shard_map/reduce_scatter | solution.py:1667
  1054.9 16.4 %collective-permute-start.8 = (bf16[2048,256]{0,1:T(8,128)(2,1)S(1)}, bf16[2048,256]{0,1:T(8,128)(2,1)S(1)}, u32[]{:S(2)}, u32[]{:S(2)}) collective-permute-start(bf16[2048,256]{0,1:T(8,128)(2,1)S(1)} %get-tuple-element.140), channel_id=1, source_target_pairs={{0,4},{4,0},{8,12},{12,8},{16,20},{20,16},{24,28},{28,24},{1,5},{5... | collective-permute-start | bytes 3145736 | tf_op jit(solution)/shard_map/ppermute | solution.py:414
  1079.1 20.7 %collective-permute-start.10 = (bf16[768,512]{1,0:T(8,128)(2,1)}, bf16[768,512]{1,0:T(8,128)(2,1)}, u32[]{:S(2)}, u32[]{:S(2)}) collective-permute-start(bf16[768,512]{1,0:T(8,128)(2,1)} %get-tuple-element.138), channel_id=1, source_target_pairs={{0,1},{1,0},{2,3},{3,2},{4,5},{5,4},{6,7},{7,6},{8,9},{9,8},{10,11... | collective-permute-start | bytes 2359304 | tf_op jit(solution)/shard_map/ppermute | solution.py:419
  1081.7 20.4 %collective-permute-start.21 = (f32[2,2048]{1,0:T(2,128)S(1)}, f32[2,2048]{1,0:T(2,128)S(1)}, u32[]{:S(2)}, u32[]{:S(2)}) collective-permute-start(f32[2,2048]{1,0:T(2,128)S(1)} %fusion.37), channel_id=1, source_target_pairs={{0,8},{4,12},{8,0},{12,4},{16,24},{20,28},{24,16},{28,20},{1,9},{5... | collective-permute-start | bytes 49160 | tf_op jit(solution)/shard_map/ppermute | solution.py:414
  1082.6 63.7 %collective-permute-start.9 = (bf16[768,512]{1,0:T(8,128)(2,1)}, bf16[768,512]{1,0:T(8,128)(2,1)}, u32[]{:S(2)}, u32[]{:S(2)}) collective-permute-start(bf16[768,512]{1,0:T(8,128)(2,1)} %get-tuple-element.137), channel_id=1, source_target_pairs={{0,1},{1,0},{2,3},{3,2},{4,5},{5,4},{6,7},{7,6},{8,9},{9,8},{10,11... | collective-permute-start | bytes 2359304 | tf_op jit(solution)/shard_map/ppermute | solution.py:419
  1102.0 46.7 %collective-permute-start.11 = (bf16[768,512]{1,0:T(8,128)(2,1)}, bf16[768,512]{1,0:T(8,128)(2,1)}, u32[]{:S(2)}, u32[]{:S(2)}) collective-permute-start(bf16[768,512]{1,0:T(8,128)(2,1)} %fusion.7), channel_id=1, source_target_pairs={{0,2},{1,3},{2,0},{3,1},{4,6},{5,7},{6,4},{7,5},{8,10},{9,11},{10,... | collective-permute-start | bytes 2359304 | tf_op jit(solution)/shard_map/ppermute | solution.py:419
  1106.0 25.2 %collective-permute-start.23 = (f32[2,2048]{1,0:T(2,128)S(1)}, f32[2,2048]{1,0:T(2,128)S(1)}, u32[]{:S(2)}, u32[]{:S(2)}) collective-permute-start(f32[2,2048]{1,0:T(2,128)S(1)} %add.370), channel_id=1, source_target_pairs={{0,1},{1,0},{2,3},{3,2},{4,5},{5,4},{6,7},{7,6},{8,9},{9,8},{10,11... | collective-permute-start | bytes 49160 | tf_op jit(solution)/shard_map/ppermute | solution.py:419
  1131.2 8.6 collective-permute-start.24
  1136.8 19.0 %collective-permute-start.2 = (bf16[144,2048]{1,0:T(8,128)(2,1)}, bf16[144,2048]{1,0:T(8,128)(2,1)}, u32[]{:S(2)}, u32[]{:S(2)}) collective-permute-start(bf16[144,2048]{1,0:T(8,128)(2,1)} %get-tuple-element.154), channel_id=1, source_target_pairs={{0,3},{1,2},{2,1},{3,0},{4,7},{5,6},{6,5},{7,4},{8,11},{9,10},{10,... | collective-permute-start | bytes 1769480 | tf_op jit(solution)/shard_map/ppermute | solution.py:419
  1139.2 76.9 %collective-permute-start.1 = (bf16[144,2048]{1,0:T(8,128)(2,1)}, bf16[144,2048]{1,0:T(8,128)(2,1)}, u32[]{:S(2)}, u32[]{:S(2)}) collective-permute-start(bf16[144,2048]{1,0:T(8,128)(2,1)} %get-tuple-element.155), channel_id=1, source_target_pairs={{0,2},{1,3},{2,0},{3,1},{4,6},{5,7},{6,4},{7,5},{8,10},{9,11},{10,... | collective-permute-start | bytes 1769480 | tf_op jit(solution)/shard_map/ppermute | solution.py:419
  1139.8 76.2 %collective-permute-start = (bf16[144,2048]{1,0:T(8,128)(2,1)}, bf16[144,2048]{1,0:T(8,128)(2,1)}, u32[]{:S(2)}, u32[]{:S(2)}) collective-permute-start(bf16[144,2048]{1,0:T(8,128)(2,1)} %get-tuple-element.156), channel_id=1, source_target_pairs={{0,1},{1,0},{2,3},{3,2},{4,5},{5,4},{6,7},{7,6},{8,9},{9,8},{10,11... | collective-permute-start | bytes 1769480 | tf_op jit(solution)/shard_map/ppermute | solution.py:419
  1146.3 80.9 %collective-permute-start.6 = (bf16[144,2048]{1,0:T(8,128)(2,1)}, bf16[144,2048]{1,0:T(8,128)(2,1)}, u32[]{:S(2)}, u32[]{:S(2)}) collective-permute-start(bf16[144,2048]{1,0:T(8,128)(2,1)} %get-tuple-element.146), channel_id=1, source_target_pairs={{0,3},{1,2},{2,1},{3,0},{4,7},{5,6},{6,5},{7,4},{8,11},{9,10},{10,... | collective-permute-start | bytes 1769480 | tf_op jit(solution)/shard_map/ppermute | solution.py:419
  1148.7 92.1 %collective-permute-start.5 = (bf16[144,2048]{1,0:T(8,128)(2,1)}, bf16[144,2048]{1,0:T(8,128)(2,1)}, u32[]{:S(2)}, u32[]{:S(2)}) collective-permute-start(bf16[144,2048]{1,0:T(8,128)(2,1)} %get-tuple-element.147), channel_id=1, source_target_pairs={{0,2},{1,3},{2,0},{3,1},{4,6},{5,7},{6,4},{7,5},{8,10},{9,11},{10,... | collective-permute-start | bytes 1769480 | tf_op jit(solution)/shard_map/ppermute | solution.py:419
  1152.4 66.6 %all-to-all-start = ((bf16[8,64,512]{2,1,0:T(8,128)(2,1)}), bf16[8,64,512]{2,1,0:T(8,128)(2,1)S(1)}, u32[]{:S(2)}, u32[]{:S(2)}) async-start(bf16[8,64,512]{2,1,0:T(8,128)(2,1)} %bitcast.51), calls=%async_computation | async-start | bytes 1048576 | tf_op jit(solution)/shard_map/all_to_all | solution.py:1555
  1155.9 84.9 %collective-permute-start.4 = (bf16[144,2048]{1,0:T(8,128)(2,1)}, bf16[144,2048]{1,0:T(8,128)(2,1)}, u32[]{:S(2)}, u32[]{:S(2)}) collective-permute-start(bf16[144,2048]{1,0:T(8,128)(2,1)} %get-tuple-element.148), channel_id=1, source_target_pairs={{0,1},{1,0},{2,3},{3,2},{4,5},{5,4},{6,7},{7,6},{8,9},{9,8},{10,11... | collective-permute-start | bytes 1769480 | tf_op jit(solution)/shard_map/ppermute | solution.py:419
  1219.0 28.9 %all-to-all-start.2 = ((bf16[8,128,512]{2,1,0:T(8,128)(2,1)}), bf16[8,128,512]{2,1,0:T(8,128)(2,1)S(1)}, u32[]{:S(2)}, u32[]{:S(2)}) async-start(bf16[8,128,512]{2,1,0:T(8,128)(2,1)} %bitcast.236), calls=%async_computation.4 | async-start | bytes 2097152 | tf_op jit(solution)/shard_map/all_to_all | solution.py:1555
  1226.8 57.2 %collective-permute-start.3 = (bf16[2,144,2048]{2,1,0:T(8,128)(2,1)}, bf16[2,144,2048]{2,1,0:T(8,128)(2,1)}, u32[]{:S(2)}, u32[]{:S(2)}) collective-permute-start(bf16[2,144,2048]{2,1,0:T(8,128)(2,1)} %fusion.16), channel_id=1, source_target_pairs={{0,4},{4,0},{8,12},{12,8},{16,20},{20,16},{24,28},{28,24},{1,5},{5... | collective-permute-start | bytes 3538952 | tf_op jit(solution)/shard_map/ppermute | solution.py:414
  1248.9 30.2 %all-to-all-start.1 = ((bf16[8,512,256]{2,1,0:T(8,128)(2,1)}), bf16[8,512,256]{2,1,0:T(8,128)(2,1)S(1)}, u32[]{:S(2)}, u32[]{:S(2)}) async-start(bf16[8,512,256]{2,1,0:T(8,128)(2,1)} %bitcast.221), calls=%async_computation.2 | async-start | bytes 4194304 | tf_op jit(solution)/shard_map/all_to_all | solution.py:1555
  1256.1 31.6 %collective-permute-start.7 = (bf16[2,144,2048]{2,1,0:T(8,128)(2,1)}, bf16[2,144,2048]{2,1,0:T(8,128)(2,1)}, u32[]{:S(2)}, u32[]{:S(2)}) collective-permute-start(bf16[2,144,2048]{2,1,0:T(8,128)(2,1)} %fusion.12), channel_id=1, source_target_pairs={{0,4},{4,0},{8,12},{12,8},{16,20},{20,16},{24,28},{28,24},{1,5},{5... | collective-permute-start | bytes 3538952 | tf_op jit(solution)/shard_map/ppermute | solution.py:414
  1256.5 8.3 collective-permute-start.14
  1258.1 11.5 collective-permute-start.13
  1258.1 11.5 collective-permute-start.12
  1294.3 4.5 collective-permute-start.19
  (49 other events, 263.0 us)
Sparse Core Ops, SparseCore 0:
  684.9 74.5 reduce-scatter.4
  762.1 144.9 reduce-scatter.2

commit v4 on v3

--- a/solution.py
+++ b/solution.py
@@ -728,6 +728,21 @@
 HBM, VMEM, SMEM = pl.ANY, pltpu.VMEM, pltpu.SMEM
 
 
+def move_rows(source, target):
+    @pl.loop(0, source.shape[0] // STRIPE)
+    def _(step):
+        span = pl.ds(step * STRIPE, STRIPE)
+        target[span] = source[span]
+
+
+def half_rows(index, rows):
+    return pl.ds(pl.multiple_of(index * rows, STRIPE), rows)
+
+
+def columns_of(index, columns):
+    return pl.ds(pl.multiple_of(index * columns, columns), columns)
+
+
 def at_step(step, actions):
     for when, action in actions.items():
         pl.when(step == when)(action)
@@ -1317,13 +1332,14 @@
         )
         late_branch, back_parts, outs_in = refs[9], refs[10:12], (refs[12:14], refs[14:16])
         middle_ref, own_grad, inputs_ref, late_grad, gain_one, gain_two = refs[16:22]
-        head_grads, early_branch, outputs, input_grad = refs[22:24], refs[24], refs[25], refs[26]
+        head_grads, early_branch, output_groups, input_grad = refs[22:24], refs[24], refs[25], refs[26]
         gain_sums = refs[27]
         parts = (refs[28:30], refs[30:32])
         landings = [refs[32 + 3 * place : 35 + 3 * place] for place in range(5)]
         stage, early_grad, own_branch, keys, values = refs[47:51], refs[51], refs[52], refs[53], refs[54]
-        sums, late_sums, wires = refs[55:57], refs[57:59], Wires(*refs[59:])
-        meet(SIDES)
+        sums, late_sums, outputs, wires = refs[55:57], refs[57:59], refs[59], Wires(*refs[60:])
+        plane = lax.axis_index("fsdp")
+        meet(SIDES + PLANES)
         gain_sums[...] = jnp.zeros(gain_sums.shape, jnp.float32)
 
         def middle_done(chunk, span, total):
@@ -1378,34 +1394,54 @@
 
             return run
 
+        back_to_planes = [
+            Remote(wires, outputs.at[flip(plane, mask)], output_groups.at[plane], 0, mask)
+            for mask in range(1, CHUNKS)
+        ]
+
+        def send_back():
+            for copy in back_to_planes:
+                copy.start()
+            wires.load([(outputs.at[plane], output_groups.at[plane])])
+
         middle_sum.first()
         output_sums[1].first()
+        output_sums[0].first()
         back_through(
             1,
             late_branch,
-            {1: middle_sum.second, 5: middle_sum.third, 7: both(middle_sum.last, move.first)},
-        )
-        move.second()
+            {
+                1: middle_sum.second,
+                4: middle_sum.third,
+                6: both(middle_sum.last, move.first),
+                7: move.second,
+            },
+        )
         input_sums[1].first()
         output_sums[1].second()
         move.third()
         move.last()
-        output_sums[0].first()
         back_through(
             0,
             early_branch,
             {
-                1: both(output_sums[1].third, input_sums[1].second),
-                4: both(output_sums[1].last, input_sums[1].third),
-                6: both(input_sums[1].last, output_sums[0].second),
+                0: output_sums[1].third,
+                2: both(output_sums[1].last, output_sums[0].second),
+                4: output_sums[0].third,
+                6: both(output_sums[0].last, send_back),
+                7: input_sums[1].second,
             },
         )
         input_sums[0].first()
-        output_sums[0].third()
+        input_sums[1].third()
         input_sums[0].second()
-        output_sums[0].last()
+        input_sums[1].last()
         input_sums[0].third()
         input_sums[0].last()
+        for copy in back_to_planes:
+            copy.arrived()
+        for copy in back_to_planes:
+            copy.left()
 
     outs = call(
         kernel,
@@ -1419,7 +1455,7 @@
         + [(gains[0], VMEM), (gains[1], VMEM)],
         [(bf16(2, CHIPS, tokens, 3 * HEAD), HBM)] * 2
         + [(bf16(2, CHIPS, tokens, width), HBM)]
-        + [(bf16(CHUNKS, rows, width), VMEM)] * 2
+        + [(bf16(CHUNKS, rows, width), HBM), (bf16(CHUNKS, rows, width), VMEM)]
         + [(f32(2, STRIPE, width), VMEM)]
         + [(shape, HBM) for shape in partial_shapes(rows, width)] * 2
         + [(shape, HBM) for shape in landing_shapes(rows, width)] * 5,
@@ -1428,10 +1464,218 @@
         + [pltpu.VMEM((CHUNKS * tokens, HEAD), jnp.bfloat16)] * 2
         + [pltpu.VMEM((CHIPS, 2 * tokens, HEAD), jnp.float32)] * 2
         + [pltpu.VMEM((2 * tokens, HEAD), jnp.float32)] * 2
-        + wire_shapes(50),
+        + [pltpu.VMEM((CHUNKS, rows, width), jnp.bfloat16)]
+        + wire_shapes(60),
         63,
     )
     return outs[:2], outs[2], outs[3], outs[4], outs[5]
+
+
+def finish(head_sum, output_sum, unit_sum, down_sum, output_groups, input_grad, gain_sums):
+    devices, planes, sub_rows, _ = head_sum.shape
+    strips = unit_sum.shape[0]
+    _, down_rows, columns = down_sum.shape
+    _, rows, width = input_grad.shape
+    in_rows = width // devices
+
+    def kernel(*refs):
+        heads, outs_in, units_in, downs_in, output_groups_ref, grads_ref, gains = refs[:7]
+        outputs, input_out, head_out, output_out, units, downs, gain_out, square_out = refs[7:15]
+        grad_groups, combined, other_half, mine, gathered = refs[15:20]
+        head_landing, output_landing, head_two, output_two = refs[20:24]
+        gain_parts, square_parts, wires = refs[24], refs[25], Wires(*refs[26:])
+        place, plane = lax.axis_index("dp"), lax.axis_index("fsdp")
+        core = lax.rem(place, 2)
+
+        def part(mask):
+            return combined.at[:, flip(plane, mask)], outs_in.at[:, columns_of(flip(plane, mask), columns)]
+
+        def both(sources, targets, mask):
+            return [Remote(wires, source, target, 0, mask) for source, target in zip(sources, targets)]
+
+        landing = [(head_landing.at[index], output_landing.at[index]) for index in range(3)]
+        third = both(part(3), landing[0], 1)
+        first = both(part(1), landing[1], 1)
+        second = both((head_two, output_two), landing[2], 2)
+        core_half = Remote(wires, heads.at[:, :, :, columns_of(2 - core, HEAD)], other_half, CORE)
+        rows_back = [
+            Remote(wires, grads_ref.at[flip(plane, mask)], grad_groups.at[plane], 0, mask)
+            for mask in range(1, CHUNKS)
+        ]
+        spread, heads_back = [], []
+        for mask in range(1, devices):
+            other = flip(place, mask)
+            spread.append(Remote(wires, units_in.at[:, columns_of(other, in_rows)], units.at[place], mask))
+            spread.append(Remote(wires, downs_in.at[other], downs.at[place], mask))
+            heads_back.append(Remote(wires, mine.at[other], gathered.at[place], mask))
+        heads_over = [
+            Remote(wires, gathered.at[pl.ds(2 * flip(plane, mask), 2)], head_out.at[plane], 0, mask)
+            for mask in range(1, CHUNKS)
+        ]
+
+        def to_owners(groups, target):
+            copies = []
+            for group in range(2):
+                copies.append(
+                    Remote(
+                        wires,
+                        groups.at[2 * (1 - core) + group],
+                        target.at[group, half_rows(core, rows)],
+                        CORE,
+                    )
+                )
+            return copies
+
+        outputs_in = to_owners(output_groups_ref, outputs)
+        grads_in = to_owners(grad_groups, input_out)
+
+        def sum_over(parts_ref):
+            steps = [(mask, 0) for mask in (CORE, SIDE_A, SIDE_B)] + [(0, 1), (0, 2)]
+            copies = [
+                Remote(wires, parts_ref.at[2 * index], parts_ref.at[2 * index + 1], mask, over)
+                for index, (mask, over) in enumerate(steps)
+            ]
+
+            def step(index):
+                copies[index].arrived()
+                copies[index].left()
+                parts_ref[2 * index + 2] = parts_ref[2 * index] + parts_ref[2 * index + 1]
+                if index + 1 < len(copies):
+                    copies[index + 1].start()
+
+            return copies[0].start, step, len(steps)
+
+        gains_start, gains_step, count = sum_over(gain_parts)
+        squares_start, squares_step, _ = sum_over(square_parts)
+
+        gain_parts[0] = jnp.concatenate(
+            [jnp.sum(gains[index], axis=0, keepdims=True) for index in range(2)]
+            + [jnp.zeros((6, width), jnp.float32)]
+        )
+        meet(PLANE + PLANES)
+        core_half.start()
+        for copy in spread + outputs_in:
+            copy.start()
+        gains_start()
+        for index in range(planes):
+            combined[:, index, :, :HEAD] = heads[:, index, :, :HEAD]
+        core_half.arrived()
+        for index in range(2):
+
+            @pl.when(core == index)
+            def _():
+                kept = (1 + index) * HEAD
+                for block in range(planes):
+                    total = heads[:, block, :, kept : kept + HEAD].astype(jnp.float32) + other_half[
+                        :, block
+                    ].astype(jnp.float32)
+                    combined[:, block, :, HEAD:] = total.astype(jnp.bfloat16)
+
+        for copy in third + first:
+            copy.start()
+        units[place] = units_in[:, columns_of(place, in_rows)]
+        downs[place] = downs_in[place]
+        for group in range(2):
+            move_rows(
+                output_groups_ref.at[2 * core + group], outputs.at[group, half_rows(core, rows)]
+            )
+        move_rows(grads_ref.at[plane], grad_groups.at[plane])
+        for copy in third:
+            copy.arrived()
+        head_two[...] = (
+            combined[:, flip(plane, 2)].astype(jnp.float32) + head_landing[0].astype(jnp.float32)
+        ).astype(jnp.bfloat16)
+        output_two[...] = (
+            outs_in[:, columns_of(flip(plane, 2), columns)].astype(jnp.float32)
+            + output_landing[0].astype(jnp.float32)
+        ).astype(jnp.bfloat16)
+        for copy in second:
+            copy.start()
+        gains_step(0)
+        for copy in rows_back:
+            copy.start()
+        for index in range(1, count):
+            gains_step(index)
+        for copy in first + second:
+            copy.arrived()
+        total = combined[:, plane].astype(jnp.float32)
+        for index in (1, 2):
+            total += head_landing[index].astype(jnp.float32)
+        mine[...] = total.astype(jnp.bfloat16)
+        for copy in heads_back:
+            copy.start()
+        gathered[place] = mine[place]
+        total = outs_in[:, columns_of(plane, columns)].astype(jnp.float32)
+        for index in (1, 2):
+            total += output_landing[index].astype(jnp.float32)
+        output_out[...] = total
+        square = jnp.sum(total * total)
+        for copy in heads_back:
+            copy.arrived()
+        for copy in heads_over:
+            copy.start()
+        head_out[plane] = gathered[pl.ds(2 * plane, 2)]
+        for copy in spread:
+            copy.arrived()
+        for index in range(devices):
+            for ref in (units, downs):
+                values = ref[index].astype(jnp.float32)
+                square += jnp.sum(values * values)
+        for copy in heads_over:
+            copy.arrived()
+        for index in range(planes):
+            values = head_out[index].astype(jnp.float32)
+            square += jnp.sum(values * values)
+        square_parts[0] = jnp.full(square_parts.shape[1:], square, jnp.float32)
+        squares_start()
+        for index in range(count):
+            squares_step(index)
+        gain_out[...] = gain_parts[2 * count]
+        square_out[...] = square_parts[2 * count]
+        for copy in rows_back:
+            copy.arrived()
+        for copy in grads_in:
+            copy.start()
+        for group in range(2):
+            move_rows(grad_groups.at[2 * core + group], input_out.at[group, half_rows(core, rows)])
+        for copy in outputs_in + grads_in:
+            copy.arrived()
+        for copy in (
+            third + first + second + [core_half] + rows_back + spread + heads_back + heads_over
+            + outputs_in + grads_in
+        ):
+            copy.left()
+
+    own = bf16(2, 2 * rows, width)
+    return call(
+        kernel,
+        5,
+        [
+            (array, VMEM)
+            for array in (
+                head_sum, output_sum, unit_sum, down_sum, output_groups, input_grad, gain_sums
+            )
+        ],
+        [(own, VMEM)] * 2
+        + [(bf16(planes, 2, sub_rows, columns), VMEM), (f32(HEAD, columns), VMEM)]
+        + [(bf16(devices, strips, in_rows), VMEM), (bf16(devices, down_rows, columns), VMEM)]
+        + [(f32(8, width), VMEM), (f32(8, 128), VMEM)],
+        [
+            pltpu.VMEM((CHUNKS, rows, width), jnp.bfloat16),
+            pltpu.VMEM((devices, planes, sub_rows, columns), jnp.bfloat16),
+            pltpu.VMEM((devices, planes, sub_rows, HEAD), jnp.bfloat16),
+            pltpu.VMEM((devices, sub_rows, columns), jnp.bfloat16),
+            pltpu.VMEM((devices, sub_rows, columns), jnp.bfloat16),
+            pltpu.VMEM((3, devices, sub_rows, columns), jnp.bfloat16),
+            pltpu.VMEM((3, HEAD, columns), jnp.bfloat16),
+            pltpu.VMEM((devices, sub_rows, columns), jnp.bfloat16),
+            pltpu.VMEM((HEAD, columns), jnp.bfloat16),
+            pltpu.VMEM((11, 8, width), jnp.float32),
+            pltpu.VMEM((11, 8, 128), jnp.float32),
+        ]
+        + wire_shapes(70),
+        62,
+    )
 
 
 def unit_weight_grads(unit_grads, rows_in):
@@ -1668,7 +1912,7 @@
     down_sum = reduce(jnp.add, [token_dot(hidden[pair], grads_all[pair]) for pair in (1, 0)]).astype(low)
     down_sum = down_sum.reshape(-1, planes, down_columns).transpose(1, 0, 2)
     down_sum = lax.psum_scatter(down_sum, "fsdp", scatter_dimension=0, tiled=False)
-    head_grads, branch_early, own_outputs, own_input_grad, gain_sums = attend_back(
+    head_grads, branch_early, output_groups, own_input_grad, gain_sums = attend_back(
         states,
         lengths,
         (place_q, place_k),
@@ -1685,37 +1929,28 @@
         middle_grad,
         (gain_one, gain_two),
     )
-    outputs = from_planes([own_outputs[chunk] for chunk in range(CHUNKS)], core, plane)
-    input_grad = from_planes([own_input_grad[chunk] for chunk in range(CHUNKS)], core, plane)
-    attention_sum = jnp.sum(gain_sums[0], axis=0)
-    feedforward_sum = jnp.sum(gain_sums[1] + gain_sum, axis=0)
-
-    strips = runs * strip
-    unit_sum = unit_sum.reshape(2 * strips, devices, in_rows).swapaxes(0, 1)
-    unit_sum = exchange(unit_sum, "dp").reshape(devices, 2, runs, strip, in_rows)
-    gate_up_owned = unit_sum.transpose(1, 4, 2, 0, 3).reshape(2, in_rows, runs * devices * strip)
-    down_owned = exchange(down_sum.reshape(devices, strip, down_columns), "dp")
-    down_owned = down_owned.reshape(devices * strip, down_columns)
+
     head_sum = reduce(
         jnp.add, [token_dot(rows_all[pair], head_grads[pair]) for pair in (1, 0)]
     ).astype(low)
     branches = (branch_early, branch_late)
     output_sum = reduce(jnp.add, [token_dot(mixed[pair], branches[pair]) for pair in (1, 0)]).astype(low)
-    given = jnp.where(core == 0, head_sum[:, 2 * HEAD :], head_sum[:, HEAD : 2 * HEAD])
-    kept = jnp.where(core == 0, head_sum[:, HEAD : 2 * HEAD], head_sum[:, 2 * HEAD :])
-    kv_sum = (kept.astype(jnp.float32) + across(given, CORE).astype(jnp.float32)).astype(low)
-    head_sum = jnp.concatenate([head_sum[:, :HEAD], kv_sum], axis=1)
-    head_sum = head_sum.reshape(devices, planes, sub_rows, 2 * HEAD).transpose(1, 0, 2, 3)
-    head_sum = head_sum.reshape(planes, spread, 2 * HEAD)
-    output_sum = output_sum.reshape(HEAD, planes, 2 * HEAD).transpose(1, 0, 2)
-    attention_parts = jnp.concatenate([head_sum, output_sum], axis=1)
-    attention_grad = sum_planes([pick(attention_parts, blocks[shard]) for shard in range(CHUNKS)])
-    output_owned = attention_grad[spread:]
-    block = exchange(attention_grad[:spread].astype(low).reshape(devices, sub_rows, 2 * HEAD), "dp")
-    block = block.reshape(planes, 2, sub_rows, 2 * HEAD).transpose(0, 2, 1, 3)
-    block = jnp.stack(trade_planes(block, plane)).reshape(in_rows, 2, 2 * HEAD)
+    outputs, input_grad, block, output_owned, units_owned, downs_owned, gain_totals, squares = finish(
+        head_sum.reshape(devices, planes, sub_rows, 3 * HEAD),
+        output_sum,
+        unit_sum,
+        down_sum.reshape(devices, strip, down_columns),
+        output_groups,
+        own_input_grad,
+        jnp.stack([gain_sums[0], gain_sums[1] + gain_sum]),
+    )
+    block = block.swapaxes(1, 2).reshape(in_rows, 2, 2 * HEAD)
     query_owned = block[:, :, :HEAD].reshape(in_rows, 2 * HEAD)
     key_owned, value_owned = block[:, 0, HEAD:], block[:, 1, HEAD:]
+    gate_up_owned = units_owned.reshape(devices, 2, runs, strip, in_rows).transpose(1, 4, 2, 0, 3)
+    gate_up_owned = gate_up_owned.reshape(2, in_rows, runs * devices * strip)
+    down_owned = downs_owned.reshape(devices * strip, down_columns)
+
     owner_grads = [
         owned.astype(jnp.float32)
         for owned in (
@@ -1728,9 +1963,8 @@
             down_owned,
         )
     ]
-    local_square = reduce(jnp.add, [jnp.sum(owned * owned) for owned in owner_grads])
-    attention_total, feedforward_total = sum_all(jnp.stack([attention_sum, feedforward_sum]))
-    square_total = sum_all(jnp.full((8, 128), local_square))[0, 0]
+    attention_total, feedforward_total = gain_totals[0], gain_totals[1]
+    square_total = squares[0, 0]
     square_sum = (
         square_total
         + jnp.sum(attention_total * attention_total)

time: 1350 us -> 1290 us (0.956)
  Pallas kernels: 967 us -> 1130 us
  waiting for transfers between devices: 109 us -> 0.04 us
  starting transfers between devices: 55.3 us -> 0.08 us
  other arithmetic: 69.1 us -> 37.5 us
    pallas_call x4 -> x5, Pallas kernels: 905 us -> 1070 us  [call(): pl.pallas_call(kernel, in_specs=[pl.BlockSpec(memory_space=place) for _,...]
    ppermute x25 -> x0, waiting for transfers between devices: 106 us -> none  [the longest x16 102 us: along(): lax.ppermute(value, 'fsdp', [(place, place ^ mask) for place in range(cou...]
    ppermute x25 -> x0, starting transfers between devices: 44.4 us -> none  [the longest x16 39.9 us: along(): lax.ppermute(value, 'fsdp', [(place, place ^ mask) for place in range(cou...]
  transfers between devices with their start and end apart: 30 -> 2, of which waited for: 14 -> 0; matrix products, arithmetic and copies ran while one was open for 6% -> 3% of each run, Pallas kernels for 26% -> 27%
where the time goes in v4:
time: 1290 us; the launch traced here: 1280 us
  Pallas kernels  1130 us (88%)
  matrix products  60.7 us (5%)
  other arithmetic  37.5 us (3%)
  local copies, waits for them, and re-layouts  35.1 us (3%)
  between operations  18 us (1%)
    pallas_call x5, Pallas kernels, call(): pl.pallas_call(kernel, in_specs=[pl.BlockSpec(memory_space=place) for _,...  1070 us
    pallas_call x1, Pallas kernels, unit_weight_grads(): pl.pallas_call(kernel, grid=(shards, 4), in_specs=specs, out_specs=pl.Blo...  62.3 us
    dot_general x6, matrix products, token_dot(): lax.dot_general(left.reshape(-1, left.shape[-1]), right.reshape(-1, right...  60.7 us
  transfers between devices with their start and end apart: 2, of which 0 were waited for; matrix products, arithmetic and copies ran while one was open for 3% of the time, Pallas kernels for 27%

profile of v4, /device:TPU:0, one launch (start us, length us, event | category | flops | bytes accessed | tf_op | source)
XLA Modules:
  0.0 1281.1 jit_solution(4089262238537944770)
XLA Ops:
  17.4 4.3 maximum_bitcast_fusion
  21.7 4.2 reshape.251.refs_4_
  27.0 3.2 multiply_sine_fusion
  31.1 184.4 %shard_map.364 = (bf16[4,144,2048]{2,1,0:T(8,128)(2,1)}, bf16[4,144,2048]{2,1,0:T(8,128)(2,1)}, bf16[2,4,288,2048]{3,2,1,0:T(8,128)(2,1)}, bf16[2,4,288,2048]{3,...) custom-call(bf16[2,288,2048]{2,1,0:T(8,128)(2,1)} %refs_0_.1, ...), custom_call_target="tpu_custom_call" | custom-call | tf_op jit(solution)/shard_map/pallas_call | solution.py:716
  216.8 215.0 %shard_map.365 = (bf16[2,4,288,768]{3,2,1,0:T(8,128)(2,1)}, bf16[2,4,288,768]{3,2,1,0:T(8,128)(2,1)}, bf16[2,4,288,256]{3,2,1,0:T(8,128)(2,1)}, bf16[2,4,288,256...) custom-call(bf16[2,4,288,2048]{3,2,1,0:T(8,128)(2,1)} %get-tuple-ele, ...), custom_call_target="tpu_custom_call" | custom-call | tf_op jit(solution)/shard_map/pallas_call | solution.py:716
  431.8 221.6 %shard_map.366 = (bf16[2,4,288,2048]{3,2,1,0:T(8,128)(2,1)}, bf16[2,4,288,2048]{3,2,1,0:T(8,128)(2,1)}, bf16[2,4,288,1024]{3,2,1,0:T(8,128)(2,1)}, bf16[2,4,288,...) custom-call(bf16[2,144,2048]{2,1,0:T(8,128)(2,1)} %get-tuple-element, ...), custom_call_target="tpu_custom_call" | custom-call | tf_op jit(solution)/shard_map/pallas_call | solution.py:716
  653.5 16.8 %fusion.9 = f32[1024,2048,1,1]{1,0,3,2:T(8,128)} fusion(bf16[2,4,288,1024]{3,2,1,0:T(8,128)(2,1)} %get-tuple-element.110, bf16[2,4,288,2048]{3,2,1,0:T(8,128)(2,1)} %get-tuple-element.91.refs_2_), kind=kOutput, calls=%fused_computation.69 | convolution fusion | flops 9663676416 | bytes 22544384 | tf_op jit(solution)/shard_map/dot_general | solution.py:1790
  670.2 12.3 fusion
  684.9 62.3 %shard_map.368 = bf16[4,512,2048]{2,1,0:T(8,128)(2,1)} custom-call(bf16[4,2,4,288,512]{4,3,2,1,0:T(8,128)(2,1)} %get-tuple-element.107.late_units, bf16[2,4,288,2048]{3,2,1,0:T(8,128)(2,1)} %get-tuple-element.90.refs_1_.late_rows, bf16[4,2,4,288,512]{4,3,2,1,0:T(8,128)(2,1)} %get-tuple-element.108.early_units, ...), custom_call_target="tpu_custom_call" | custom-call | tf_op jit(solution)/shard_map/pallas_call | solution.py:1719
  747.2 289.1 %shard_map.367 = (bf16[2,4,288,768]{3,2,1,0:T(8,128)(2,1)}, bf16[2,4,288,768]{3,2,1,0:T(8,128)(2,1)}, bf16[2,4,288,2048]{3,2,1,0:T(8,128)(2,1)}, bf16[4,144,2048...) custom-call(bf16[2,4,288,768]{3,2,1,0:T(8,128)(2,1)} %get-tuple-elem, ...), custom_call_target="tpu_custom_call" | custom-call | tf_op jit(solution)/shard_map/pallas_call | solution.py:716
  1038.9 6.1 convolution_bitcast_fusion
  1045.0 7.4 fusion.3.refs_1_
  1052.5 8.4 fusion.8
  1060.9 9.7 fusion.1
  1070.7 157.3 %shard_map.369 = (bf16[2,288,2048]{2,1,0:T(8,128)(2,1)}, bf16[2,288,2048]{2,1,0:T(8,128)(2,1)}, bf16[4,2,64,512]{3,2,1,0:T(8,128)(2,1)}, f32[256,512]{1,0:T(8,12...) custom-call(bf16[8,4,64,768]{3,2,1,0:T(8,128)(2,1)} %bitcast.118, ...), custom_call_target="tpu_custom_call" | custom-call | tf_op jit(solution)/shard_map/pallas_call | solution.py:716
  1236.6 2.5 convert_multiply_fusion.1
  1239.2 3.0 copy.57
  1242.2 2.7 mul.240
  1244.9 3.0 copy.56
  1248.0 2.8 mul.237
  1255.6 2.8 multiply_subtract_fusion.3
  1258.5 2.9 multiply_subtract_fusion.2
  1262.8 2.8 multiply_subtract_fusion.1
  1266.2 2.8 multiply_subtract_fusion
  (127 shorter events, 35.5 us)
Async XLA Ops:
  7.2 6.4 copy-start.16
  7.2 7.2 copy-start
  7.2 1063.5 %reduce-scatter.5.cloned.1.call-start = ((), (), s32[]{:S(2)}) async-start(), calls=%async_computation.3 | async-start | bytes 5242880 | tf_op jit(solution)/shard_map/reduce_scatter | solution.py:1914
  21.6 4.3 copy-start.4
  653.4 16.8 %copy-start.27 = (bf16[2,4,288,2048]{3,2,1,0:T(8,128)(2,1)S(1)}, bf16[2,4,288,2048]{3,2,1,0:T(8,128)(2,1)}, u32[]{:S(2)}) copy-start(bf16[2,4,288,2048]{3,2,1,0:T(8,128)(2,1)} %get-tuple-element.112) | copy-start | bytes 28311556
  653.5 16.8 %copy-start.28 = (bf16[2,4,288,1024]{3,2,1,0:T(8,128)(2,1)S(1)}, bf16[2,4,288,1024]{3,2,1,0:T(8,128)(2,1)}, u32[]{:S(2)}) copy-start(bf16[2,4,288,1024]{3,2,1,0:T(8,128)(2,1)} %get-tuple-element.111) | copy-start | bytes 14155780
  684.8 385.9 %reduce-scatter.3.cloned.1.call-start = ((), (), s32[]{:S(2)}) async-start(), calls=%async_computation.2 | async-start | bytes 10485760 | tf_op jit(solution)/shard_map/reduce_scatter | solution.py:1911
  747.1 290.0 %copy-start.22 = (f32[16,2048]{1,0:T(8,128)S(1)}, f32[16,2048]{1,0:T(8,128)}, u32[]{:S(2)}) copy-start(f32[16,2048]{1,0:T(8,128)} %get-tuple-element.116) | copy-start | bytes 393220
  1038.8 6.1 copy-start.18
  1038.8 13.6 %slice-start.3 = ((s8[9437184]{0:T(1024)(128)(4,1)}), s8[4194304]{0:T(1024)(128)(4,1)S(1)}, s32[]{:S(2)}) async-start(s8[9437184]{0:T(1024)(128)(4,1)} %bitcast.112), calls=%async_computation.7 | async-start | bytes 8388608
  1038.9 13.6 %slice-start.4 = ((s8[9437184]{0:T(1024)(128)(4,1)}), s8[4194304]{0:T(1024)(128)(4,1)S(1)}, s32[]{:S(2)}) async-start(s8[9437184]{0:T(1024)(128)(4,1)} %bitcast.112), calls=%async_computation.8 | async-start | bytes 8388608
  1045.0 7.5 slice-start.5
  1045.0 7.5 copy-start.30
  1045.0 15.9 %slice-start = ((s8[9437184]{0:T(1024)(128)(4,1)}), s8[4194304]{0:T(1024)(128)(4,1)S(1)}, s32[]{:S(2)}) async-start(s8[9437184]{0:T(1024)(128)(4,1)} %bitcast.110), calls=%async_computation.4 | async-start | bytes 8388608
  1052.5 8.4 slice-start.1
  1052.5 8.4 slice-start.2
  1052.5 8.4 copy-start.29
  1248.0 4.0 copy-start.19
  1248.0 6.5 copy-start.14
  1250.8 3.7 copy-start.21
  1252.0 6.4 copy-start.10
  1254.4 4.0 copy-start.1
  1254.4 4.0 copy-start.7
  1258.5 4.4 copy-start.11
  (15 other events, 40.9 us)
Sparse Core Ops, SparseCore 0:
  684.9 74.6 reduce-scatter.4
  762.1 144.9 reduce-scatter.2

commit v5 on v4

--- a/solution.py
+++ b/solution.py
@@ -1,3 +1,4 @@
+import functools
 from functools import reduce
 import math
 
@@ -1471,19 +1472,49 @@
     return outs[:2], outs[2], outs[3], outs[4], outs[5]
 
 
-def finish(head_sum, output_sum, unit_sum, down_sum, output_groups, input_grad, gain_sums):
-    devices, planes, sub_rows, _ = head_sum.shape
+def weight_grad_phase(rows_in, grads, total, fresh, actions):
+    _, chips, tokens, width = rows_in.shape
+    columns = grads.shape[3]
+
+    def body(rows_ref, grads_ref):
+        chunk, step = pl.program_id(0), pl.program_id(1)
+        at_step(2 * chunk + step, actions)
+        term = dot_tn(rows_ref[0].reshape(2 * tokens, width), grads_ref[0].reshape(2 * tokens, columns))
+        if fresh:
+
+            @pl.when(chunk + step == 0)
+            def _():
+                total[...] = jnp.zeros(total.shape, jnp.float32)
+
+        total[...] += term
+
+    here = lambda chunk, step: (chunk, step, 0, 0)
+    pltpu.emit_pipeline(
+        body,
+        grid=(2, chips // 2),
+        in_specs=[
+            pl.BlockSpec((1, 2, tokens, width), here),
+            pl.BlockSpec((1, 2, tokens, columns), here),
+        ],
+    )(rows_in, grads)
+
+
+def finish(head_terms, output_terms, unit_sum, down_sum, output_groups, input_grad, gain_sums):
+    devices, planes = lax.axis_size("dp"), lax.axis_size("fsdp")
     strips = unit_sum.shape[0]
     _, down_rows, columns = down_sum.shape
     _, rows, width = input_grad.shape
     in_rows = width // devices
+    sub_rows = in_rows // planes
 
     def kernel(*refs):
-        heads, outs_in, units_in, downs_in, output_groups_ref, grads_ref, gains = refs[:7]
-        outputs, input_out, head_out, output_out, units, downs, gain_out, square_out = refs[7:15]
-        grad_groups, combined, other_half, mine, gathered = refs[15:20]
-        head_landing, output_landing, head_two, output_two = refs[20:24]
-        gain_parts, square_parts, wires = refs[24], refs[25], Wires(*refs[26:])
+        head_refs, output_refs, refs = refs[:4], refs[4:8], refs[8:]
+        units_in, downs_in, output_groups_ref, grads_ref, gains = refs[:5]
+        outputs, input_out, head_out, output_out, gate_up, downs, gain_out, square_out = refs[5:13]
+        grad_groups, combined, other_half, mine, gathered = refs[13:18]
+        head_landing, output_landing, head_two, output_two = refs[18:22]
+        gain_parts, square_parts, units = refs[22:25]
+        head_total, output_total, given, outs_in, wires = *refs[25:29], Wires(*refs[29:])
         place, plane = lax.axis_index("dp"), lax.axis_index("fsdp")
         core = lax.rem(place, 2)
 
@@ -1497,7 +1528,7 @@
         third = both(part(3), landing[0], 1)
         first = both(part(1), landing[1], 1)
         second = both((head_two, output_two), landing[2], 2)
-        core_half = Remote(wires, heads.at[:, :, :, columns_of(2 - core, HEAD)], other_half, CORE)
+        core_half = Remote(wires, given, other_half, CORE)
         rows_back = [
             Remote(wires, grads_ref.at[flip(plane, mask)], grad_groups.at[plane], 0, mask)
             for mask in range(1, CHUNKS)
@@ -1553,26 +1584,9 @@
             + [jnp.zeros((6, width), jnp.float32)]
         )
         meet(PLANE + PLANES)
-        core_half.start()
-        for copy in spread + outputs_in:
+        for copy in rows_back + spread + outputs_in:
             copy.start()
         gains_start()
-        for index in range(planes):
-            combined[:, index, :, :HEAD] = heads[:, index, :, :HEAD]
-        core_half.arrived()
-        for index in range(2):
-
-            @pl.when(core == index)
-            def _():
-                kept = (1 + index) * HEAD
-                for block in range(planes):
-                    total = heads[:, block, :, kept : kept + HEAD].astype(jnp.float32) + other_half[
-                        :, block
-                    ].astype(jnp.float32)
-                    combined[:, block, :, HEAD:] = total.astype(jnp.bfloat16)
-
-        for copy in third + first:
-            copy.start()
         units[place] = units_in[:, columns_of(place, in_rows)]
         downs[place] = downs_in[place]
         for group in range(2):
@@ -1580,22 +1594,76 @@
                 output_groups_ref.at[2 * core + group], outputs.at[group, half_rows(core, rows)]
             )
         move_rows(grads_ref.at[plane], grad_groups.at[plane])
-        for copy in third:
-            copy.arrived()
+        weight_grad_phase(head_refs[0], head_refs[1], head_total, True, {3: lambda: gains_step(0)})
+        weight_grad_phase(
+            head_refs[2], head_refs[3], head_total, False, {1: lambda: gains_step(1), 3: lambda: gains_step(2)}
+        )
+
+        def split(index):
+            kept, sent = (1 + index) * HEAD, (2 - index) * HEAD
+
+            @pl.loop(0, devices)
+            def _(block):
+                span = pl.ds(pl.multiple_of(block * in_rows, in_rows), in_rows)
+                shape = (planes, sub_rows, HEAD)
+                given[block] = head_total[span, sent : sent + HEAD].astype(jnp.bfloat16).reshape(shape)
+                combined[block, :, :, :HEAD] = head_total[span, :HEAD].astype(jnp.bfloat16).reshape(shape)
+
+        for index in range(2):
+            pl.when(core == index)(functools.partial(split, index))
+        core_half.start()
+        weight_grad_phase(output_refs[0], output_refs[1], output_total, True, {})
+        core_half.arrived()
+
+        def join(index):
+            kept = (1 + index) * HEAD
+
+            @pl.loop(0, devices)
+            def _(block):
+                span = pl.ds(pl.multiple_of(block * in_rows, in_rows), in_rows)
+                total = head_total[span, kept : kept + HEAD].reshape(planes, sub_rows, HEAD)
+                total = total + other_half[block].astype(jnp.float32)
+                combined[block, :, :, HEAD:] = total.astype(jnp.bfloat16)
+
+        for index in range(2):
+            pl.when(core == index)(functools.partial(join, index))
+        third[0].start()
+        weight_grad_phase(output_refs[2], output_refs[3], output_total, False, {})
+        outs_in[...] = output_total[...].astype(jnp.bfloat16)
+        third[1].start()
+        third[0].arrived()
         head_two[...] = (
             combined[:, flip(plane, 2)].astype(jnp.float32) + head_landing[0].astype(jnp.float32)
         ).astype(jnp.bfloat16)
+        second[0].start()
+        third[1].arrived()
         output_two[...] = (
             outs_in[:, columns_of(flip(plane, 2), columns)].astype(jnp.float32)
             + output_landing[0].astype(jnp.float32)
         ).astype(jnp.bfloat16)
-        for copy in second:
+        second[1].start()
+        for copy in first:
             copy.start()
-        gains_step(0)
+        for index in range(3, count):
+            gains_step(index)
         for copy in rows_back:
+            copy.arrived()
+        for copy in grads_in:
             copy.start()
-        for index in range(1, count):
-            gains_step(index)
+        for group in range(2):
+            move_rows(grad_groups.at[2 * core + group], input_out.at[group, half_rows(core, rows)])
+        for copy in spread:
+            copy.arrived()
+        square = jnp.zeros((), jnp.float32)
+        for index in range(devices):
+            values = downs[index].astype(jnp.float32)
+            square += jnp.sum(values * values)
+            for block in range(strips // down_rows):
+                values = units[index, block * down_rows : (block + 1) * down_rows].astype(jnp.float32)
+                square += jnp.sum(values * values)
+                matrix, run = block // 2, block % 2
+                at = (run * devices + index) * down_rows
+                gate_up[matrix, :, at : at + down_rows] = values.T.astype(jnp.bfloat16)
         for copy in first + second:
             copy.arrived()
         total = combined[:, plane].astype(jnp.float32)
@@ -1609,18 +1677,12 @@
         for index in (1, 2):
             total += output_landing[index].astype(jnp.float32)
         output_out[...] = total
-        square = jnp.sum(total * total)
+        square += jnp.sum(total * total)
         for copy in heads_back:
             copy.arrived()
         for copy in heads_over:
             copy.start()
         head_out[plane] = gathered[pl.ds(2 * plane, 2)]
-        for copy in spread:
-            copy.arrived()
-        for index in range(devices):
-            for ref in (units, downs):
-                values = ref[index].astype(jnp.float32)
-                square += jnp.sum(values * values)
         for copy in heads_over:
             copy.arrived()
         for index in range(planes):
@@ -1632,12 +1694,6 @@
             squares_step(index)
         gain_out[...] = gain_parts[2 * count]
         square_out[...] = square_parts[2 * count]
-        for copy in rows_back:
-            copy.arrived()
-        for copy in grads_in:
-            copy.start()
-        for group in range(2):
-            move_rows(grad_groups.at[2 * core + group], input_out.at[group, half_rows(core, rows)])
         for copy in outputs_in + grads_in:
             copy.arrived()
         for copy in (
@@ -1650,15 +1706,11 @@
     return call(
         kernel,
         5,
-        [
-            (array, VMEM)
-            for array in (
-                head_sum, output_sum, unit_sum, down_sum, output_groups, input_grad, gain_sums
-            )
-        ],
+        [(array, HBM) for array in head_terms + output_terms]
+        + [(array, VMEM) for array in (unit_sum, down_sum, output_groups, input_grad, gain_sums)],
         [(own, VMEM)] * 2
         + [(bf16(planes, 2, sub_rows, columns), VMEM), (f32(HEAD, columns), VMEM)]
-        + [(bf16(devices, strips, in_rows), VMEM), (bf16(devices, down_rows, columns), VMEM)]
+        + [(bf16(2, in_rows, devices * strips // 2), VMEM), (bf16(devices, down_rows, columns), VMEM)]
         + [(f32(8, width), VMEM), (f32(8, 128), VMEM)],
         [
             pltpu.VMEM((CHUNKS, rows, width), jnp.bfloat16),
@@ -1672,6 +1724,11 @@
             pltpu.VMEM((HEAD, columns), jnp.bfloat16),
             pltpu.VMEM((11, 8, width), jnp.float32),
             pltpu.VMEM((11, 8, 128), jnp.float32),
+            pltpu.VMEM((devices, strips, in_rows), jnp.bfloat16),
+            pltpu.VMEM((width, 3 * HEAD), jnp.float32),
+            pltpu.VMEM((HEAD, width), jnp.float32),
+            pltpu.VMEM((devices, planes, sub_rows, HEAD), jnp.bfloat16),
+            pltpu.VMEM((HEAD, width), jnp.bfloat16),
         ]
         + wire_shapes(70),
         62,
@@ -1930,14 +1987,9 @@
         (gain_one, gain_two),
     )
 
-    head_sum = reduce(
-        jnp.add, [token_dot(rows_all[pair], head_grads[pair]) for pair in (1, 0)]
-    ).astype(low)
-    branches = (branch_early, branch_late)
-    output_sum = reduce(jnp.add, [token_dot(mixed[pair], branches[pair]) for pair in (1, 0)]).astype(low)
-    outputs, input_grad, block, output_owned, units_owned, downs_owned, gain_totals, squares = finish(
-        head_sum.reshape(devices, planes, sub_rows, 3 * HEAD),
-        output_sum,
+    outputs, input_grad, block, output_owned, gate_up_owned, downs_owned, gain_totals, squares = finish(
+        [rows_all[1], head_grads[1], rows_all[0], head_grads[0]],
+        [mixed[1], branch_late, mixed[0], branch_early],
         unit_sum,
         down_sum.reshape(devices, strip, down_columns),
         output_groups,
@@ -1947,8 +1999,6 @@
     block = block.swapaxes(1, 2).reshape(in_rows, 2, 2 * HEAD)
     query_owned = block[:, :, :HEAD].reshape(in_rows, 2 * HEAD)
     key_owned, value_owned = block[:, 0, HEAD:], block[:, 1, HEAD:]
-    gate_up_owned = units_owned.reshape(devices, 2, runs, strip, in_rows).transpose(1, 4, 2, 0, 3)
-    gate_up_owned = gate_up_owned.reshape(2, in_rows, runs * devices * strip)
     down_owned = downs_owned.reshape(devices * strip, down_columns)
 
     owner_grads = [

time: 1290 us -> 1230 us (0.953)
  matrix products: 60.7 us -> 29 us
    dot_general x6 -> x2, matrix products: 60.7 us -> 29 us  [token_dot(): lax.dot_general(left.reshape(-1, left.shape[-1]), right.reshape(-1, right...]
  transfers between devices with their start and end apart: 2 -> 2, of which waited for: 0 -> 0; matrix products, arithmetic and copies ran while one was open for 3% -> 0% of each run, Pallas kernels for 27% -> 29%
where the time goes in v5:
time: 1230 us
  Pallas kernels  1120 us (91%)
  other arithmetic  30.2 us (2%)
  matrix products  29 us (2%)
  local copies, waits for them, and re-layouts  23.7 us (2%)
  between operations  18.2 us (1%)
    pallas_call x5, Pallas kernels, call(): pl.pallas_call(kernel, in_specs=[pl.BlockSpec(memory_space=place) for _,...  1060 us
    pallas_call x1, Pallas kernels, unit_weight_grads(): pl.pallas_call(kernel, grid=(shards, 4), in_specs=specs, out_specs=pl.Blo...  62.3 us
    dot_general x2, matrix products, token_dot(): lax.dot_general(left.reshape(-1, left.shape[-1]), right.reshape(-1, right...  29 us
  transfers between devices with their start and end apart: 2, of which 0 were waited for; matrix products, arithmetic and copies ran while one was open for 0% of the time, Pallas kernels for 29%

profile of v5, /device:TPU:0, one launch (start us, length us, event | category | flops | bytes accessed | tf_op | source)
XLA Modules:
  0.0 1225.1 jit_solution(14411614228011419344)
XLA Ops:
  7.4 1.4 scatter.4.refs_6_
  17.4 4.3 maximum_bitcast_fusion
  21.6 4.2 reshape.232.refs_4_
  25.9 1.1 convert_element_type.68
  27.0 3.2 multiply_sine_fusion
  31.1 184.3 %shard_map.364 = (bf16[4,144,2048]{2,1,0:T(8,128)(2,1)}, bf16[4,144,2048]{2,1,0:T(8,128)(2,1)}, bf16[2,4,288,2048]{3,2,1,0:T(8,128)(2,1)}, bf16[2,4,288,2048]{3,...) custom-call(bf16[2,288,2048]{2,1,0:T(8,128)(2,1)} %refs_0_.1, ...), custom_call_target="tpu_custom_call" | custom-call | tf_op jit(solution)/shard_map/pallas_call | solution.py:717
  216.7 215.3 %shard_map.365 = (bf16[2,4,288,768]{3,2,1,0:T(8,128)(2,1)}, bf16[2,4,288,768]{3,2,1,0:T(8,128)(2,1)}, bf16[2,4,288,256]{3,2,1,0:T(8,128)(2,1)}, bf16[2,4,288,256...) custom-call(bf16[2,4,288,2048]{3,2,1,0:T(8,128)(2,1)} %get-tuple-ele, ...), custom_call_target="tpu_custom_call" | custom-call | tf_op jit(solution)/shard_map/pallas_call | solution.py:717
  432.1 221.4 %shard_map.366 = (bf16[2,4,288,2048]{3,2,1,0:T(8,128)(2,1)}, bf16[2,4,288,2048]{3,2,1,0:T(8,128)(2,1)}, bf16[2,4,288,1024]{3,2,1,0:T(8,128)(2,1)}, bf16[2,4,288,...) custom-call(bf16[2,144,2048]{2,1,0:T(8,128)(2,1)} %get-tuple-element, ...), custom_call_target="tpu_custom_call" | custom-call | tf_op jit(solution)/shard_map/pallas_call | solution.py:717
  653.5 16.8 %fusion.5 = f32[1024,2048,1,1]{1,0,3,2:T(8,128)} fusion(bf16[2,4,288,1024]{3,2,1,0:T(8,128)(2,1)} %get-tuple-element.110, bf16[2,4,288,2048]{3,2,1,0:T(8,128)(2,1)} %get-tuple-element.91.refs_2_), kind=kOutput, calls=%fused_computation.60 | convolution fusion | flops 9663676416 | bytes 22544384 | tf_op jit(solution)/shard_map/dot_general | solution.py:1847
  670.3 12.3 %fusion = bf16[1024,2048]{1,0:T(8,128)(2,1)S(1)} fusion(f32[1024,2048,1,1]{1,0,3,2:T(8,128)} %fusion.5, bf16[2,4,288,1024]{3,2,1,0:T(8,128)(2,1)S(1)} %copy-done.28, bf16[2,4,288,2048]{3,2,1,0:T(8,128)(2,1)S(1)} %copy-done.27), kind=kOutput, calls=%fused_computation.1 | convolution fusion | flops 9667870720 | bytes 26738688 | tf_op jit(solution)/shard_map/dot_general | solution.py:1847
  682.6 2.3 copy.61
  685.0 62.3 %shard_map.368 = bf16[4,512,2048]{2,1,0:T(8,128)(2,1)} custom-call(bf16[4,2,4,288,512]{4,3,2,1,0:T(8,128)(2,1)} %get-tuple-element.107.late_units, bf16[2,4,288,2048]{3,2,1,0:T(8,128)(2,1)} %get-tuple-element.90.refs_1_.late_rows, bf16[4,2,4,288,512]{4,3,2,1,0:T(8,128)(2,1)} %get-tuple-element.108.early_units, ...), custom_call_target="tpu_custom_call" | custom-call | tf_op jit(solution)/shard_map/pallas_call | solution.py:1776
  747.3 289.2 %shard_map.367 = (bf16[2,4,288,768]{3,2,1,0:T(8,128)(2,1)}, bf16[2,4,288,768]{3,2,1,0:T(8,128)(2,1)}, bf16[2,4,288,2048]{3,2,1,0:T(8,128)(2,1)}, bf16[4,144,2048...) custom-call(bf16[2,4,288,768]{3,2,1,0:T(8,128)(2,1)} %get-tuple-elem, ...), custom_call_target="tpu_custom_call" | custom-call | tf_op jit(solution)/shard_map/pallas_call | solution.py:717
  1039.1 151.2 %shard_map.369 = (bf16[2,288,2048]{2,1,0:T(8,128)(2,1)}, bf16[2,288,2048]{2,1,0:T(8,128)(2,1)}, bf16[4,2,64,512]{3,2,1,0:T(8,128)(2,1)}, f32[256,512]{1,0:T(8,12...) custom-call(bf16[2,4,288,2048]{3,2,1,0:T(8,128)(2,1)} %get-tuple-elemen, ...), custom_call_target="tpu_custom_call" | custom-call | tf_op jit(solution)/shard_map/pallas_call | solution.py:717
  1190.3 1.3 slice.72
  1191.6 1.5 multiply_reduce_fusion
  1200.2 1.1 multiply_subtract_fusion.4
  1201.4 1.2 multiply_subtract_fusion.3
  1203.3 2.9 multiply_subtract_fusion
  1206.5 1.1 copy-done.11
  1208.8 4.0 multiply_subtract_fusion.1
  1212.8 1.4 copy.64
  1214.2 1.1 copy-done.6
  1215.3 1.4 copy.65
  (99 shorter events, 20.4 us)
Async XLA Ops:
  7.2 6.4 copy-start.10
  7.2 7.2 copy-start.4
  7.2 1031.9 %reduce-scatter.5.cloned.1.call-start = ((), (), s32[]{:S(2)}) async-start(), calls=%async_computation.3 | async-start | bytes 5242880 | tf_op jit(solution)/shard_map/reduce_scatter | solution.py:1971
  21.6 4.3 copy-start
  653.5 16.8 %copy-start.27 = (bf16[2,4,288,2048]{3,2,1,0:T(8,128)(2,1)S(1)}, bf16[2,4,288,2048]{3,2,1,0:T(8,128)(2,1)}, u32[]{:S(2)}) copy-start(bf16[2,4,288,2048]{3,2,1,0:T(8,128)(2,1)} %get-tuple-element.112) | copy-start | bytes 28311556
  653.5 16.8 %copy-start.28 = (bf16[2,4,288,1024]{3,2,1,0:T(8,128)(2,1)S(1)}, bf16[2,4,288,1024]{3,2,1,0:T(8,128)(2,1)}, u32[]{:S(2)}) copy-start(bf16[2,4,288,1024]{3,2,1,0:T(8,128)(2,1)} %get-tuple-element.111) | copy-start | bytes 14155780
  684.9 354.2 %reduce-scatter.3.cloned.1.call-start = ((), (), s32[]{:S(2)}) async-start(), calls=%async_computation.2 | async-start | bytes 10485760 | tf_op jit(solution)/shard_map/reduce_scatter | solution.py:1968
  747.3 290.1 %copy-start.22 = (f32[16,2048]{1,0:T(8,128)S(1)}, f32[16,2048]{1,0:T(8,128)}, u32[]{:S(2)}) copy-start(f32[16,2048]{1,0:T(8,128)} %get-tuple-element.116) | copy-start | bytes 393220
  1190.3 7.1 copy-start.16
  1197.3 1.9 copy-start.14
  1197.3 1.9 copy-start.15
  1197.4 2.8 copy-start.9
  1197.4 2.8 copy-start.17
  1199.2 2.2 copy-start.18
  1199.2 2.2 copy-start.19
  1200.2 2.4 copy-start.1
  1200.2 3.0 copy-start.8
  1203.3 3.0 copy-start.3
  1203.3 3.3 copy-start.5
  1203.3 4.4 copy-start.11
  1203.3 5.0 copy-start.12
  1203.3 5.6 copy-start.13
  1208.8 4.0 copy-start.7
  1212.8 2.5 copy-start.6
  (7 other events, 9.3 us)
Sparse Core Ops, SparseCore 0:
  685.0 74.5 reduce-scatter.4
  762.1 144.9 reduce-scatter.2

commit v6 on v5

--- a/solution.py
+++ b/solution.py
@@ -941,6 +941,60 @@
     )(rows_in, grads_in, hidden, unit_grads, *back_parts, *out_parts)
 
 
+def down_grad_phase(hidden, grads, out, total, actions):
+    _, chips, tokens, units = hidden[0].shape
+    planes, _, columns = out.shape
+
+    def body(*refs):
+        out_ref = refs[4]
+        block, step = pl.program_id(0), pl.program_id(1)
+        at_step(8 * block + step, actions)
+
+        @pl.when(step == 0)
+        def _():
+            total[...] = jnp.zeros(total.shape, jnp.float32)
+
+        for place in range(2):
+
+            @pl.when(lax.div(step, 4) == place)
+            def _():
+                left, right = refs[2 * place], refs[2 * place + 1]
+                total[...] += dot_tn(
+                    left[0].reshape(2 * tokens, units), right[0].reshape(2 * tokens, columns)
+                )
+
+        @pl.when(step == 7)
+        def _():
+            out_ref[0] = total[...].astype(jnp.bfloat16)
+
+    specs, operands = [], []
+    for pair in (1, 0):
+        first = 0 if pair == 1 else 4
+
+        def at(step, first=first):
+            return jnp.clip(step - first, 0, 3)
+
+        specs.append(
+            pl.BlockSpec(
+                (1, 2, tokens, units),
+                lambda block, step, at=at: (lax.div(at(step), 2), lax.rem(at(step), 2), 0, 0),
+            )
+        )
+        specs.append(
+            pl.BlockSpec(
+                (1, 2, tokens, columns),
+                lambda block, step, at=at: (lax.div(at(step), 2), lax.rem(at(step), 2), 0, block),
+            )
+        )
+        operands += [hidden[pair], grads[pair]]
+    pltpu.emit_pipeline(
+        body,
+        grid=(planes, 8),
+        in_specs=specs,
+        out_specs=[pl.BlockSpec((1, units, columns), lambda block, step: (block, 0, 0))],
+    )(*operands, out)
+
+
 def bf16(*shape):
     return jax.ShapeDtypeStruct(shape, jnp.bfloat16)
 
@@ -1072,7 +1126,7 @@
         cot_own()
         for copy in act_outside:
             copy.arrived()
-        for copy in head_near + out_near:
+        for copy in head_near + out_near + cot_outside:
             copy.start()
 
         for chunk in range(CHUNKS):
@@ -1093,8 +1147,6 @@
             copy.arrived()
         head_relay.start()
         out_relay.start()
-        for copy in cot_outside:
-            copy.start()
         moves[0].last()
         moves[1].third()
         head_relay.arrived()
@@ -1268,7 +1320,8 @@
         hidden, unit_grads = refs[10:12], refs[12:14]
         back_parts, out_parts = (refs[14:16], refs[16:18]), (refs[18:20], refs[20:22])
         middle_grad, gain_sum, landing = refs[22], refs[23], refs[24:27]
-        stage, own_branch, wires = refs[28:32], refs[32], Wires(*refs[33:])
+        down_parts = refs[28]
+        stage, own_branch, wires = refs[29:33], refs[33], Wires(*refs[34:])
         meet(SIDES)
         gain_sum[...] = jnp.zeros(gain_sum.shape, jnp.float32)
 
@@ -1298,7 +1351,12 @@
             {1: sums.second, 4: sums.third, 6: lambda: (sums.last(), late_move.first()) and None},
         )
         late_move.second()
-        late_move.third()
+        pl.run_scoped(
+            lambda total: down_grad_phase(
+                hidden, (grads_early, grads_late_ref), down_parts, total, {30: late_move.third}
+            ),
+            pltpu.VMEM((units, columns), jnp.float32),
+        )
         late_move.last()
 
     outs = call(
@@ -1312,11 +1370,14 @@
         + [(shape, HBM) for shape in partial_shapes(rows, width)] * 4
         + [(f32(2, rows, width), VMEM), (f32(STRIPE, width), VMEM)]
         + [(shape, HBM) for shape in landing_shapes(rows, width)]
-        + [(whole_pair, HBM)],
+        + [(whole_pair, HBM), (bf16(shards, units, columns), HBM)],
         stage_shapes(rows, width) + [pltpu.VMEM((2, rows, width), jnp.bfloat16)] + wire_shapes(50),
         62,
     )
-    return outs[19], outs[0], outs[1], outs[2:4], outs[4:6], outs[6:8], (outs[10:12], outs[12:14]), outs[14], outs[15]
+    return (
+        outs[19], outs[0], outs[1], outs[20], outs[4:6], outs[6:8], (outs[10:12], outs[12:14]), outs[14],
+        outs[15],
+    )
 
 
 def attend_back(
@@ -1736,51 +1797,24 @@
 
 
 def unit_weight_grads(unit_grads, rows_in):
-    shards, _, _, tokens, columns = unit_grads[0].shape
+    shards, chunks, chips, tokens, columns = unit_grads[0].shape
     width = rows_in[0].shape[3]
-
-    def kernel(late_units, late_rows, early_units, early_rows, out, total):
-        step = pl.program_id(1)
-
-        @pl.when(step == 0)
-        def _():
-            total[...] = jnp.zeros(total.shape, jnp.float32)
-
-        for place, (units, rows_ref) in enumerate(((late_units, late_rows), (early_units, early_rows))):
-
-            @pl.when(lax.div(step, 2) == place)
-            def _():
-                left = units[0, 0].reshape(CHIPS * tokens, columns)
-                right = rows_ref[0].reshape(CHIPS * tokens, width)
-                total[...] += dot_tn(left, right)
-
-        @pl.when(step == 3)
-        def _():
-            out[0] = total[...].astype(jnp.bfloat16)
-
-    late = lambda step: jnp.minimum(step, 1)
-    early = lambda step: jnp.maximum(step - 2, 0)
-    specs = []
-    for at in (late, early):
-        specs.append(
-            pl.BlockSpec(
-                (1, 1, CHIPS, tokens, columns),
-                (lambda at: lambda shard, step: (shard, at(step), 0, 0, 0))(at),
-            )
-        )
-        specs.append(
-            pl.BlockSpec(
-                (1, CHIPS, tokens, width), (lambda at: lambda shard, step: (at(step), 0, 0, 0))(at)
-            )
-        )
+    count = chunks * chips * tokens
+
+    def kernel(late_units, late_rows, early_units, early_rows, out):
+        total = dot_tn(late_units[0].reshape(count, columns), late_rows[...].reshape(count, width))
+        total += dot_tn(early_units[0].reshape(count, columns), early_rows[...].reshape(count, width))
+        out[0] = total.astype(jnp.bfloat16)
+
+    block = pl.BlockSpec((1, chunks, chips, tokens, columns), lambda shard: (shard, 0, 0, 0, 0))
+    rows_block = whole(rows_in[0].shape)
     return pl.pallas_call(
         kernel,
-        grid=(shards, 4),
-        in_specs=specs,
-        out_specs=pl.BlockSpec((1, columns, width), lambda shard, step: (shard, 0, 0)),
+        grid=(shards,),
+        in_specs=[block, rows_block] * 2,
+        out_specs=pl.BlockSpec((1, columns, width), lambda shard: (shard, 0, 0)),
         out_shape=bf16(shards, columns, width),
-        scratch_shapes=[pltpu.VMEM((columns, width), jnp.float32)],
-        compiler_params=params(60),
+        compiler_params=params(62),
     )(unit_grads[1], rows_in[1], unit_grads[0], rows_in[0])
 
 
@@ -1956,19 +1990,16 @@
         grads_early,
         normed_early,
         branch_late,
-        hidden,
+        down_sum,
         unit_grads,
         back_early,
         out_parts,
         middle_grad,
         gain_sum,
     ) = feed_forward(normed_two, normed_late, grads_late, feed_weights, middle, own_grads, gain_two, units)
-    grads_all = (grads_early, grads_late)
+    down_sum = lax.psum_scatter(down_sum, "fsdp", scatter_dimension=0, tiled=False)
     unit_sum = unit_weight_grads(unit_grads, (normed_early, normed_late))
     unit_sum = lax.psum_scatter(unit_sum, "fsdp", scatter_dimension=0, tiled=False)
-    down_sum = reduce(jnp.add, [token_dot(hidden[pair], grads_all[pair]) for pair in (1, 0)]).astype(low)
-    down_sum = down_sum.reshape(-1, planes, down_columns).transpose(1, 0, 2)
-    down_sum = lax.psum_scatter(down_sum, "fsdp", scatter_dimension=0, tiled=False)
     head_grads, branch_early, output_groups, own_input_grad, gain_sums = attend_back(
         states,
         lengths,

time: 1230 us -> 1190 us (0.967)
  matrix products: 29 us -> 0 us
    dot_general x2 -> x0, matrix products: 29 us -> none  [token_dot(): lax.dot_general(left.reshape(-1, left.shape[-1]), right.reshape(-1, right...]
    pallas_call x1, Pallas kernels: 62.3 us -> 49.7 us  [unit_weight_grads(): pl.pallas_call(kernel, grid=(shards,), in_specs=[block, rows_block] * 2,...]
where the time goes in v6:
time: 1190 us; the launch traced here: 1180 us
  Pallas kernels  1110 us (93%)
  other arithmetic  30.2 us (3%)
  local copies, waits for them, and re-layouts  21.5 us (2%)
  between operations  18.2 us (2%)
    pallas_call x5, Pallas kernels, call(): pl.pallas_call(kernel, in_specs=[pl.BlockSpec(memory_space=place) for _,...  1060 us
    pallas_call x1, Pallas kernels, unit_weight_grads(): pl.pallas_call(kernel, grid=(shards,), in_specs=[block, rows_block] * 2,...  49.7 us
  transfers between devices with their start and end apart: 2, of which 0 were waited for; matrix products, arithmetic and copies ran while one was open for 0% of the time, Pallas kernels for 29%

profile of v6, /device:TPU:0, one launch (start us, length us, event | category | flops | bytes accessed | tf_op | source)
XLA Modules:
  0.0 1181.8 jit_solution(8296042824640523896)
XLA Ops:
  7.4 1.4 scatter.4.refs_6_
  12.4 1.1 convert_element_type.59
  17.4 4.3 maximum_bitcast_fusion
  21.6 4.2 reshape.225.refs_4_
  25.9 1.1 convert_element_type.65
  27.0 3.2 multiply_sine_fusion
  31.0 170.1 %shard_map.364 = (bf16[4,144,2048]{2,1,0:T(8,128)(2,1)}, bf16[4,144,2048]{2,1,0:T(8,128)(2,1)}, bf16[2,4,288,2048]{3,2,1,0:T(8,128)(2,1)}, bf16[2,4,288,2048]{3,...) custom-call(bf16[2,288,2048]{2,1,0:T(8,128)(2,1)} %refs_0_.1, ...), custom_call_target="tpu_custom_call" | custom-call | tf_op jit(solution)/shard_map/pallas_call | solution.py:717
  202.5 215.7 %shard_map.365 = (bf16[2,4,288,768]{3,2,1,0:T(8,128)(2,1)}, bf16[2,4,288,768]{3,2,1,0:T(8,128)(2,1)}, bf16[2,4,288,256]{3,2,1,0:T(8,128)(2,1)}, bf16[2,4,288,256...) custom-call(bf16[2,4,288,2048]{3,2,1,0:T(8,128)(2,1)} %get-tuple-ele, ...), custom_call_target="tpu_custom_call" | custom-call | tf_op jit(solution)/shard_map/pallas_call | solution.py:717
  418.1 233.6 %shard_map.366 = (bf16[2,4,288,2048]{3,2,1,0:T(8,128)(2,1)}, bf16[2,4,288,2048]{3,2,1,0:T(8,128)(2,1)}, bf16[2,4,288,1024]{3,2,1,0:T(8,128)(2,1)}, bf16[2,4,288,...) custom-call(bf16[2,144,2048]{2,1,0:T(8,128)(2,1)} %get-tuple-element, ...), custom_call_target="tpu_custom_call" | custom-call | tf_op jit(solution)/shard_map/pallas_call | solution.py:717
  651.8 49.7 %shard_map.368 = bf16[4,512,2048]{2,1,0:T(8,128)(2,1)} custom-call(bf16[4,2,4,288,512]{4,3,2,1,0:T(8,128)(2,1)} %get-tuple-element.105.late_units, bf16[2,4,288,2048]{3,2,1,0:T(8,128)(2,1)} %get-tuple-element.88.refs_1_.late_rows, bf16[4,2,4,288,512]{4,3,2,1,0:T(8,128)(2,1)} %get-tuple-element.106.early_units, ...), custom_call_target="tpu_custom_call" | custom-call | tf_op jit(solution)/shard_map/pallas_call | solution.py:1811
  701.5 293.5 %shard_map.367 = (bf16[2,4,288,768]{3,2,1,0:T(8,128)(2,1)}, bf16[2,4,288,768]{3,2,1,0:T(8,128)(2,1)}, bf16[2,4,288,2048]{3,2,1,0:T(8,128)(2,1)}, bf16[4,144,2048...) custom-call(bf16[2,4,288,768]{3,2,1,0:T(8,128)(2,1)} %get-tuple-elem, ...), custom_call_target="tpu_custom_call" | custom-call | tf_op jit(solution)/shard_map/pallas_call | solution.py:717
  997.6 149.2 %shard_map.369 = (bf16[2,288,2048]{2,1,0:T(8,128)(2,1)}, bf16[2,288,2048]{2,1,0:T(8,128)(2,1)}, bf16[4,2,64,512]{3,2,1,0:T(8,128)(2,1)}, f32[256,512]{1,0:T(8,12...) custom-call(bf16[2,4,288,2048]{3,2,1,0:T(8,128)(2,1)} %get-tuple-elemen, ...), custom_call_target="tpu_custom_call" | custom-call | tf_op jit(solution)/shard_map/pallas_call | solution.py:717
  1146.9 1.3 slice.72
  1148.1 1.5 multiply_reduce_fusion
  1152.6 1.1 copy.50
  1155.8 1.0 multiply_subtract_fusion.5
  1156.8 1.2 multiply_subtract_fusion.4
  1158.0 1.2 multiply_subtract_fusion.3
  1159.9 2.9 multiply_subtract_fusion
  1163.1 1.1 copy-done.11
  1165.4 4.0 multiply_subtract_fusion.1
  1169.4 1.4 copy.57
  1170.8 1.1 copy-done.6
  1171.9 1.4 copy.58
  (92 shorter events, 17.3 us)
Async XLA Ops:
  7.2 6.4 copy-start.10
  7.2 7.2 copy-start.4
  7.2 990.4 %reduce-scatter.5.cloned.1.call-start = ((), (), s32[]{:S(2)}) async-start(), calls=%async_computation.3 | async-start | bytes 5242880 | tf_op jit(solution)/shard_map/reduce_scatter | solution.py:2000
  21.6 4.3 copy-start
  651.7 345.9 %reduce-scatter.3.cloned.1.call-start = ((), (), s32[]{:S(2)}) async-start(), calls=%async_computation.2 | async-start | bytes 10485760 | tf_op jit(solution)/shard_map/reduce_scatter | solution.py:2002
  701.5 294.4 %copy-start.22 = (f32[16,2048]{1,0:T(8,128)S(1)}, f32[16,2048]{1,0:T(8,128)}, u32[]{:S(2)}) copy-start(f32[16,2048]{1,0:T(8,128)} %get-tuple-element.112) | copy-start | bytes 393220
  1146.8 7.1 copy-start.16
  1153.8 1.9 copy-start.14
  1153.8 1.9 copy-start.15
  1153.9 1.9 copy-start.20
  1153.9 1.9 copy-start.21
  1153.9 2.8 copy-start.9
  1154.0 2.8 copy-start.17
  1155.7 2.2 copy-start.18
  1155.7 2.2 copy-start.19
  1156.8 2.4 copy-start.1
  1156.8 3.0 copy-start.8
  1159.8 3.0 copy-start.3
  1159.8 3.3 copy-start.5
  1159.8 4.4 copy-start.11
  1159.8 5.0 copy-start.12
  1159.8 5.6 copy-start.13
  1165.4 4.0 copy-start.7
  1169.4 2.5 copy-start.6
  (5 other events, 5.6 us)
Sparse Core Ops, SparseCore 0:
  651.8 76.1 reduce-scatter.4
  730.5 144.9 reduce-scatter.2

commit v7 on v6

--- a/solution.py
+++ b/solution.py
@@ -1467,37 +1467,35 @@
             wires.load([(outputs.at[plane], output_groups.at[plane])])
 
         middle_sum.first()
-        output_sums[1].first()
-        output_sums[0].first()
         back_through(
             1,
             late_branch,
             {
                 1: middle_sum.second,
-                4: middle_sum.third,
-                6: both(middle_sum.last, move.first),
-                7: move.second,
+                3: output_sums[1].first,
+                5: output_sums[0].first,
+                7: middle_sum.third,
             },
         )
         input_sums[1].first()
         output_sums[1].second()
+        middle_sum.last()
+        move.first()
+        move.second()
+        output_sums[1].third()
+        input_sums[1].second()
         move.third()
+        output_sums[1].last()
         move.last()
         back_through(
             0,
             early_branch,
-            {
-                0: output_sums[1].third,
-                2: both(output_sums[1].last, output_sums[0].second),
-                4: output_sums[0].third,
-                6: both(output_sums[0].last, send_back),
-                7: input_sums[1].second,
-            },
+            {1: input_sums[1].third, 4: both(input_sums[1].last, output_sums[0].second), 7: output_sums[0].third},
         )
         input_sums[0].first()
-        input_sums[1].third()
+        output_sums[0].last()
+        send_back()
         input_sums[0].second()
-        input_sums[1].last()
         input_sums[0].third()
         input_sums[0].last()
         for copy in back_to_planes:
@@ -1692,6 +1690,8 @@
         weight_grad_phase(output_refs[2], output_refs[3], output_total, False, {})
         outs_in[...] = output_total[...].astype(jnp.bfloat16)
         third[1].start()
+        for copy in first:
+            copy.start()
         third[0].arrived()
         head_two[...] = (
             combined[:, flip(plane, 2)].astype(jnp.float32) + head_landing[0].astype(jnp.float32)
@@ -1703,8 +1703,6 @@
             + output_landing[0].astype(jnp.float32)
         ).astype(jnp.bfloat16)
         second[1].start()
-        for copy in first:
-            copy.start()
         for index in range(3, count):
             gains_step(index)
         for copy in rows_back:

time: 1190 us -> 1180 us (level)
  no operation moved by 1% of the time
where the time goes in v7:
time: 1180 us; the launch traced here: 1170 us
  Pallas kernels  1100 us (93%)
  other arithmetic  30.2 us (3%)
  local copies, waits for them, and re-layouts  21.5 us (2%)
  between operations  18.1 us (2%)
    pallas_call x5, Pallas kernels, call(): pl.pallas_call(kernel, in_specs=[pl.BlockSpec(memory_space=place) for _,...  1050 us
    pallas_call x1, Pallas kernels, unit_weight_grads(): pl.pallas_call(kernel, grid=(shards,), in_specs=[block, rows_block] * 2,...  49.9 us
  transfers between devices with their start and end apart: 2, of which 0 were waited for; matrix products, arithmetic and copies ran while one was open for 0% of the time, Pallas kernels for 29%

profile of v7, /device:TPU:0, one launch (start us, length us, event | category | flops | bytes accessed | tf_op | source)
XLA Modules:
  0.0 1172.2 jit_solution(8713178856541747286)
XLA Ops:
  7.4 1.4 scatter.4.refs_6_
  12.4 1.1 convert_element_type.59
  17.4 4.3 maximum_bitcast_fusion
  21.6 4.2 reshape.225.refs_4_
  25.9 1.1 convert_element_type.65
  27.0 3.2 multiply_sine_fusion
  31.0 170.1 %shard_map.364 = (bf16[4,144,2048]{2,1,0:T(8,128)(2,1)}, bf16[4,144,2048]{2,1,0:T(8,128)(2,1)}, bf16[2,4,288,2048]{3,2,1,0:T(8,128)(2,1)}, bf16[2,4,288,2048]{3,...) custom-call(bf16[2,288,2048]{2,1,0:T(8,128)(2,1)} %refs_0_.1, ...), custom_call_target="tpu_custom_call" | custom-call | tf_op jit(solution)/shard_map/pallas_call | solution.py:717
  202.5 215.7 %shard_map.365 = (bf16[2,4,288,768]{3,2,1,0:T(8,128)(2,1)}, bf16[2,4,288,768]{3,2,1,0:T(8,128)(2,1)}, bf16[2,4,288,256]{3,2,1,0:T(8,128)(2,1)}, bf16[2,4,288,256...) custom-call(bf16[2,4,288,2048]{3,2,1,0:T(8,128)(2,1)} %get-tuple-ele, ...), custom_call_target="tpu_custom_call" | custom-call | tf_op jit(solution)/shard_map/pallas_call | solution.py:717
  418.1 233.6 %shard_map.366 = (bf16[2,4,288,2048]{3,2,1,0:T(8,128)(2,1)}, bf16[2,4,288,2048]{3,2,1,0:T(8,128)(2,1)}, bf16[2,4,288,1024]{3,2,1,0:T(8,128)(2,1)}, bf16[2,4,288,...) custom-call(bf16[2,144,2048]{2,1,0:T(8,128)(2,1)} %get-tuple-element, ...), custom_call_target="tpu_custom_call" | custom-call | tf_op jit(solution)/shard_map/pallas_call | solution.py:717
  651.8 49.9 %shard_map.368 = bf16[4,512,2048]{2,1,0:T(8,128)(2,1)} custom-call(bf16[4,2,4,288,512]{4,3,2,1,0:T(8,128)(2,1)} %get-tuple-element.105.late_units, bf16[2,4,288,2048]{3,2,1,0:T(8,128)(2,1)} %get-tuple-element.88.refs_1_.late_rows, bf16[4,2,4,288,512]{4,3,2,1,0:T(8,128)(2,1)} %get-tuple-element.106.early_units, ...), custom_call_target="tpu_custom_call" | custom-call | tf_op jit(solution)/shard_map/pallas_call | solution.py:1809
  701.7 285.9 %shard_map.367 = (bf16[2,4,288,768]{3,2,1,0:T(8,128)(2,1)}, bf16[2,4,288,768]{3,2,1,0:T(8,128)(2,1)}, bf16[2,4,288,2048]{3,2,1,0:T(8,128)(2,1)}, bf16[4,144,2048...) custom-call(bf16[2,4,288,768]{3,2,1,0:T(8,128)(2,1)} %get-tuple-elem, ...), custom_call_target="tpu_custom_call" | custom-call | tf_op jit(solution)/shard_map/pallas_call | solution.py:717
  990.2 147.2 %shard_map.369 = (bf16[2,288,2048]{2,1,0:T(8,128)(2,1)}, bf16[2,288,2048]{2,1,0:T(8,128)(2,1)}, bf16[4,2,64,512]{3,2,1,0:T(8,128)(2,1)}, f32[256,512]{1,0:T(8,12...) custom-call(bf16[2,4,288,2048]{3,2,1,0:T(8,128)(2,1)} %get-tuple-elemen, ...), custom_call_target="tpu_custom_call" | custom-call | tf_op jit(solution)/shard_map/pallas_call | solution.py:717
  1137.3 1.3 slice.72
  1138.6 1.5 multiply_reduce_fusion
  1143.1 1.1 copy.50
  1146.2 1.0 multiply_subtract_fusion.5
  1147.3 1.2 multiply_subtract_fusion.4
  1148.4 1.2 multiply_subtract_fusion.3
  1150.3 2.9 multiply_subtract_fusion
  1153.6 1.1 copy-done.11
  1155.9 4.0 multiply_subtract_fusion.1
  1159.8 1.4 copy.57
  1161.3 1.1 copy-done.6
  1162.4 1.4 copy.58
  (92 shorter events, 17.3 us)
Async XLA Ops:
  7.2 6.4 copy-start.10
  7.2 7.2 copy-start.4
  7.2 982.9 %reduce-scatter.5.cloned.1.call-start = ((), (), s32[]{:S(2)}) async-start(), calls=%async_computation.3 | async-start | bytes 5242880 | tf_op jit(solution)/shard_map/reduce_scatter | solution.py:1998
  21.6 4.3 copy-start
  651.7 338.4 %reduce-scatter.3.cloned.1.call-start = ((), (), s32[]{:S(2)}) async-start(), calls=%async_computation.2 | async-start | bytes 10485760 | tf_op jit(solution)/shard_map/reduce_scatter | solution.py:2000
  701.7 286.8 %copy-start.22 = (f32[16,2048]{1,0:T(8,128)S(1)}, f32[16,2048]{1,0:T(8,128)}, u32[]{:S(2)}) copy-start(f32[16,2048]{1,0:T(8,128)} %get-tuple-element.112) | copy-start | bytes 393220
  1137.3 7.1 copy-start.16
  1144.3 1.9 copy-start.14
  1144.3 1.9 copy-start.15
  1144.3 1.9 copy-start.20
  1144.3 1.9 copy-start.21
  1144.4 2.8 copy-start.9
  1144.4 2.8 copy-start.17
  1146.2 2.2 copy-start.18
  1146.2 2.2 copy-start.19
  1147.3 2.4 copy-start.1
  1147.3 3.0 copy-start.8
  1150.3 3.0 copy-start.3
  1150.3 3.3 copy-start.5
  1150.3 4.4 copy-start.11
  1150.3 5.0 copy-start.12
  1150.3 5.6 copy-start.13
  1155.9 4.0 copy-start.7
  1159.8 2.5 copy-start.6
  (5 other events, 5.6 us)
Sparse Core Ops, SparseCore 0:
  651.8 76.1 reduce-scatter.4
  730.5 144.9 reduce-scatter.2
